TPU v7x, 128 devices: a whole 4x4x4 slice. The times are simulated.
128 devices in a mesh: gx: 32 (over z, y, core), gy: 4 (over x).
Axes of the slice: x: 4, y: 4, z: 4, core: 2. Of those that a mesh axis runs over, the one named last changes fastest.
Arguments:
- features: bfloat16 [32, 4, 2048, 256], P('gx', 'gy'), may hold values from -6 to 6
- pre_norm: bfloat16 [32, 4, 2048, 256], P('gx', 'gy')
- out_grad: bfloat16 [32, 4, 2048, 256], P('gx', 'gy'), may hold values from -6 to 6
- weight: bfloat16 [27, 256, 256], replicated, may hold values from -0.375 to 0.375
- gamma: float32 [256], replicated, may hold values from 0.1 to 1.9
- beta: float32 [256], replicated, may hold values from -3 to 3
- neighbors: int32 [32, 4, 27, 2048], P('gx', 'gy'), may hold values from 0 to 8384, as said below
- boundary: int32 [32, 4, 704], P('gx', 'gy'), may hold values from 0 to 2048, as said below
- counts: int32 [32, 4], P('gx', 'gy'), may hold values from 1 to 2048, as said below
Outputs:
- in_grad: bfloat16 [32, 4, 2048, 256], P('gx', 'gy')
- weight_grad: float32 [6912, 256], P(('gx', 'gy'))
- gamma_grad: float32 [256], replicated
- beta_grad: float32 [256], replicated
Inputs may be any that keep to these rules, and one draw needn't show every extreme that they name: `neighbors`: the map is that of a submanifold convolution on a voxel grid: each device owns an 8 x 16 x 16 block of positions, its live rows are its occupied positions in order, rows at or past its count name no row at any offset, offset 13 names the row itself, and if pair (r, k) on one device names row q then row q's device names r at offset 26 - k. Rows named on other devices lie on that device's faces and are listed in its boundary list. `boundary`: A device's live rows on its x and y faces in increasing order, then 2048 in the unused slots. `counts`: some device holds 2048 live rows.
All inputs are finite; a program needn't handle non-finite values.
Results may differ from a plain program's by a relative error of at most 0.0049.
Values may be sent and summed in bfloat16 or wider, within the bound.
A program may use at most 64 MiB of HBM per device.

v0:
```python
import functools

import jax
import jax.numpy as jnp
from jax import lax
from jax.sharding import Mesh
from jax.sharding import PartitionSpec as P

GX_GY = ("gx_0", "gx_1", "gx_2", "gy")
GX = ("gx_0", "gx_1", "gx_2")


def one_axis_at_a_time(shard, axes):
    return functools.reduce(lax.psum, axes, shard)


def extended(block, sides, width):
    for axis, dim in sides:
        count = lax.axis_size(axis)
        forward = [(i, i + 1) for i in range(count - 1)]
        backward = [(target, source) for source, target in forward]
        low = lax.ppermute(
            lax.slice_in_dim(block, block.shape[dim] - width, None, axis=dim), axis, forward
        )
        high = lax.ppermute(lax.slice_in_dim(block, 0, width, axis=dim), axis, backward)
        block = jnp.concatenate([low, block, high], axis=dim)
    return block


def sum_in_order(blocks, axes, order):
    lengths = [lax.axis_size(a) for a in axes]
    blocks = blocks.reshape(*lengths, *blocks.shape[1:])
    blocks = blocks.transpose(*order, *range(len(axes), blocks.ndim))
    blocks = blocks.reshape(-1, *blocks.shape[len(axes) :])
    for k in order:
        blocks = lax.psum_scatter(blocks, axes[k], scatter_dimension=0, tiled=True)
    return blocks[0]


def cut_along(shard, dim, length):
    before, after = (shard.shape[:dim], shard.shape[dim + 1 :])
    return jnp.moveaxis(shard.reshape(*before, length, -1, *after), dim, 0)


def sum_by_axis_2(shard, axes, order, dim):
    length = lax.axis_size(axes)
    return sum_in_order(cut_along(shard, dim, length), axes, order)


def sum_at_owner(shard, axis, dim):
    blocks = cut_along(shard, dim, lax.axis_size(axis))
    arrived = lax.all_to_all(blocks, axis, split_axis=0, concat_axis=0, tiled=True)
    return arrived.sum(axis=0)


def gather_rows(local, border):
    padded = jnp.concatenate([local, jnp.zeros((1, local.shape[1]), local.dtype)], axis=0)
    return jnp.take(padded, border, axis=0, mode="clip")


def make_table(local, around):
    flat = around.reshape(-1, local.shape[1])
    return jnp.concatenate([local, flat, jnp.zeros((1, local.shape[1]), local.dtype)], axis=0)


def body(features, pre_norm, out_grad, weight, gamma, beta, neighbors, boundary, counts):
    feat = features[0, 0]
    rows = feat.shape[0]
    chans = feat.shape[1]
    border = boundary[0, 0]
    links = neighbors[0, 0]
    live = (lax.iota(jnp.int32, rows) < counts[0, 0])[:, None]
    zval = pre_norm[0, 0].astype(jnp.float32)
    zlive = jnp.where(live, zval, jnp.float32(0.0))
    sum_z, sum_sq, sum_count = (
        one_axis_at_a_time(jnp.sum(zlive, axis=0), GX_GY),
        one_axis_at_a_time(jnp.sum(zlive * zval, axis=0), GX_GY),
        one_axis_at_a_time(counts[0].astype(jnp.float32), GX_GY),
    )
    count = sum_count[0]
    mean = sum_z / count
    var = sum_sq / count - mean * mean
    rstd = lax.rsqrt(var + 1e-05)
    zhat = (zval - mean) * rstd
    act = gamma * zhat + beta
    sig = jax.nn.sigmoid(act)
    grad_act = jnp.where(
        live, out_grad[0, 0].astype(jnp.float32) * sig * (1.0 + act * (1.0 - sig)), jnp.float32(0.0)
    )
    beta_grad, gamma_grad = (
        one_axis_at_a_time(jnp.sum(grad_act, axis=0), GX_GY),
        one_axis_at_a_time(jnp.sum(grad_act * zhat, axis=0), GX_GY),
    )
    dz = jnp.where(
        live,
        gamma * rstd * (grad_act - beta_grad / count - zhat * gamma_grad / count),
        jnp.float32(0.0),
    ).astype(jnp.bfloat16)
    grad_edge = gather_rows(dz, border)
    grad_around = extended(grad_edge[None, None], ((GX, 0), ("gy", 1)), 1)
    grad_table = make_table(dz, grad_around)

    def offset_step(accum, item):
        mirror_row, w_k = item
        picked = jnp.take(grad_table, mirror_row, axis=0, mode="clip")
        accum = accum + lax.dot_general(
            picked, w_k, (((1,), (1,)), ((), ())), preferred_element_type=jnp.float32
        )
        term = lax.dot_general(
            feat, picked, (((0,), (0,)), ((), ())), preferred_element_type=jnp.float32
        )
        return (accum, term)

    in_accum, wterms = lax.scan(
        offset_step, jnp.zeros((rows, chans), jnp.float32), (links[::-1], weight)
    )
    local_wgrad = wterms.reshape(-1, chans)
    slab_part = sum_by_axis_2(local_wgrad, GX, (2, 0, 1), 0)
    weight_grad = sum_at_owner(slab_part, "gy", 0)
    in_grad = in_accum.astype(jnp.bfloat16)[None, None]
    return (in_grad, weight_grad, gamma_grad, beta_grad)


def solution(mesh):
    torus = Mesh(mesh.devices.reshape(4, 4, 2, mesh.shape["gy"]), ("gx_0", "gx_1", "gx_2", "gy"))
    return jax.shard_map(
        body,
        mesh=torus,
        in_specs=(
            P(GX, "gy", None, None),
            P(GX, "gy", None, None),
            P(GX, "gy", None, None),
            P(),
            P(),
            P(),
            P(GX, "gy", None, None),
            P(GX, "gy", None),
            P(GX, "gy"),
        ),
        out_specs=(P(GX, "gy", None, None), P(GX_GY, None), P(), P()),
        check_vma=False,
    )
```

profile of v0, /device:TPU:0, one launch (start us, length us, event | category | flops | bytes accessed | tf_op | source)
XLA Modules:
  0.0 667.6 jit_solution(7263673636512412923)
XLA Ops:
  10.2 13.1 %all-reduce.6 = (f32[256]{0:T(256)S(1)}, f32[1]{0:T(128)}, f32[256]{0:T(256)S(1)}) all-reduce(f32[256]{0:T(256)S(1)} %get-tuple-element.71, f32[1]{0:T(128)} %bitcast.2, f32[256]{0:T(256)S(1)} %get-tuple-element.70), channel_id=1, replica_groups=mesh['gx_0'=4,'gx_1'=4,'gx_2'=2,'gy'=4] {'gx_0'}, use_global_device_ids=true, to_apply=%region_10.11 | all-reduce | flops 513 | bytes 4104 | tf_op jit(solution)/shard_map/psum | solution.py:14
  23.3 11.4 %all-reduce.4 = (f32[256]{0:T(256)S(1)}, f32[1]{0:T(128)}, f32[256]{0:T(256)S(1)}) all-reduce(f32[256]{0:T(256)S(1)} %get-tuple-element.98, f32[1]{0:T(128)} %get-tuple-element.99, f32[256]{0:T(256)S(1)} %get-tuple-element.100), channel_id=1, replica_groups=mesh['gx_0'=4,'gx_1'=4,'gx_2'=2,'gy'=4] {'gx_1'}, use_global_device_ids=true, to_apply=%region_11.12 | all-reduce | flops 513 | bytes 4104 | tf_op jit(solution)/shard_map/psum | solution.py:14
  34.6 3.1 all-reduce.8
  37.7 11.1 %all-reduce.2 = (f32[256]{0:T(256)S(1)}, f32[]{:T(128)}, f32[256]{0:T(256)S(1)}) all-reduce(f32[256]{0:T(256)S(1)} %get-tuple-element.103, f32[]{:T(128)} %bitcast.3, f32[256]{0:T(256)S(1)} %get-tuple-element.105), channel_id=1, replica_groups=mesh['gx_0'=4,'gx_1'=4,'gx_2'=2,'gy'=4] {'gy'}, use_global_device_ids=true, to_apply=%region_13.14 | all-reduce | flops 513 | bytes 4104 | tf_op jit(solution)/shard_map/psum | solution.py:14
  50.1 3.7 fusion.24
  53.8 7.7 %all-reduce.5 = (f32[256]{0:T(256)S(1)}, f32[256]{0:T(256)S(1)}) all-reduce(f32[256]{0:T(256)S(1)} %get-tuple-element.69, f32[256]{0:T(256)S(1)} %get-tuple-element.68), channel_id=1, replica_groups=mesh['gx_0'=4,'gx_1'=4,'gx_2'=2,'gy'=4] {'gx_0'}, use_global_device_ids=true, to_apply=%region_20.21 | all-reduce | flops 512 | bytes 4096 | tf_op jit(solution)/shard_map/psum | solution.py:14
  61.6 7.7 %all-reduce.3 = (f32[256]{0:T(256)S(1)}, f32[256]{0:T(256)S(1)}) all-reduce(f32[256]{0:T(256)S(1)} %get-tuple-element.96, f32[256]{0:T(256)S(1)} %get-tuple-element.97), channel_id=1, replica_groups=mesh['gx_0'=4,'gx_1'=4,'gx_2'=2,'gy'=4] {'gx_1'}, use_global_device_ids=true, to_apply=%region_21.22 | all-reduce | flops 512 | bytes 4096 | tf_op jit(solution)/shard_map/psum | solution.py:14
  69.3 2.4 all-reduce.7
  71.7 7.7 %all-reduce.1 = (f32[256]{0:T(256)S(1)}, f32[256]{0:T(256)S(1)}) all-reduce(f32[256]{0:T(256)S(1)} %get-tuple-element.101, f32[256]{0:T(256)S(1)} %get-tuple-element.102), channel_id=1, replica_groups=mesh['gx_0'=4,'gx_1'=4,'gx_2'=2,'gy'=4] {'gy'}, use_global_device_ids=true, to_apply=%region_23.24 | all-reduce | flops 512 | bytes 4096 | tf_op jit(solution)/shard_map/psum | solution.py:14
  80.1 2.6 fusion.23
  82.8 2.8 gather_fusion.1
  87.0 3.1 collective-permute-start
  93.7 5.6 collective-permute-start.2
  99.3 1.7 copy.24
  101.0 8.0 %rev.3 = s32[27,2048]{1,0:T(8,128)} reverse(s32[27,2048]{1,0:T(8,128)} %bitcast.60), dimensions={0} | reverse | bytes 442368 | tf_op jit(solution)/shard_map/rev | solution.py:115
  109.0 8.2 %collective-permute-done.3 = bf16[3,1,704,256]{3,2,1,0:T(8,128)(2,1)} collective-permute-done((bf16[3,1,704,256]{3,2,1,0:T(8,128)(2,1)}, bf16[3,1,704,256]{3,2,1,0:T(8,128)(2,1)}, u32[]{:S(2)}, u32[]{:S(2)}) %collective-permute-start.3) | collective-permute-done | bytes 1081376 | tf_op jit(solution)/shard_map/ppermute | solution.py:25
  117.3 1.7 collective-permute-done.2
  119.0 2.0 pad_maximum_fusion
  121.0 11.1 %maximum_maximum_fusion = bf16[8385,256]{1,0:T(8,128)(2,1)} fusion(bf16[6336,256]{1,0:T(8,128)(2,1)S(1)} %bitcast.54, bf16[2048,256]{1,0:T(8,128)(2,1)S(1)} %fusion.23, bf16[8385]{0:T(1024)(128)(2,1)S(1)} %pad.3.clone), kind=kLoop, calls=%fused_computation.10 | loop fusion | flops 12879360 | bytes 8602498 | tf_op jit(solution)/shard_map/concatenate | solution.py:63
  132.1 412.4 %while.13 = (s32[]{:T(128)}, f32[2048,256]{1,0:T(8,128)S(1)}, f32[27,256,256]{2,1,0:T(8,128)}, s32[27,2048]{1,0:T(8,128)}, bf16[8385,256]{1,0:T(8,128)(2,1)}, /*...) while((s32[]{:T(128)}, f32[2048,256]{1,0:T(8,128)S(1)}, ...), condition=%wide.region_25.26_spmd.clone, body=%wide.region_24.25_spmd.clone.sunk | while | flops 537921536 | bytes 11968663 | solution.py:114
  132.9 9.4 %gather_fusion = bf16[2048,256]{1,0:T(8,128)(2,1)S(1)} fusion(bf16[8385,256]{1,0:T(8,128)(2,1)} %get-tuple-element.175, s32[2048]{0:T(1024)S(1)} %broadcast_clamp_fusion.2), kind=kCustom, calls=%fused_computation.clone.clone.1 | custom fusion | bytes 2105344 | tf_op jit(solution)/shard_map/while/body/eval_jaxpr/jit(_take)/gather | solution.py:105
  148.2 9.4 %gather_fusion = bf16[2048,256]{1,0:T(8,128)(2,1)S(1)} fusion(bf16[8385,256]{1,0:T(8,128)(2,1)} %get-tuple-element.175, s32[2048]{0:T(1024)S(1)} %broadcast_clamp_fusion.2), kind=kCustom, calls=%fused_computation.clone.clone.1 | custom fusion | bytes 2105344 | tf_op jit(solution)/shard_map/while/body/eval_jaxpr/jit(_take)/gather | solution.py:105
  160.1 1.7 convolution_add_fusion.2
  163.4 9.4 %gather_fusion = bf16[2048,256]{1,0:T(8,128)(2,1)S(1)} fusion(bf16[8385,256]{1,0:T(8,128)(2,1)} %get-tuple-element.175, s32[2048]{0:T(1024)S(1)} %broadcast_clamp_fusion.2), kind=kCustom, calls=%fused_computation.clone.clone.1 | custom fusion | bytes 2105344 | tf_op jit(solution)/shard_map/while/body/eval_jaxpr/jit(_take)/gather | solution.py:105
  178.7 9.4 %gather_fusion = bf16[2048,256]{1,0:T(8,128)(2,1)S(1)} fusion(bf16[8385,256]{1,0:T(8,128)(2,1)} %get-tuple-element.175, s32[2048]{0:T(1024)S(1)} %broadcast_clamp_fusion.2), kind=kCustom, calls=%fused_computation.clone.clone.1 | custom fusion | bytes 2105344 | tf_op jit(solution)/shard_map/while/body/eval_jaxpr/jit(_take)/gather | solution.py:105
  194.0 9.4 %gather_fusion = bf16[2048,256]{1,0:T(8,128)(2,1)S(1)} fusion(bf16[8385,256]{1,0:T(8,128)(2,1)} %get-tuple-element.175, s32[2048]{0:T(1024)S(1)} %broadcast_clamp_fusion.2), kind=kCustom, calls=%fused_computation.clone.clone.1 | custom fusion | bytes 2105344 | tf_op jit(solution)/shard_map/while/body/eval_jaxpr/jit(_take)/gather | solution.py:105
  209.3 9.4 %gather_fusion = bf16[2048,256]{1,0:T(8,128)(2,1)S(1)} fusion(bf16[8385,256]{1,0:T(8,128)(2,1)} %get-tuple-element.175, s32[2048]{0:T(1024)S(1)} %broadcast_clamp_fusion.2), kind=kCustom, calls=%fused_computation.clone.clone.1 | custom fusion | bytes 2105344 | tf_op jit(solution)/shard_map/while/body/eval_jaxpr/jit(_take)/gather | solution.py:105
  224.5 9.4 %gather_fusion = bf16[2048,256]{1,0:T(8,128)(2,1)S(1)} fusion(bf16[8385,256]{1,0:T(8,128)(2,1)} %get-tuple-element.175, s32[2048]{0:T(1024)S(1)} %broadcast_clamp_fusion.2), kind=kCustom, calls=%fused_computation.clone.clone.1 | custom fusion | bytes 2105344 | tf_op jit(solution)/shard_map/while/body/eval_jaxpr/jit(_take)/gather | solution.py:105
  236.5 1.7 convolution_add_fusion.2
  239.8 9.4 %gather_fusion = bf16[2048,256]{1,0:T(8,128)(2,1)S(1)} fusion(bf16[8385,256]{1,0:T(8,128)(2,1)} %get-tuple-element.175, s32[2048]{0:T(1024)S(1)} %broadcast_clamp_fusion.2), kind=kCustom, calls=%fused_computation.clone.clone.1 | custom fusion | bytes 2105344 | tf_op jit(solution)/shard_map/while/body/eval_jaxpr/jit(_take)/gather | solution.py:105
  255.1 9.4 %gather_fusion = bf16[2048,256]{1,0:T(8,128)(2,1)S(1)} fusion(bf16[8385,256]{1,0:T(8,128)(2,1)} %get-tuple-element.175, s32[2048]{0:T(1024)S(1)} %broadcast_clamp_fusion.2), kind=kCustom, calls=%fused_computation.clone.clone.1 | custom fusion | bytes 2105344 | tf_op jit(solution)/shard_map/while/body/eval_jaxpr/jit(_take)/gather | solution.py:105
  270.4 9.4 %gather_fusion = bf16[2048,256]{1,0:T(8,128)(2,1)S(1)} fusion(bf16[8385,256]{1,0:T(8,128)(2,1)} %get-tuple-element.175, s32[2048]{0:T(1024)S(1)} %broadcast_clamp_fusion.2), kind=kCustom, calls=%fused_computation.clone.clone.1 | custom fusion | bytes 2105344 | tf_op jit(solution)/shard_map/while/body/eval_jaxpr/jit(_take)/gather | solution.py:105
  282.3 1.7 convolution_add_fusion.2
  285.7 9.4 %gather_fusion = bf16[2048,256]{1,0:T(8,128)(2,1)S(1)} fusion(bf16[8385,256]{1,0:T(8,128)(2,1)} %get-tuple-element.175, s32[2048]{0:T(1024)S(1)} %broadcast_clamp_fusion.2), kind=kCustom, calls=%fused_computation.clone.clone.1 | custom fusion | bytes 2105344 | tf_op jit(solution)/shard_map/while/body/eval_jaxpr/jit(_take)/gather | solution.py:105
  297.6 1.7 convolution_add_fusion.2
  300.9 9.4 %gather_fusion = bf16[2048,256]{1,0:T(8,128)(2,1)S(1)} fusion(bf16[8385,256]{1,0:T(8,128)(2,1)} %get-tuple-element.175, s32[2048]{0:T(1024)S(1)} %broadcast_clamp_fusion.2), kind=kCustom, calls=%fused_computation.clone.clone.1 | custom fusion | bytes 2105344 | tf_op jit(solution)/shard_map/while/body/eval_jaxpr/jit(_take)/gather | solution.py:105
  312.9 1.7 convolution_add_fusion.2
  316.2 9.4 %gather_fusion = bf16[2048,256]{1,0:T(8,128)(2,1)S(1)} fusion(bf16[8385,256]{1,0:T(8,128)(2,1)} %get-tuple-element.175, s32[2048]{0:T(1024)S(1)} %broadcast_clamp_fusion.2), kind=kCustom, calls=%fused_computation.clone.clone.1 | custom fusion | bytes 2105344 | tf_op jit(solution)/shard_map/while/body/eval_jaxpr/jit(_take)/gather | solution.py:105
  331.5 9.4 %gather_fusion = bf16[2048,256]{1,0:T(8,128)(2,1)S(1)} fusion(bf16[8385,256]{1,0:T(8,128)(2,1)} %get-tuple-element.175, s32[2048]{0:T(1024)S(1)} %broadcast_clamp_fusion.2), kind=kCustom, calls=%fused_computation.clone.clone.1 | custom fusion | bytes 2105344 | tf_op jit(solution)/shard_map/while/body/eval_jaxpr/jit(_take)/gather | solution.py:105
  346.8 9.4 %gather_fusion = bf16[2048,256]{1,0:T(8,128)(2,1)S(1)} fusion(bf16[8385,256]{1,0:T(8,128)(2,1)} %get-tuple-element.175, s32[2048]{0:T(1024)S(1)} %broadcast_clamp_fusion.2), kind=kCustom, calls=%fused_computation.clone.clone.1 | custom fusion | bytes 2105344 | tf_op jit(solution)/shard_map/while/body/eval_jaxpr/jit(_take)/gather | solution.py:105
  358.7 1.7 convolution_add_fusion.2
  362.0 9.4 %gather_fusion = bf16[2048,256]{1,0:T(8,128)(2,1)S(1)} fusion(bf16[8385,256]{1,0:T(8,128)(2,1)} %get-tuple-element.175, s32[2048]{0:T(1024)S(1)} %broadcast_clamp_fusion.2), kind=kCustom, calls=%fused_computation.clone.clone.1 | custom fusion | bytes 2105344 | tf_op jit(solution)/shard_map/while/body/eval_jaxpr/jit(_take)/gather | solution.py:105
  377.3 9.4 %gather_fusion = bf16[2048,256]{1,0:T(8,128)(2,1)S(1)} fusion(bf16[8385,256]{1,0:T(8,128)(2,1)} %get-tuple-element.175, s32[2048]{0:T(1024)S(1)} %broadcast_clamp_fusion.2), kind=kCustom, calls=%fused_computation.clone.clone.1 | custom fusion | bytes 2105344 | tf_op jit(solution)/shard_map/while/body/eval_jaxpr/jit(_take)/gather | solution.py:105
  392.6 9.4 %gather_fusion = bf16[2048,256]{1,0:T(8,128)(2,1)S(1)} fusion(bf16[8385,256]{1,0:T(8,128)(2,1)} %get-tuple-element.175, s32[2048]{0:T(1024)S(1)} %broadcast_clamp_fusion.2), kind=kCustom, calls=%fused_computation.clone.clone.1 | custom fusion | bytes 2105344 | tf_op jit(solution)/shard_map/while/body/eval_jaxpr/jit(_take)/gather | solution.py:105
  404.5 1.7 convolution_add_fusion.2
  407.8 9.4 %gather_fusion = bf16[2048,256]{1,0:T(8,128)(2,1)S(1)} fusion(bf16[8385,256]{1,0:T(8,128)(2,1)} %get-tuple-element.175, s32[2048]{0:T(1024)S(1)} %broadcast_clamp_fusion.2), kind=kCustom, calls=%fused_computation.clone.clone.1 | custom fusion | bytes 2105344 | tf_op jit(solution)/shard_map/while/body/eval_jaxpr/jit(_take)/gather | solution.py:105
  423.1 9.4 %gather_fusion = bf16[2048,256]{1,0:T(8,128)(2,1)S(1)} fusion(bf16[8385,256]{1,0:T(8,128)(2,1)} %get-tuple-element.175, s32[2048]{0:T(1024)S(1)} %broadcast_clamp_fusion.2), kind=kCustom, calls=%fused_computation.clone.clone.1 | custom fusion | bytes 2105344 | tf_op jit(solution)/shard_map/while/body/eval_jaxpr/jit(_take)/gather | solution.py:105
  435.1 1.7 convolution_add_fusion.2
  438.4 9.4 %gather_fusion = bf16[2048,256]{1,0:T(8,128)(2,1)S(1)} fusion(bf16[8385,256]{1,0:T(8,128)(2,1)} %get-tuple-element.175, s32[2048]{0:T(1024)S(1)} %broadcast_clamp_fusion.2), kind=kCustom, calls=%fused_computation.clone.clone.1 | custom fusion | bytes 2105344 | tf_op jit(solution)/shard_map/while/body/eval_jaxpr/jit(_take)/gather | solution.py:105
  450.3 1.7 convolution_add_fusion.2
  453.7 9.4 %gather_fusion = bf16[2048,256]{1,0:T(8,128)(2,1)S(1)} fusion(bf16[8385,256]{1,0:T(8,128)(2,1)} %get-tuple-element.175, s32[2048]{0:T(1024)S(1)} %broadcast_clamp_fusion.2), kind=kCustom, calls=%fused_computation.clone.clone.1 | custom fusion | bytes 2105344 | tf_op jit(solution)/shard_map/while/body/eval_jaxpr/jit(_take)/gather | solution.py:105
  469.0 9.4 %gather_fusion = bf16[2048,256]{1,0:T(8,128)(2,1)S(1)} fusion(bf16[8385,256]{1,0:T(8,128)(2,1)} %get-tuple-element.175, s32[2048]{0:T(1024)S(1)} %broadcast_clamp_fusion.2), kind=kCustom, calls=%fused_computation.clone.clone.1 | custom fusion | bytes 2105344 | tf_op jit(solution)/shard_map/while/body/eval_jaxpr/jit(_take)/gather | solution.py:105
  480.9 1.7 convolution_add_fusion.2
  484.2 9.4 %gather_fusion = bf16[2048,256]{1,0:T(8,128)(2,1)S(1)} fusion(bf16[8385,256]{1,0:T(8,128)(2,1)} %get-tuple-element.175, s32[2048]{0:T(1024)S(1)} %broadcast_clamp_fusion.2), kind=kCustom, calls=%fused_computation.clone.clone.1 | custom fusion | bytes 2105344 | tf_op jit(solution)/shard_map/while/body/eval_jaxpr/jit(_take)/gather | solution.py:105
  499.5 9.4 %gather_fusion = bf16[2048,256]{1,0:T(8,128)(2,1)S(1)} fusion(bf16[8385,256]{1,0:T(8,128)(2,1)} %get-tuple-element.175, s32[2048]{0:T(1024)S(1)} %broadcast_clamp_fusion.2), kind=kCustom, calls=%fused_computation.clone.clone.1 | custom fusion | bytes 2105344 | tf_op jit(solution)/shard_map/while/body/eval_jaxpr/jit(_take)/gather | solution.py:105
  514.8 9.4 %gather_fusion = bf16[2048,256]{1,0:T(8,128)(2,1)S(1)} fusion(bf16[8385,256]{1,0:T(8,128)(2,1)} %get-tuple-element.175, s32[2048]{0:T(1024)S(1)} %broadcast_clamp_fusion.2), kind=kCustom, calls=%fused_computation.clone.clone.1 | custom fusion | bytes 2105344 | tf_op jit(solution)/shard_map/while/body/eval_jaxpr/jit(_take)/gather | solution.py:105
  526.7 1.7 convolution_add_fusion.2
  530.0 9.4 %gather_fusion = bf16[2048,256]{1,0:T(8,128)(2,1)S(1)} fusion(bf16[8385,256]{1,0:T(8,128)(2,1)} %get-tuple-element.175, s32[2048]{0:T(1024)S(1)} %broadcast_clamp_fusion.2), kind=kCustom, calls=%fused_computation.clone.clone.1 | custom fusion | bytes 2105344 | tf_op jit(solution)/shard_map/while/body/eval_jaxpr/jit(_take)/gather | solution.py:105
  544.5 6.7 %copy.14 = f32[2,4,4,216,256]{4,3,2,1,0:T(8,128)} copy(f32[2,4,4,216,256]{4,3,0,2,1:T(8,128)} %bitcast.55) | data formatting | bytes 14155776 | tf_op jit(solution)/shard_map/transpose | solution.py:33
  551.2 26.2 %reduce-scatter.4.cloned.1.call-done = f32[16,216,256]{2,1,0:T(8,128)} async-done(((f32[32,216,256]{2,1,0:T(8,128)}), f32[16,216,256]{2,1,0:T(8,128)}) %reduce-scatter.4.cloned.1.call-update) | async-done | bytes 3538960 | tf_op jit(solution)/shard_map/reduce_scatter | solution.py:36
  577.5 45.6 %reduce-scatter.6.cloned.1.call-done = f32[4,216,256]{2,1,0:T(8,128)} async-done(((f32[16,216,256]{2,1,0:T(8,128)}), f32[4,216,256]{2,1,0:T(8,128)}) %reduce-scatter.6.cloned.1.call-update) | async-done | bytes 884752 | tf_op jit(solution)/shard_map/reduce_scatter | solution.py:36
  623.1 24.9 %reduce-scatter.8.cloned.1.call-done = f32[1,216,256]{2,1,0:T(8,128)} async-done(((f32[4,216,256]{2,1,0:T(8,128)}), f32[1,216,256]{2,1,0:T(8,128)}) %reduce-scatter.8.cloned.1.call-update) | async-done | bytes 221200 | tf_op jit(solution)/shard_map/reduce_scatter | solution.py:36
  649.7 4.3 all-to-all-start
  655.0 5.4 all-to-all-done
  (239 shorter events, 151.6 us)
Async XLA Ops:
  7.2 570.2 %reduce-scatter.4.cloned.1.call-start = ((), (), s32[]{:S(2)}) async-start(), calls=%async_computation.4 | async-start | bytes 10616832 | tf_op jit(solution)/shard_map/reduce_scatter | solution.py:36
  50.1 30.0 %copy-start.1 = (bf16[1,1,2048,256]{3,2,1,0:T(8,128)(2,1)S(1)}, bf16[1,1,2048,256]{3,2,1,0:T(8,128)(2,1)}, u32[]{:S(2)}) copy-start(bf16[1,1,2048,256]{3,2,1,0:T(8,128)(2,1)} %param.12) | copy-start | bytes 3145732
  79.5 3.3 copy-start.4
  79.5 3.3 copy-start.5
  85.7 4.4 collective-permute-start.1
  87.0 4.3 collective-permute-start
  90.0 9.2 %copy-start.2 = (bf16[1,1,704,256]{3,2,1,0:T(8,128)(2,1)}, bf16[1,1,704,256]{3,2,1,0:T(8,128)(2,1)S(1)}, u32[]{:S(2)}) copy-start(bf16[1,1,704,256]{3,2,1,0:T(8,128)(2,1)S(1)} %collective-permute-done.1) | copy-start | bytes 1081348
  91.3 8.0 %copy-start.3 = (bf16[1,1,704,256]{3,2,1,0:T(8,128)(2,1)}, bf16[1,1,704,256]{3,2,1,0:T(8,128)(2,1)S(1)}, u32[]{:S(2)}) copy-start(bf16[1,1,704,256]{3,2,1,0:T(8,128)(2,1)S(1)} %collective-permute-done) | copy-start | bytes 1081348
  92.4 24.9 %collective-permute-start.3 = (bf16[3,1,704,256]{3,2,1,0:T(8,128)(2,1)}, bf16[3,1,704,256]{3,2,1,0:T(8,128)(2,1)}, u32[]{:S(2)}, u32[]{:S(2)}) collective-permute-start(bf16[3,1,704,256]{3,2,1,0:T(8,128)(2,1)} %pad_maximum_fusion.1), channel_id=1, source_target_pairs={{1,0},{2,1},{3,2},{5,4},{6,5},{7,6},{9,8},{10,9},{11,10},{13,12},{... | collective-permute-start | bytes 3244040 | tf_op jit(solution)/shard_map/ppermute | solution.py:25
  93.7 25.3 %collective-permute-start.2 = (bf16[3,1,704,256]{3,2,1,0:T(8,128)(2,1)}, bf16[3,1,704,256]{3,2,1,0:T(8,128)(2,1)}, u32[]{:S(2)}, u32[]{:S(2)}) collective-permute-start(bf16[3,1,704,256]{3,2,1,0:T(8,128)(2,1)} %pad_maximum_fusion.1), channel_id=1, source_target_pairs={{0,1},{1,2},{2,3},{4,5},{5,6},{6,7},{8,9},{9,10},{10,11},{12,13},{... | collective-permute-start | bytes 3244040 | tf_op jit(solution)/shard_map/ppermute | solution.py:22
  144.9 1.7 copy-start
  160.1 1.7 copy-start
  175.4 1.7 copy-start
  190.7 1.7 copy-start
  205.9 1.7 copy-start
  221.2 1.7 copy-start
  236.5 1.7 copy-start
  251.8 1.7 copy-start
  267.0 1.7 copy-start
  282.3 1.7 copy-start
  297.6 1.7 copy-start
  312.9 1.7 copy-start
  328.2 1.7 copy-start
  343.4 1.7 copy-start
  358.7 1.7 copy-start
  374.0 1.7 copy-start
  389.3 1.7 copy-start
  404.5 1.7 copy-start
  419.8 1.7 copy-start
  435.0 1.7 copy-start
  450.3 1.7 copy-start
  465.6 1.7 copy-start
  480.9 1.7 copy-start
  496.2 1.7 copy-start
  511.4 1.7 copy-start
  526.7 1.7 copy-start
  542.0 1.7 copy-start
  551.2 71.9 %reduce-scatter.6.cloned.1.call-start = ((), (), s32[]{:S(2)}) async-start(), calls=%async_computation.5 | async-start | bytes 4423680 | tf_op jit(solution)/shard_map/reduce_scatter | solution.py:36
  577.4 70.6 %reduce-scatter.8.cloned.1.call-start = ((), (), s32[]{:S(2)}) async-start(), calls=%async_computation.6 | async-start | bytes 1105920 | tf_op jit(solution)/shard_map/reduce_scatter | solution.py:36
  649.7 10.8 %all-to-all-start = ((f32[4,54,256]{2,1,0:T(8,128)}), f32[4,54,256]{2,1,0:T(8,128)S(1)}, u32[]{:S(2)}, u32[]{:S(2)}) async-start(f32[4,54,256]{2,1,0:T(8,128)} %reshape_squeeze.3), calls=%async_computation.3 | async-start | bytes 458752 | tf_op jit(solution)/shard_map/all_to_all | solution.py:52
Sparse Core Ops, SparseCore 0:
  551.3 26.0 reduce-scatter.3
  580.0 43.0 reduce-scatter.5
  625.7 22.3 reduce-scatter.7
where the time goes:
time: 673 us; the launch traced here: 668 us
  local copies, waits for them, and re-layouts  340 us (51%)
  waiting for transfers between devices  113 us (17%)
  matrix products  92.1 us (14%)
  blocking collectives  64.2 us (10%)
  other arithmetic  26.7 us (4%)
  starting transfers between devices  15.6 us (2%)
  between operations  14.5 us (2%)
    gather x27, local copies, waits for them, and re-layouts, offset_step(): picked = jnp.take(grad_table, mirror_row, axis=0, mode='clip')  254 us
    reduce_scatter x3, waiting for transfers between devices, sum_in_order(): blocks = lax.psum_scatter(blocks, axes[k], scatter_dimension=0, tiled=True)  96.7 us
    psum x8, blocking collectives, one_axis_at_a_time(): return functools.reduce(lax.psum, axes, shard)  64.2 us
    dot_general x27, matrix products, offset_step(): lax.dot_general(picked, w_k, (((1,), (1,)), ((), ())), preferred_element_...  46.3 us
    dot_general x27, matrix products, offset_step(): lax.dot_general(feat, picked, (((0,), (0,)), ((), ())), preferred_element...  45.8 us
    dynamic_update_slice x54, local copies, waits for them, and re-layouts, body(): lax.scan(offset_step, jnp.zeros((rows, chans), jnp.float32), (links[::-1]...  42.3 us
    dynamic_slice x27, local copies, waits for them, and re-layouts, body(): lax.scan(offset_step, jnp.zeros((rows, chans), jnp.float32), (links[::-1]...  22.9 us
  transfers between devices with their start and end apart: 8, of which 7 were waited for; matrix products, arithmetic and copies ran while one was open for 2% of the time, Pallas kernels for 0%

commit v1 on v0

--- a/solution.py
+++ b/solution.py
@@ -3,6 +3,8 @@
 import jax
 import jax.numpy as jnp
 from jax import lax
+from jax.experimental import pallas as pl
+from jax.experimental.pallas import tpu as pltpu
 from jax.sharding import Mesh
 from jax.sharding import PartitionSpec as P
 
@@ -60,7 +62,169 @@
 
 def make_table(local, around):
     flat = around.reshape(-1, local.shape[1])
-    return jnp.concatenate([local, flat, jnp.zeros((1, local.shape[1]), local.dtype)], axis=0)
+    tail = jnp.zeros((WIN, C), local.dtype)
+    return jnp.concatenate([local, flat, tail], axis=0)
+
+
+C = 256
+R = 2048
+SUB = 128
+TILE = 256
+WIN = 256
+NROW = 8384
+FAR = 1.0e6
+
+
+def plan_windows(links):
+    idx = links[::-1]
+    idx = jnp.where(idx < NROW, idx, jnp.int32(FAR))
+    cut = idx.reshape(9, 3, R // SUB, SUB)
+    starts = []
+    for _ in range(3):
+        low = jnp.min(cut, axis=(1, 3))
+        start = jnp.where(low < NROW, low // 16 * 16, jnp.int32(FAR))
+        starts.append(start)
+        cut = jnp.where(cut >= start[:, None, :, None] + WIN, cut, jnp.int32(FAR))
+    first, second, third = starts
+    starts = jnp.stack([jnp.minimum(first, NROW), jnp.minimum(second, NROW), third], axis=-1)
+    columns = jnp.pad(idx.astype(jnp.float32).T, ((0, 0), (0, 5)), constant_values=FAR)
+    return columns, starts.reshape(-1)
+
+
+def one_hot(columns, start):
+    lanes = lax.broadcasted_iota(jnp.int32, (SUB, WIN), 1).astype(jnp.float32)
+    place = columns - start.astype(jnp.float32)
+    return jnp.where(place == lanes, 1.0, 0.0).astype(jnp.bfloat16)
+
+
+def dot(a, b, dims):
+    return lax.dot_general(a, b, (dims, ((), ())), preferred_element_type=jnp.float32)
+
+
+def conv_kernel(starts, idx, table, feat, weight, in_grad, wgrad, acc, feat_t, picked, colbuf):
+    step = pl.program_id(0)
+    tiles = R // TILE
+
+    @pl.when(step == 0)
+    def _():
+        acc[...] = jnp.zeros_like(acc)
+
+        @pl.loop(0, tiles)
+        def _(t):
+            rows = pl.ds(pl.multiple_of(t * TILE, TILE), TILE)
+            feat_t[t] = feat[rows, :].T
+
+    def gather(t, slot):
+        for half in range(TILE // SUB):
+            row = pl.multiple_of(t * TILE + half * SUB, SUB)
+            at = (step * (R // SUB) + t * (TILE // SUB) + half) * 3
+            columns = pltpu.roll(idx[pl.ds(row, SUB), :], (128 - 3 * step) % 128, 1)
+            colbuf[pl.ds(half * SUB, SUB), :] = columns
+            total = None
+            cols = [jnp.broadcast_to(columns[:, i : i + 1], (SUB, WIN)) for i in range(3)]
+            for w in range(2):
+                start = pl.multiple_of(starts[at + w], 16)
+                hot = jnp.concatenate([one_hot(c, start) for c in cols], axis=0)
+                part = dot(hot, table[pl.ds(start, WIN), :], ((1,), (0,)))
+                total = part if total is None else total + part
+            total = total.astype(jnp.bfloat16)
+            for i in range(3):
+                picked[slot, pl.ds(row, SUB), i * C : (i + 1) * C] = total[i * SUB : (i + 1) * SUB]
+
+    def gather_rest(t, slot):
+        for half in range(TILE // SUB):
+            row = pl.multiple_of(t * TILE + half * SUB, SUB)
+            at = (step * (R // SUB) + t * (TILE // SUB) + half) * 3
+
+            def more(start):
+                columns = colbuf[pl.ds(half * SUB, SUB), :]
+                start = pl.multiple_of(start, 16)
+                cols = [jnp.broadcast_to(columns[:, i : i + 1], (SUB, WIN)) for i in range(3)]
+                hot = jnp.concatenate([one_hot(c, start) for c in cols], axis=0)
+                part = dot(hot, table[pl.ds(start, WIN), :], ((1,), (0,))).astype(jnp.bfloat16)
+                for i in range(3):
+                    picked[slot, pl.ds(row, SUB), i * C : (i + 1) * C] += part[
+                        i * SUB : (i + 1) * SUB
+                    ]
+                lane = lax.broadcasted_iota(jnp.int32, (SUB, 128), 1)
+                ahead = (lane < 3) & (columns >= (start + WIN).astype(jnp.float32))
+                low = jnp.min(jnp.where(ahead, columns, FAR)).astype(jnp.int32)
+                return jnp.where(low < NROW, low // 16 * 16, jnp.int32(FAR))
+
+            lax.while_loop(lambda start: start < NROW, more, starts[at + 2])
+
+    def dense(t, slot):
+        rows = pl.ds(pl.multiple_of(t * TILE, TILE), TILE)
+        total = acc[rows, :]
+        for i in range(3):
+            block = picked[slot, rows, i * C : (i + 1) * C]
+            total = total + dot(block, weight[i], ((1,), (1,)))
+            wgrad[i] += dot(feat_t[t], block, ((1,), (0,)))
+        acc[rows, :] = total
+
+    now = step % 2
+
+    @pl.when(step > 0)
+    def _():
+        wgrad[...] = jnp.zeros_like(wgrad)
+
+    @pl.when(step == 0)
+    def _():
+        @pl.loop(0, tiles)
+        def _(t):
+            gather(t, now)
+            gather_rest(t, now)
+
+    @pl.when((step > 0) & (step < 9))
+    def _():
+        @pl.loop(0, tiles)
+        def _(t):
+            gather(t, now)
+            dense(t, 1 - now)
+            gather_rest(t, now)
+
+    @pl.when(step == 9)
+    def _():
+        @pl.loop(0, tiles)
+        def _(t):
+            dense(t, 1 - now)
+        in_grad[...] = acc[...].astype(jnp.bfloat16)
+
+
+def convolve(starts, idx, table, feat, weight):
+    idx = jnp.pad(idx, ((0, 0), (0, 96)), constant_values=FAR)
+    whole = pl.BlockSpec(memory_space=pltpu.VMEM)
+    in_grad, wgrad = pl.pallas_call(
+        conv_kernel,
+        grid=(10,),
+        out_shape=(
+            jax.ShapeDtypeStruct((R, C), jnp.bfloat16),
+            jax.ShapeDtypeStruct((27, C, C), jnp.float32),
+        ),
+        in_specs=[
+            pl.BlockSpec(memory_space=pltpu.SMEM),
+            whole,
+            whole,
+            whole,
+            pl.BlockSpec((3, C, C), lambda g: (jnp.maximum(g - 1, 0), 0, 0)),
+        ],
+        out_specs=(
+            whole,
+            pl.BlockSpec((3, C, C), lambda g: (jnp.maximum(g - 1, 0), 0, 0)),
+        ),
+        scratch_shapes=[
+            pltpu.VMEM((R, C), jnp.float32),
+            pltpu.VMEM((R // TILE, C, TILE), jnp.bfloat16),
+            pltpu.VMEM((2, R, 3 * C), jnp.bfloat16),
+            pltpu.VMEM((TILE, 128), jnp.float32),
+        ],
+        compiler_params=pltpu.CompilerParams(vmem_limit_bytes=56 * 1024 * 1024),
+        cost_estimate=pl.CostEstimate(
+            flops=30_000_000_000, bytes_accessed=20_000_000, transcendentals=0
+        ),
+        name="conv_backward",
+    )(starts, idx, table, feat, weight)
+    return in_grad, wgrad.reshape(27 * C, C)
 
 
 def body(features, pre_norm, out_grad, weight, gamma, beta, neighbors, boundary, counts):
@@ -100,24 +264,11 @@
     grad_around = extended(grad_edge[None, None], ((GX, 0), ("gy", 1)), 1)
     grad_table = make_table(dz, grad_around)
 
-    def offset_step(accum, item):
-        mirror_row, w_k = item
-        picked = jnp.take(grad_table, mirror_row, axis=0, mode="clip")
-        accum = accum + lax.dot_general(
-            picked, w_k, (((1,), (1,)), ((), ())), preferred_element_type=jnp.float32
-        )
-        term = lax.dot_general(
-            feat, picked, (((0,), (0,)), ((), ())), preferred_element_type=jnp.float32
-        )
-        return (accum, term)
-
-    in_accum, wterms = lax.scan(
-        offset_step, jnp.zeros((rows, chans), jnp.float32), (links[::-1], weight)
-    )
-    local_wgrad = wterms.reshape(-1, chans)
+    idx, starts = plan_windows(links)
+    in_grad, local_wgrad = convolve(starts, idx, grad_table, feat, weight)
     slab_part = sum_by_axis_2(local_wgrad, GX, (2, 0, 1), 0)
     weight_grad = sum_at_owner(slab_part, "gy", 0)
-    in_grad = in_accum.astype(jnp.bfloat16)[None, None]
+    in_grad = in_grad[None, None]
     return (in_grad, weight_grad, gamma_grad, beta_grad)
 
 

time: 673 us -> 332 us (0.49)
  local copies, waits for them, and re-layouts: 340 us -> 20.8 us
  matrix products: 92.1 us -> 0 us
  Pallas kernels: 0 us -> 70 us
  blocking collectives: 64.2 us -> 74.7 us
    gather x27 -> x0, local copies, waits for them, and re-layouts: 254 us -> none  [offset_step(): picked = jnp.take(grad_table, mirror_row, axis=0, mode='clip')]
    dot_general x54 -> x0, matrix products: 92.1 us -> none  [the longest x27 46.3 us: offset_step(): lax.dot_general(picked, w_k, (((1,), (1,)), ((), ())), preferred_element_...]
    pallas_call x0 -> x1, Pallas kernels: none -> 70 us  [convolve(): pl.pallas_call(conv_kernel, grid=(10,), out_shape=(jax.ShapeDtypeStruct((...]
    dynamic_update_slice x54 -> x0, local copies, waits for them, and re-layouts: 42.3 us -> none  [body(): lax.scan(offset_step, jnp.zeros((rows, chans), jnp.float32), (links[::-1]...]
    dynamic_slice x27 -> x0, local copies, waits for them, and re-layouts: 22.9 us -> none  [body(): lax.scan(offset_step, jnp.zeros((rows, chans), jnp.float32), (links[::-1]...]
    ppermute x2, waiting for transfers between devices: 8.23 us -> 19 us  [extended(): lax.ppermute(lax.slice_in_dim(block, 0, width, axis=dim), axis, backward)]
    all_to_all x0 -> x1, blocking collectives: none -> 10.6 us  [sum_at_owner(): lax.all_to_all(blocks, axis, split_axis=0, concat_axis=0, tiled=True)]
    reduce_scatter x3, waiting for transfers between devices: 96.7 us -> 89.5 us  [sum_in_order(): blocks = lax.psum_scatter(blocks, axes[k], scatter_dimension=0, tiled=True)]
  transfers between devices with their start and end apart: 8 -> 7, of which waited for: 7 -> 5; matrix products, arithmetic and copies ran while one was open for 2% -> 4% of each run, Pallas kernels for 0% -> 0%
where the time goes in v1:
time: 332 us
  waiting for transfers between devices  110 us (33%)
  blocking collectives  74.7 us (22%)
  Pallas kernels  70 us (21%)
  other arithmetic  29.2 us (9%)
  local copies, waits for them, and re-layouts  20.8 us (6%)
  between operations  14.6 us (4%)
  starting transfers between devices  12 us (4%)
    reduce_scatter x3, waiting for transfers between devices, sum_in_order(): blocks = lax.psum_scatter(blocks, axes[k], scatter_dimension=0, tiled=True)  89.5 us
    pallas_call x1, Pallas kernels, convolve(): pl.pallas_call(conv_kernel, grid=(10,), out_shape=(jax.ShapeDtypeStruct((...  70 us
    psum x8, blocking collectives, one_axis_at_a_time(): return functools.reduce(lax.psum, axes, shard)  64.1 us
    ppermute x2, waiting for transfers between devices, extended(): lax.ppermute(lax.slice_in_dim(block, 0, width, axis=dim), axis, backward)  19 us
    concatenate x1, other arithmetic, make_table(): return jnp.concatenate([local, flat, tail], axis=0)  11.4 us
    all_to_all x1, blocking collectives, sum_at_owner(): lax.all_to_all(blocks, axis, split_axis=0, concat_axis=0, tiled=True)  10.6 us
    ppermute x2, starting transfers between devices, extended(): lax.ppermute(lax.slice_in_dim(block, block.shape[dim] - width, None, axis...  9.35 us
    another operation x1, local copies, waits for them, and re-layouts, sum_in_order(): blocks = blocks.reshape(*lengths, *blocks.shape[1:])  6.68 us
  transfers between devices with their start and end apart: 7, of which 5 were waited for; matrix products, arithmetic and copies ran while one was open for 4% of the time, Pallas kernels for 0%

profile of v1, /device:TPU:0, one launch (start us, length us, event | category | flops | bytes accessed | tf_op | source)
XLA Modules:
  0.0 331.7 jit_solution(15713127855684234601)
XLA Ops:
  7.2 0.0 reduce-scatter.4.cloned.1.call-start
  7.9 0.7 reduce
  8.6 1.6 fusion.1
  10.2 13.0 %all-reduce.8 = (f32[256]{0:T(256)S(1)}, f32[1]{0:T(128)}, f32[256]{0:T(256)S(1)}) all-reduce(f32[256]{0:T(256)S(1)} %get-tuple-element.11, f32[1]{0:T(128)} %bitcast.7, f32[256]{0:T(256)S(1)} %get-tuple-element.10), channel_id=1, replica_groups=mesh['gx_0'=4,'gx_1'=4,'gx_2'=2,'gy'=4] {'gx_0'}, use_global_device_ids=true, to_apply=%region_13.14 | all-reduce | flops 513 | bytes 4104 | tf_op jit(solution)/shard_map/psum | solution.py:16
  23.2 11.4 %all-reduce.6 = (f32[256]{0:T(256)S(1)}, f32[1]{0:T(128)}, f32[256]{0:T(256)S(1)}) all-reduce(f32[256]{0:T(256)S(1)} %get-tuple-element.24, f32[1]{0:T(128)} %get-tuple-element.25, f32[256]{0:T(256)S(1)} %get-tuple-element.26), channel_id=1, replica_groups=mesh['gx_0'=4,'gx_1'=4,'gx_2'=2,'gy'=4] {'gx_1'}, use_global_device_ids=true, to_apply=%region_14.15 | all-reduce | flops 513 | bytes 4104 | tf_op jit(solution)/shard_map/psum | solution.py:16
  34.6 3.1 all-reduce.10
  37.6 11.1 %all-reduce.4 = (f32[256]{0:T(256)S(1)}, f32[]{:T(128)}, f32[256]{0:T(256)S(1)}) all-reduce(f32[256]{0:T(256)S(1)} %get-tuple-element.29, f32[]{:T(128)} %bitcast.8, f32[256]{0:T(256)S(1)} %get-tuple-element.31), channel_id=1, replica_groups=mesh['gx_0'=4,'gx_1'=4,'gx_2'=2,'gy'=4] {'gy'}, use_global_device_ids=true, to_apply=%region_16.17 | all-reduce | flops 513 | bytes 4104 | tf_op jit(solution)/shard_map/psum | solution.py:16
  48.7 1.3 fusion.51
  50.1 0.0 copy-start
  50.1 3.7 %fusion.50 = (f32[256]{0:T(256)S(1)}, f32[256]{0:T(256)S(1)}, f32[2048,256]{1,0:T(8,128)}) fusion(f32[256]{0:T(256)S(1)} %get-tuple-element.33, f32[256]{0:T(256)S(1)} %get-tuple-element.34, bf16[1,1,2048,256]{3,2,1,0:T(8,128)(2,1)} %param.10, f32[256]{0:T(256)} %param.14, f32[256]{0:T(256)} %param.13, bf16[1,1,2048,256]{3,2,1,0:T(8,128)(2,1)} %param.11, ...), kind=kLoop, calls=%fused_computation.100 | loop fusion | flops 9436672 | bytes 4202496 | tf_op jit(solution)/shard_map/reduce_sum | solution.py:255
  53.8 7.7 %all-reduce.7 = (f32[256]{0:T(256)S(1)}, f32[256]{0:T(256)S(1)}) all-reduce(f32[256]{0:T(256)S(1)} %get-tuple-element.9, f32[256]{0:T(256)S(1)} %get-tuple-element.8), channel_id=1, replica_groups=mesh['gx_0'=4,'gx_1'=4,'gx_2'=2,'gy'=4] {'gx_0'}, use_global_device_ids=true, to_apply=%region_23.24 | all-reduce | flops 512 | bytes 4096 | tf_op jit(solution)/shard_map/psum | solution.py:16
  61.5 7.7 %all-reduce.5 = (f32[256]{0:T(256)S(1)}, f32[256]{0:T(256)S(1)}) all-reduce(f32[256]{0:T(256)S(1)} %get-tuple-element.22, f32[256]{0:T(256)S(1)} %get-tuple-element.23), channel_id=1, replica_groups=mesh['gx_0'=4,'gx_1'=4,'gx_2'=2,'gy'=4] {'gx_1'}, use_global_device_ids=true, to_apply=%region_24.25 | all-reduce | flops 512 | bytes 4096 | tf_op jit(solution)/shard_map/psum | solution.py:16
  69.2 2.4 all-reduce.9
  71.7 7.7 %all-reduce.3 = (f32[256]{0:T(256)S(1)}, f32[256]{0:T(256)S(1)}) all-reduce(f32[256]{0:T(256)S(1)} %get-tuple-element.27, f32[256]{0:T(256)S(1)} %get-tuple-element.28), channel_id=1, replica_groups=mesh['gx_0'=4,'gx_1'=4,'gx_2'=2,'gy'=4] {'gy'}, use_global_device_ids=true, to_apply=%region_26.27 | all-reduce | flops 512 | bytes 4096 | tf_op jit(solution)/shard_map/psum | solution.py:16
  79.4 0.0 copy-start.2
  79.4 0.0 copy-start.3
  79.4 0.7 broadcast_divide_fusion
  80.1 0.0 copy-done
  80.1 2.6 fusion.20
  82.7 0.0 copy-done.2
  82.7 0.0 copy-done.3
  82.7 0.1 concatenate.12
  82.8 0.0 copy-start.1
  82.8 2.8 gather_fusion
  85.6 1.3 collective-permute-start.1
  86.9 3.8 %collective-permute-start = (bf16[1,1,704,256]{3,2,1,0:T(8,128)(2,1)S(1)}, bf16[1,1,704,256]{3,2,1,0:T(8,128)(2,1)}, u32[]{:S(2)}, u32[]{:S(2)}) collective-permute-start(bf16[1,1,704,256]{3,2,1,0:T(8,128)(2,1)S(1)} %bitcast.96), channel_id=1, source_target_pairs={{0,4},{4,8},{8,12},{12,16},{16,20},{20,24},{24,28},{28,32},{32,36}... | collective-permute-start | bytes 1081352 | tf_op jit(solution)/shard_map/ppermute | solution.py:24
  90.7 0.0 copy-done.1
  90.7 0.4 copy.17
  91.0 5.8 %rev.3 = s32[27,2048]{0,1:T(8,128)} reverse(s32[27,2048]{0,1:T(8,128)S(1)} %bitcast.91), dimensions={0} | reverse | bytes 442368 | tf_op jit(solution)/shard_map/rev | solution.py:79
  96.9 1.4 convert_bitcast_fusion
  98.3 1.0 copy.18
  99.3 1.0 copy.21
  100.3 0.2 reduce_min.33
  100.6 0.0 collective-permute-done.1
  100.6 0.0 collective-permute-done
  100.6 2.2 pad_maximum_fusion.1
  102.8 1.3 collective-permute-start.3
  104.1 5.6 %collective-permute-start.2 = (bf16[3,1,704,256]{3,2,1,0:T(8,128)(2,1)}, bf16[3,1,704,256]{3,2,1,0:T(8,128)(2,1)}, u32[]{:S(2)}, u32[]{:S(2)}) collective-permute-start(bf16[3,1,704,256]{3,2,1,0:T(8,128)(2,1)} %pad_maximum_fusion.1), channel_id=1, source_target_pairs={{0,1},{1,2},{2,3},{4,5},{5,6},{6,7},{8,9},{9,10},{10,11},{12,13},{... | collective-permute-start | bytes 3244040 | tf_op jit(solution)/shard_map/ppermute | solution.py:24
  109.7 0.3 fusion.22
  110.0 0.3 fusion.21
  110.4 0.1 copy.19
  110.6 0.8 reshape.262.starts
  111.3 0.1 pad.13.clone
  111.4 1.1 pad.26.idx
  112.5 19.0 %collective-permute-done.3 = bf16[3,1,704,256]{3,2,1,0:T(8,128)(2,1)} collective-permute-done((bf16[3,1,704,256]{3,2,1,0:T(8,128)(2,1)}, bf16[3,1,704,256]{3,2,1,0:T(8,128)(2,1)}, u32[]{:S(2)}, u32[]{:S(2)}) %collective-permute-start.3) | collective-permute-done | bytes 1081376 | tf_op jit(solution)/shard_map/ppermute | solution.py:27
  131.5 1.6 collective-permute-done.2
  133.1 2.0 pad_maximum_fusion
  135.1 11.4 %maximum_maximum_fusion.table = bf16[8640,256]{1,0:T(8,128)(2,1)} fusion(bf16[6336,256]{1,0:T(8,128)(2,1)S(1)} %bitcast.89, bf16[2048,256]{1,0:T(8,128)(2,1)S(1)} %fusion.20, bf16[8640]{0:T(1024)(128)(2,1)S(1)} %pad.13.clone), kind=kLoop, calls=%fused_computation.1 | loop fusion | flops 13271040 | bytes 8733568 | tf_op jit(solution)/shard_map/concatenate | solution.py:66
  146.5 70.0 %conv_backward.1 = (bf16[2048,256]{1,0:T(8,128)(2,1)}, f32[27,256,256]{2,1,0:T(8,128)}) custom-call(s32[432]{0:T(512)} %reshape.262.starts, f32[2048,128]{1,0:T(8,128)} %pad.26.idx, bf16[8640,256]{1,0:T(8,128)(2,1)} %maximum_maximum_fusion.table, bf16[2048,256]{1,0:T(8,128)(2,1)} %bitcast.101, bf16[27,256,256]{2,1,0:T(8,128)(2,1)} %weight.1), custom_call_target="tpu_custom_call" | custom-call | flops 30000001024 | bytes 20000000 | tf_op jit(solution)/shard_map/conv_backward/pallas_call | solution.py:197
  216.6 6.7 %copy.20 = f32[4,4,2,216,256]{4,3,1,0,2:T(8,128)} copy(f32[4,4,2,216,256]{4,3,2,1,0:T(8,128)} %bitcast.90) | data formatting | bytes 14155776 | tf_op jit(solution)/shard_map/reshape;reshape;reshape | solution.py:34
  223.3 0.0 reduce-scatter.4.cloned.1.call-update
  223.3 0.0 reduce-scatter.6.cloned.1.call-start
  223.3 18.8 %reduce-scatter.4.cloned.1.call-done = f32[16,216,256]{2,1,0:T(8,128)} async-done(((f32[32,216,256]{2,1,0:T(8,128)}), f32[16,216,256]{2,1,0:T(8,128)}) %reduce-scatter.4.cloned.1.call-update) | async-done | bytes 3538960 | tf_op jit(solution)/shard_map/reduce_scatter | solution.py:38
  242.2 0.0 reduce-scatter.6.cloned.1.call-update
  242.2 0.0 reduce-scatter.8.cloned.1.call-start
  242.2 45.7 %reduce-scatter.6.cloned.1.call-done = f32[4,216,256]{2,1,0:T(8,128)} async-done(((f32[16,216,256]{2,1,0:T(8,128)}), f32[4,216,256]{2,1,0:T(8,128)}) %reduce-scatter.6.cloned.1.call-update) | async-done | bytes 884752 | tf_op jit(solution)/shard_map/reduce_scatter | solution.py:38
  288.0 0.0 reduce-scatter.8.cloned.1.call-update
  288.0 25.0 %reduce-scatter.8.cloned.1.call-done = f32[1,216,256]{2,1,0:T(8,128)} async-done(((f32[4,216,256]{2,1,0:T(8,128)}), f32[1,216,256]{2,1,0:T(8,128)}) %reduce-scatter.8.cloned.1.call-update) | async-done | bytes 221200 | tf_op jit(solution)/shard_map/reduce_scatter | solution.py:38
  313.0 1.0 reshape_squeeze.3
  313.9 10.6 %all_to_all.5 = f32[4,54,256]{2,1,0:T(8,128)S(1)} all-to-all(f32[4,54,256]{2,1,0:T(8,128)S(1)} %reshape_squeeze.3), channel_id=1, replica_groups=mesh['gx_0'=4,'gx_1'=4,'gx_2'=2,'gy'=4] {'gy'}, dimensions={0} | all-to-all | bytes 442368 | tf_op jit(solution)/shard_map/all_to_all | solution.py:54
  324.5 0.6 reduce_sum.49
  (9 shorter events, 0.1 us)
Async XLA Ops:
  7.2 235.0 %reduce-scatter.4.cloned.1.call-start = ((), (), s32[]{:S(2)}) async-start(), calls=%async_computation.4 | async-start | bytes 10616832 | tf_op jit(solution)/shard_map/reduce_scatter | solution.py:38
  50.1 30.0 %copy-start = (bf16[1,1,2048,256]{3,2,1,0:T(8,128)(2,1)S(1)}, bf16[1,1,2048,256]{3,2,1,0:T(8,128)(2,1)}, u32[]{:S(2)}) copy-start(bf16[1,1,2048,256]{3,2,1,0:T(8,128)(2,1)} %param.10) | copy-start | bytes 3145732
  79.4 3.3 copy-start.2
  79.4 3.3 copy-start.3
  82.8 7.9 %copy-start.1 = (s32[1,1,27,2048]{3,1,2,0:T(1,128)S(1)}, s32[1,1,27,2048]{3,1,2,0:T(1,128)}, u32[]{:S(2)}) copy-start(s32[1,1,27,2048]{3,1,2,0:T(1,128)} %param.15) | copy-start | bytes 663556
  85.6 15.0 %collective-permute-start.1 = (bf16[1,1,704,256]{3,2,1,0:T(8,128)(2,1)S(1)}, bf16[1,1,704,256]{3,2,1,0:T(8,128)(2,1)}, u32[]{:S(2)}, u32[]{:S(2)}) collective-permute-start(bf16[1,1,704,256]{3,2,1,0:T(8,128)(2,1)S(1)} %bitcast.95), channel_id=1, source_target_pairs={{4,0},{8,4},{12,8},{16,12},{20,16},{24,20},{28,24},{32,28},{36,32}... | collective-permute-start | bytes 1081352 | tf_op jit(solution)/shard_map/ppermute | solution.py:27
  86.9 13.7 %collective-permute-start = (bf16[1,1,704,256]{3,2,1,0:T(8,128)(2,1)S(1)}, bf16[1,1,704,256]{3,2,1,0:T(8,128)(2,1)}, u32[]{:S(2)}, u32[]{:S(2)}) collective-permute-start(bf16[1,1,704,256]{3,2,1,0:T(8,128)(2,1)S(1)} %bitcast.96), channel_id=1, source_target_pairs={{0,4},{4,8},{8,12},{12,16},{16,20},{20,24},{24,28},{28,32},{32,36}... | collective-permute-start | bytes 1081352 | tf_op jit(solution)/shard_map/ppermute | solution.py:24
  102.8 28.7 %collective-permute-start.3 = (bf16[3,1,704,256]{3,2,1,0:T(8,128)(2,1)}, bf16[3,1,704,256]{3,2,1,0:T(8,128)(2,1)}, u32[]{:S(2)}, u32[]{:S(2)}) collective-permute-start(bf16[3,1,704,256]{3,2,1,0:T(8,128)(2,1)} %pad_maximum_fusion.1), channel_id=1, source_target_pairs={{1,0},{2,1},{3,2},{5,4},{6,5},{7,6},{9,8},{10,9},{11,10},{13,12},{... | collective-permute-start | bytes 3244040 | tf_op jit(solution)/shard_map/ppermute | solution.py:27
  104.1 29.0 %collective-permute-start.2 = (bf16[3,1,704,256]{3,2,1,0:T(8,128)(2,1)}, bf16[3,1,704,256]{3,2,1,0:T(8,128)(2,1)}, u32[]{:S(2)}, u32[]{:S(2)}) collective-permute-start(bf16[3,1,704,256]{3,2,1,0:T(8,128)(2,1)} %pad_maximum_fusion.1), channel_id=1, source_target_pairs={{0,1},{1,2},{2,3},{4,5},{5,6},{6,7},{8,9},{9,10},{10,11},{12,13},{... | collective-permute-start | bytes 3244040 | tf_op jit(solution)/shard_map/ppermute | solution.py:24
  223.3 64.7 %reduce-scatter.6.cloned.1.call-start = ((), (), s32[]{:S(2)}) async-start(), calls=%async_computation.5 | async-start | bytes 4423680 | tf_op jit(solution)/shard_map/reduce_scatter | solution.py:38
  242.2 70.8 %reduce-scatter.8.cloned.1.call-start = ((), (), s32[]{:S(2)}) async-start(), calls=%async_computation.6 | async-start | bytes 1105920 | tf_op jit(solution)/shard_map/reduce_scatter | solution.py:38
Sparse Core Ops, SparseCore 0:
  223.4 18.7 reduce-scatter.3
  244.7 43.1 reduce-scatter.5
  290.5 22.3 reduce-scatter.7

commit v2 on v1

--- a/solution.py
+++ b/solution.py
@@ -10,6 +10,7 @@
 
 GX_GY = ("gx_0", "gx_1", "gx_2", "gy")
 GX = ("gx_0", "gx_1", "gx_2")
+MESH = pl.DeviceIdType.MESH
 
 
 def one_axis_at_a_time(shard, axes):
@@ -27,32 +28,6 @@
         high = lax.ppermute(lax.slice_in_dim(block, 0, width, axis=dim), axis, backward)
         block = jnp.concatenate([low, block, high], axis=dim)
     return block
-
-
-def sum_in_order(blocks, axes, order):
-    lengths = [lax.axis_size(a) for a in axes]
-    blocks = blocks.reshape(*lengths, *blocks.shape[1:])
-    blocks = blocks.transpose(*order, *range(len(axes), blocks.ndim))
-    blocks = blocks.reshape(-1, *blocks.shape[len(axes) :])
-    for k in order:
-        blocks = lax.psum_scatter(blocks, axes[k], scatter_dimension=0, tiled=True)
-    return blocks[0]
-
-
-def cut_along(shard, dim, length):
-    before, after = (shard.shape[:dim], shard.shape[dim + 1 :])
-    return jnp.moveaxis(shard.reshape(*before, length, -1, *after), dim, 0)
-
-
-def sum_by_axis_2(shard, axes, order, dim):
-    length = lax.axis_size(axes)
-    return sum_in_order(cut_along(shard, dim, length), axes, order)
-
-
-def sum_at_owner(shard, axis, dim):
-    blocks = cut_along(shard, dim, lax.axis_size(axis))
-    arrived = lax.all_to_all(blocks, axis, split_axis=0, concat_axis=0, tiled=True)
-    return arrived.sum(axis=0)
 
 
 def gather_rows(local, border):
@@ -225,6 +200,185 @@
         name="conv_backward",
     )(starts, idx, table, feat, weight)
     return in_grad, wgrad.reshape(27 * C, C)
+
+
+AXES = ("gy", "gx_1", "gx_0")
+TILE_AT = (0, 16, 32, 38)
+HOLDS = ((0,), (1,), (2, 3))
+
+
+def scatter_kernel(part, out, local, s_a, r_a, *rest):
+    s_b, r_b, s_c, r_c, s_d, r_d = (rest[3 * i : 3 * i + 3] for i in range(6))
+    load_sem, a_sem, b_sem, c_sem, d_sem = rest[18:]
+    pos = [lax.axis_index(a) for a in AXES]
+    core = lax.axis_index("gx_2")
+    z = pos[2]
+
+    def around(i):
+        return lax.rem(z + 1 + i, 4)
+
+    loads = []
+    for i in range(4):
+        rows = pl.ds(pl.multiple_of(around(i) * 1728, 64), 1728)
+        loads.append(pltpu.make_async_copy(part.at[rows, :], local.at[i], load_sem.at[i]))
+        loads[-1].start()
+
+    barrier = pltpu.get_barrier_semaphore()
+    pl.semaphore_signal(barrier, 1, device_id={"gx_2": 1 - core}, device_id_type=MESH)
+    for axis, at in zip(AXES, pos):
+        for d in range(1, 4):
+            peer = {axis: lax.rem(at + d, 4)}
+            pl.semaphore_signal(barrier, 1, device_id=peer, device_id_type=MESH)
+
+    def block(i, y, x, side, t):
+        skip = (x * 54 + TILE_AT[t]) % 8
+        base = (y * 2 + side) * 216 + x * 54 + TILE_AT[t] - skip
+        rows = local[i, pl.ds(pl.multiple_of(base, 8), 24 if skip else 16), :]
+        return rows[skip : skip + 16]
+
+    sends = []
+
+    def send(src, dst, sems, at, device):
+        copy = pltpu.make_async_remote_copy(
+            src_ref=src,
+            dst_ref=dst,
+            send_sem=sems.at[(0,) + at],
+            recv_sem=sems.at[(1,) + at],
+            device_id=device,
+            device_id_type=MESH,
+        )
+        copy.start()
+        sends.append(copy)
+        return copy
+
+    first = []
+    for i in range(4):
+        loads[i].wait()
+
+        @pl.loop(0, 4)
+        def _(y):
+            for x in range(4):
+                for t in range(4):
+                    mine = block(i, y, x, 1 - core, t)
+                    s_a[i, y * 4 + x, t] = mine.astype(jnp.bfloat16)
+
+        if i == 0:
+            pl.semaphore_wait(barrier, 10)
+        first.append(send(s_a.at[i], r_a.at[i], a_sem, (i,), {"gx_2": 1 - core}))
+
+    def spread(p, stage, sems, src, dst):
+        axis = (p + stage) % 3
+        return [
+            send(
+                src.at[lax.rem(pos[axis] + d, 4)],
+                dst.at[d - 1],
+                sems,
+                (p, d - 1),
+                {AXES[axis]: lax.rem(pos[axis] + d, 4)},
+            )
+            for d in range(1, 4)
+        ]
+
+    second = [None, None, []]
+    for i in range(4):
+        first[i].wait_recv()
+        z_of = around(i)
+
+        @pl.loop(0, 4)
+        def _(y):
+            for x in range(4):
+                for t in range(4):
+                    both = block(i, y, x, core, t) + r_a[i, y * 4 + x, t].astype(jnp.float32)
+                    both = both.astype(jnp.bfloat16)
+                    if t == 0:
+                        s_b[0][x, y * 4 + z_of, 0] = both
+                    elif t == 1:
+                        s_b[1][y, z_of * 4 + x, 0] = both
+                    else:
+                        s_b[2][z_of, x * 4 + y, t - 2] = both
+
+        if i < 3:
+            second[2].append(
+                send(s_b[2].at[z_of], r_b[2].at[i], b_sem, (2, i), {"gx_0": z_of})
+            )
+    for p in range(2):
+        second[p] = spread(p, 0, b_sem, s_b[p], r_b[p])
+
+    def total(own, came, at):
+        kind = jnp.float32
+        return (own[at].astype(kind) + came[(0,) + at[1:]].astype(kind)) + (
+            came[(1,) + at[1:]].astype(kind) + came[(2,) + at[1:]].astype(kind)
+        )
+
+    third = []
+    for p in range(3):
+        for copy in second[p]:
+            copy.wait_recv()
+        me = pos[p]
+
+        @pl.loop(0, 16)
+        def _(j):
+            for t in range(len(HOLDS[p])):
+                s_c[p][j // 4, j % 4, t] = total(s_b[p], r_b[p], (me, j, t)).astype(jnp.bfloat16)
+
+        third.append(spread(p, 1, c_sem, s_c[p], r_c[p]))
+
+    fourth = []
+    for p in range(3):
+        for copy in third[p]:
+            copy.wait_recv()
+        me = pos[(p + 1) % 3]
+
+        @pl.loop(0, 4)
+        def _(j):
+            for t in range(len(HOLDS[p])):
+                s_d[p][j, t] = total(s_c[p], r_c[p], (me, j, t))
+
+        fourth.append(spread(p, 2, d_sem, s_d[p], r_d[p]))
+
+    for p in range(3):
+        for copy in fourth[p]:
+            copy.wait_recv()
+        me = pos[(p + 2) % 3]
+        for t, which in enumerate(HOLDS[p]):
+            out[TILE_AT[which] : TILE_AT[which] + 16, :] = total(s_d[p], r_d[p], (me, t))
+
+    for copy in sends:
+        copy.wait_send()
+
+
+def scatter_sum(part):
+    def stage(lead, kind):
+        return [pltpu.VMEM(lead + (len(h), 16, C), kind) for h in HOLDS]
+
+    half, full = jnp.bfloat16, jnp.float32
+    return pl.pallas_call(
+        scatter_kernel,
+        out_shape=jax.ShapeDtypeStruct((54, C), jnp.float32),
+        in_specs=[pl.BlockSpec(memory_space=pl.ANY)],
+        out_specs=pl.BlockSpec(memory_space=pltpu.VMEM),
+        scratch_shapes=[
+            pltpu.VMEM((4, 1728, C), jnp.float32),
+            pltpu.VMEM((4, 16, 4, 16, C), jnp.bfloat16),
+            pltpu.VMEM((4, 16, 4, 16, C), jnp.bfloat16),
+            *stage((4, 16), half),
+            *stage((3, 16), half),
+            *stage((4, 4), half),
+            *stage((3, 4), half),
+            *stage((4,), full),
+            *stage((3,), full),
+            pltpu.SemaphoreType.DMA((4,)),
+            pltpu.SemaphoreType.DMA((2, 4)),
+            pltpu.SemaphoreType.DMA((2, 3, 3)),
+            pltpu.SemaphoreType.DMA((2, 3, 3)),
+            pltpu.SemaphoreType.DMA((2, 3, 3)),
+        ],
+        compiler_params=pltpu.CompilerParams(
+            collective_id=1, has_side_effects=True, vmem_limit_bytes=40 * 1024 * 1024
+        ),
+        cost_estimate=pl.CostEstimate(flops=10_000_000, bytes_accessed=7_000_000, transcendentals=0),
+        name="scatter_sum",
+    )(part)
 
 
 def body(features, pre_norm, out_grad, weight, gamma, beta, neighbors, boundary, counts):
@@ -266,8 +420,7 @@
 
     idx, starts = plan_windows(links)
     in_grad, local_wgrad = convolve(starts, idx, grad_table, feat, weight)
-    slab_part = sum_by_axis_2(local_wgrad, GX, (2, 0, 1), 0)
-    weight_grad = sum_at_owner(slab_part, "gy", 0)
+    weight_grad = scatter_sum(local_wgrad)
     in_grad = in_grad[None, None]
     return (in_grad, weight_grad, gamma_grad, beta_grad)
 

time: 332 us -> 248 us (0.75)
  waiting for transfers between devices: 110 us -> 20.7 us
  Pallas kernels: 70 us -> 104 us
  between operations: 14.6 us -> 1.49 us
  blocking collectives: 74.7 us -> 64.1 us
  local copies, waits for them, and re-layouts: 20.8 us -> 16.8 us
    reduce_scatter x3 -> x0, waiting for transfers between devices: 89.5 us -> none  [sum_in_order(): blocks = lax.psum_scatter(blocks, axes[k], scatter_dimension=0, tiled=True)]
    pallas_call x0 -> x1, Pallas kernels: none -> 34.5 us  [scatter_sum(): pl.pallas_call(scatter_kernel, out_shape=jax.ShapeDtypeStruct((54, C), jn...]
    all_to_all x1 -> x0, blocking collectives: 10.6 us -> none  [sum_at_owner(): lax.all_to_all(blocks, axis, split_axis=0, concat_axis=0, tiled=True)]
    another operation x2 -> x0, local copies, waits for them, and re-layouts: 7.64 us -> none  [the longest x1 6.68 us: sum_in_order(): blocks = blocks.reshape(*lengths, *blocks.shape[1:])]
    unnamed x11 -> x14, local copies, waits for them, and re-layouts: 1.39 us -> 5.02 us
  transfers between devices with their start and end apart: 7 -> 4, of which waited for: 5 -> 2; matrix products, arithmetic and copies ran while one was open for 4% -> 5% of each run, Pallas kernels for 0% -> 0%
where the time goes in v2:
time: 248 us
  Pallas kernels  104 us (42%)
  blocking collectives  64.1 us (26%)
  other arithmetic  28.6 us (12%)
  waiting for transfers between devices  20.7 us (8%)
  local copies, waits for them, and re-layouts  16.8 us (7%)
  starting transfers between devices  11.9 us (5%)
    pallas_call x1, Pallas kernels, convolve(): pl.pallas_call(conv_kernel, grid=(10,), out_shape=(jax.ShapeDtypeStruct((...  69.5 us
    psum x8, blocking collectives, one_axis_at_a_time(): return functools.reduce(lax.psum, axes, shard)  64.1 us
    pallas_call x1, Pallas kernels, scatter_sum(): pl.pallas_call(scatter_kernel, out_shape=jax.ShapeDtypeStruct((54, C), jn...  34.5 us
    ppermute x2, waiting for transfers between devices, extended(): lax.ppermute(lax.slice_in_dim(block, 0, width, axis=dim), axis, backward)  19 us
    concatenate x1, other arithmetic, make_table(): return jnp.concatenate([local, flat, tail], axis=0)  11.4 us
    ppermute x2, starting transfers between devices, extended(): lax.ppermute(lax.slice_in_dim(block, block.shape[dim] - width, None, axis...  9.35 us
    rev x1, local copies, waits for them, and re-layouts, plan_windows(): idx = links[::-1]  5.85 us
    unnamed x14, local copies, waits for them, and re-layouts  5.02 us
  transfers between devices with their start and end apart: 4, of which 2 were waited for; matrix products, arithmetic and copies ran while one was open for 5% of the time, Pallas kernels for 0%

profile of v2, /device:TPU:0, one launch (start us, length us, event | category | flops | bytes accessed | tf_op | source)
XLA Modules:
  0.0 247.6 jit_solution(3563170952980404343)
XLA Ops:
  1.3 0.7 reduce
  2.0 1.6 fusion.1
  3.6 13.0 %all-reduce.8 = (f32[256]{0:T(256)S(1)}, f32[1]{0:T(128)}, f32[256]{0:T(256)S(1)}) all-reduce(f32[256]{0:T(256)S(1)} %get-tuple-element.11, f32[1]{0:T(128)} %bitcast.7, f32[256]{0:T(256)S(1)} %get-tuple-element.10), channel_id=1, replica_groups=mesh['gx_0'=4,'gx_1'=4,'gx_2'=2,'gy'=4] {'gx_0'}, use_global_device_ids=true, to_apply=%region_13.14 | all-reduce | flops 513 | bytes 4104 | tf_op jit(solution)/shard_map/psum | solution.py:17
  16.6 11.4 %all-reduce.6 = (f32[256]{0:T(256)S(1)}, f32[1]{0:T(128)}, f32[256]{0:T(256)S(1)}) all-reduce(f32[256]{0:T(256)S(1)} %get-tuple-element.24, f32[1]{0:T(128)} %get-tuple-element.25, f32[256]{0:T(256)S(1)} %get-tuple-element.26), channel_id=1, replica_groups=mesh['gx_0'=4,'gx_1'=4,'gx_2'=2,'gy'=4] {'gx_1'}, use_global_device_ids=true, to_apply=%region_14.15 | all-reduce | flops 513 | bytes 4104 | tf_op jit(solution)/shard_map/psum | solution.py:17
  28.0 3.1 %all-reduce.10 = (f32[256]{0:T(256)S(1)}, f32[1]{0:T(128)}, f32[256]{0:T(256)S(1)}) all-reduce(f32[256]{0:T(256)S(1)} %get-tuple-element.19, f32[1]{0:T(128)} %get-tuple-element.20, f32[256]{0:T(256)S(1)} %get-tuple-element.21), channel_id=1, replica_groups=mesh['gx_0'=4,'gx_1'=4,'gx_2'=2,'gy'=4] {'gx_2'}, use_global_device_ids=true, to_apply=%region_15.16 | all-reduce | flops 513 | bytes 4104 | tf_op jit(solution)/shard_map/psum | solution.py:17
  31.0 11.1 %all-reduce.4 = (f32[256]{0:T(256)S(1)}, f32[]{:T(128)}, f32[256]{0:T(256)S(1)}) all-reduce(f32[256]{0:T(256)S(1)} %get-tuple-element.29, f32[]{:T(128)} %bitcast.8, f32[256]{0:T(256)S(1)} %get-tuple-element.31), channel_id=1, replica_groups=mesh['gx_0'=4,'gx_1'=4,'gx_2'=2,'gy'=4] {'gy'}, use_global_device_ids=true, to_apply=%region_16.17 | all-reduce | flops 513 | bytes 4104 | tf_op jit(solution)/shard_map/psum | solution.py:17
  42.1 1.3 fusion.51
  43.5 0.0 copy-start.1
  43.5 3.7 %fusion.50 = (f32[256]{0:T(256)S(1)}, f32[256]{0:T(256)S(1)}, f32[2048,256]{1,0:T(8,128)}) fusion(f32[256]{0:T(256)S(1)} %get-tuple-element.33, f32[256]{0:T(256)S(1)} %get-tuple-element.34, bf16[1,1,2048,256]{3,2,1,0:T(8,128)(2,1)} %param.10, f32[256]{0:T(256)} %param.14, f32[256]{0:T(256)} %param.13, bf16[1,1,2048,256]{3,2,1,0:T(8,128)(2,1)} %param.11, ...), kind=kLoop, calls=%fused_computation.100 | loop fusion | flops 9436672 | bytes 4202496 | tf_op jit(solution)/shard_map/reduce_sum | solution.py:409
  47.2 7.7 %all-reduce.7 = (f32[256]{0:T(256)S(1)}, f32[256]{0:T(256)S(1)}) all-reduce(f32[256]{0:T(256)S(1)} %get-tuple-element.9, f32[256]{0:T(256)S(1)} %get-tuple-element.8), channel_id=1, replica_groups=mesh['gx_0'=4,'gx_1'=4,'gx_2'=2,'gy'=4] {'gx_0'}, use_global_device_ids=true, to_apply=%region_23.24 | all-reduce | flops 512 | bytes 4096 | tf_op jit(solution)/shard_map/psum | solution.py:17
  54.9 7.7 %all-reduce.5 = (f32[256]{0:T(256)S(1)}, f32[256]{0:T(256)S(1)}) all-reduce(f32[256]{0:T(256)S(1)} %get-tuple-element.22, f32[256]{0:T(256)S(1)} %get-tuple-element.23), channel_id=1, replica_groups=mesh['gx_0'=4,'gx_1'=4,'gx_2'=2,'gy'=4] {'gx_1'}, use_global_device_ids=true, to_apply=%region_24.25 | all-reduce | flops 512 | bytes 4096 | tf_op jit(solution)/shard_map/psum | solution.py:17
  62.6 2.4 all-reduce.9
  65.1 7.7 %all-reduce.3 = (f32[256]{0:T(256)S(1)}, f32[256]{0:T(256)S(1)}) all-reduce(f32[256]{0:T(256)S(1)} %get-tuple-element.27, f32[256]{0:T(256)S(1)} %get-tuple-element.28), channel_id=1, replica_groups=mesh['gx_0'=4,'gx_1'=4,'gx_2'=2,'gy'=4] {'gy'}, use_global_device_ids=true, to_apply=%region_26.27 | all-reduce | flops 512 | bytes 4096 | tf_op jit(solution)/shard_map/psum | solution.py:17
  72.8 0.0 copy-start.3
  72.8 0.0 copy-start.4
  72.8 0.7 broadcast_divide_fusion
  73.5 0.0 copy-done.1
  73.5 2.6 %fusion.20 = bf16[2048,256]{1,0:T(8,128)(2,1)S(1)} fusion(f32[2048,256]{1,0:T(8,128)} %get-tuple-element.35, bf16[1,1,2048,256]{3,2,1,0:T(8,128)(2,1)S(1)} %copy-done.1, f32[]{:T(128)} %get-tuple-element.15, f32[256]{0:T(256)S(1)} %get-tuple-element.46, f32[256]{0:T(256)S(1)} %broadcast_divide_fusion, f32[256]{0:T(256)S(1)} %get-tuple-element.33, ...), kind=kLoop, calls=%fused_computation.28 | loop fusion | flops 5242880 | bytes 4201476 | tf_op jit(solution)/shard_map/convert_element_type | solution.py:416
  76.1 0.0 copy-done.3
  76.1 0.0 copy-done.4
  76.1 0.1 concatenate.12
  76.2 0.0 copy-start.2
  76.2 2.8 %gather_fusion = bf16[704,256]{1,0:T(8,128)(2,1)S(1)} fusion(bf16[2049,256]{1,0:T(8,128)(2,1)S(1)} %concatenate.12, s32[1024]{0:T(1024)S(1)} %pad_clamp_fusion), kind=kCustom, calls=%fused_computation | custom fusion | bytes 723712 | tf_op jit(solution)/shard_map/jit(_take)/gather | solution.py:35
  79.0 1.3 collective-permute-start.1
  80.3 3.8 %collective-permute-start = (bf16[1,1,704,256]{3,2,1,0:T(8,128)(2,1)S(1)}, bf16[1,1,704,256]{3,2,1,0:T(8,128)(2,1)}, u32[]{:S(2)}, u32[]{:S(2)}) collective-permute-start(bf16[1,1,704,256]{3,2,1,0:T(8,128)(2,1)S(1)} %bitcast.92), channel_id=1, source_target_pairs={{0,4},{4,8},{8,12},{12,16},{16,20},{20,24},{24,28},{28,32},{32,36}... | collective-permute-start | bytes 1081352 | tf_op jit(solution)/shard_map/ppermute | solution.py:25
  84.1 0.0 copy-done.2
  84.1 0.4 copy.16
  84.5 5.8 %rev.3 = s32[27,2048]{0,1:T(8,128)} reverse(s32[27,2048]{0,1:T(8,128)S(1)} %bitcast.87), dimensions={0} | reverse | bytes 442368 | tf_op jit(solution)/shard_map/rev | solution.py:54
  90.3 1.4 convert_bitcast_fusion
  91.7 1.0 copy.17
  92.7 1.0 copy.19
  93.7 0.2 reduce_min.33
  94.0 0.0 collective-permute-done.1
  94.0 0.0 collective-permute-done
  94.0 2.2 pad_maximum_fusion.1
  96.2 1.3 collective-permute-start.3
  97.5 5.6 %collective-permute-start.2 = (bf16[3,1,704,256]{3,2,1,0:T(8,128)(2,1)}, bf16[3,1,704,256]{3,2,1,0:T(8,128)(2,1)}, u32[]{:S(2)}, u32[]{:S(2)}) collective-permute-start(bf16[3,1,704,256]{3,2,1,0:T(8,128)(2,1)} %pad_maximum_fusion.1), channel_id=1, source_target_pairs={{0,1},{1,2},{2,3},{4,5},{5,6},{6,7},{8,9},{9,10},{10,11},{12,13},{... | collective-permute-start | bytes 3244040 | tf_op jit(solution)/shard_map/ppermute | solution.py:25
  103.1 0.3 fusion.22
  103.4 0.3 fusion.21
  103.8 0.1 copy.18
  104.0 0.8 reshape.262.starts
  104.8 0.1 pad.13.clone
  104.8 1.1 pad.26.idx
  105.9 19.0 %collective-permute-done.3 = bf16[3,1,704,256]{3,2,1,0:T(8,128)(2,1)} collective-permute-done((bf16[3,1,704,256]{3,2,1,0:T(8,128)(2,1)}, bf16[3,1,704,256]{3,2,1,0:T(8,128)(2,1)}, u32[]{:S(2)}, u32[]{:S(2)}) %collective-permute-start.3) | collective-permute-done | bytes 1081376 | tf_op jit(solution)/shard_map/ppermute | solution.py:28
  124.9 1.6 collective-permute-done.2
  126.5 2.0 pad_maximum_fusion
  128.5 11.4 %maximum_maximum_fusion.table = bf16[8640,256]{1,0:T(8,128)(2,1)} fusion(bf16[6336,256]{1,0:T(8,128)(2,1)S(1)} %bitcast.86, bf16[2048,256]{1,0:T(8,128)(2,1)S(1)} %fusion.20, bf16[8640]{0:T(1024)(128)(2,1)S(1)} %pad.13.clone), kind=kLoop, calls=%fused_computation.1 | loop fusion | flops 13271040 | bytes 8733568 | tf_op jit(solution)/shard_map/concatenate | solution.py:41
  140.0 69.5 %conv_backward.1 = (bf16[2048,256]{1,0:T(8,128)(2,1)}, f32[27,256,256]{2,1,0:T(8,128)}) custom-call(s32[432]{0:T(512)} %reshape.262.starts, f32[2048,128]{1,0:T(8,128)} %pad.26.idx, bf16[8640,256]{1,0:T(8,128)(2,1)} %maximum_maximum_fusion.table, bf16[2048,256]{1,0:T(8,128)(2,1)} %bitcast.97, bf16[27,256,256]{2,1,0:T(8,128)(2,1)} %weight.1), custom_call_target="tpu_custom_call" | custom-call | flops 30000001024 | bytes 20000000 | tf_op jit(solution)/shard_map/conv_backward/pallas_call | solution.py:172
  209.4 0.0 copy-start
  209.4 3.0 %copy-done = f32[27,256,256]{2,1,0:T(8,128)S(1)} copy-done((f32[27,256,256]{2,1,0:T(8,128)S(1)}, f32[27,256,256]{2,1,0:T(8,128)}, u32[]{:S(2)}) %copy-start) | copy-done | bytes 7077912
  212.4 34.5 %scatter_sum.1 = f32[54,256]{1,0:T(8,128)S(1)} custom-call(f32[6912,256]{1,0:T(8,128)S(1)} %bitcast.85), custom_call_target="tpu_custom_call" | custom-call | flops 10000000 | bytes 7000000 | tf_op jit(solution)/shard_map/scatter_sum/pallas_call | solution.py:355
  246.9 0.6 copy.22
  (9 shorter events, 0.1 us)
Async XLA Ops:
  43.5 30.0 %copy-start.1 = (bf16[1,1,2048,256]{3,2,1,0:T(8,128)(2,1)S(1)}, bf16[1,1,2048,256]{3,2,1,0:T(8,128)(2,1)}, u32[]{:S(2)}) copy-start(bf16[1,1,2048,256]{3,2,1,0:T(8,128)(2,1)} %param.10) | copy-start | bytes 3145732
  72.8 3.3 %copy-start.3 = (f32[256]{0:T(256)}, f32[256]{0:T(256)S(1)}, u32[]{:S(2)}) copy-start(f32[256]{0:T(256)S(1)} %get-tuple-element.47) | copy-start | bytes 3076
  72.8 3.3 %copy-start.4 = (f32[256]{0:T(256)}, f32[256]{0:T(256)S(1)}, u32[]{:S(2)}) copy-start(f32[256]{0:T(256)S(1)} %get-tuple-element.46) | copy-start | bytes 3076
  76.2 7.9 %copy-start.2 = (s32[1,1,27,2048]{3,1,2,0:T(1,128)S(1)}, s32[1,1,27,2048]{3,1,2,0:T(1,128)}, u32[]{:S(2)}) copy-start(s32[1,1,27,2048]{3,1,2,0:T(1,128)} %param.15) | copy-start | bytes 663556
  79.0 15.0 %collective-permute-start.1 = (bf16[1,1,704,256]{3,2,1,0:T(8,128)(2,1)S(1)}, bf16[1,1,704,256]{3,2,1,0:T(8,128)(2,1)}, u32[]{:S(2)}, u32[]{:S(2)}) collective-permute-start(bf16[1,1,704,256]{3,2,1,0:T(8,128)(2,1)S(1)} %bitcast.91), channel_id=1, source_target_pairs={{4,0},{8,4},{12,8},{16,12},{20,16},{24,20},{28,24},{32,28},{36,32}... | collective-permute-start | bytes 1081352 | tf_op jit(solution)/shard_map/ppermute | solution.py:28
  80.3 13.7 %collective-permute-start = (bf16[1,1,704,256]{3,2,1,0:T(8,128)(2,1)S(1)}, bf16[1,1,704,256]{3,2,1,0:T(8,128)(2,1)}, u32[]{:S(2)}, u32[]{:S(2)}) collective-permute-start(bf16[1,1,704,256]{3,2,1,0:T(8,128)(2,1)S(1)} %bitcast.92), channel_id=1, source_target_pairs={{0,4},{4,8},{8,12},{12,16},{16,20},{20,24},{24,28},{28,32},{32,36}... | collective-permute-start | bytes 1081352 | tf_op jit(solution)/shard_map/ppermute | solution.py:25
  96.2 28.7 %collective-permute-start.3 = (bf16[3,1,704,256]{3,2,1,0:T(8,128)(2,1)}, bf16[3,1,704,256]{3,2,1,0:T(8,128)(2,1)}, u32[]{:S(2)}, u32[]{:S(2)}) collective-permute-start(bf16[3,1,704,256]{3,2,1,0:T(8,128)(2,1)} %pad_maximum_fusion.1), channel_id=1, source_target_pairs={{1,0},{2,1},{3,2},{5,4},{6,5},{7,6},{9,8},{10,9},{11,10},{13,12},{... | collective-permute-start | bytes 3244040 | tf_op jit(solution)/shard_map/ppermute | solution.py:28
  97.5 29.0 %collective-permute-start.2 = (bf16[3,1,704,256]{3,2,1,0:T(8,128)(2,1)}, bf16[3,1,704,256]{3,2,1,0:T(8,128)(2,1)}, u32[]{:S(2)}, u32[]{:S(2)}) collective-permute-start(bf16[3,1,704,256]{3,2,1,0:T(8,128)(2,1)} %pad_maximum_fusion.1), channel_id=1, source_target_pairs={{0,1},{1,2},{2,3},{4,5},{5,6},{6,7},{8,9},{9,10},{10,11},{12,13},{... | collective-permute-start | bytes 3244040 | tf_op jit(solution)/shard_map/ppermute | solution.py:25
  209.4 3.0 %copy-start = (f32[27,256,256]{2,1,0:T(8,128)S(1)}, f32[27,256,256]{2,1,0:T(8,128)}, u32[]{:S(2)}) copy-start(f32[27,256,256]{2,1,0:T(8,128)} %get-tuple-element.7) | copy-start | bytes 21233668

commit v3 on v2

--- a/solution.py
+++ b/solution.py
@@ -1,5 +1,3 @@
-import functools
-
 import jax
 import jax.numpy as jnp
 from jax import lax
@@ -13,34 +11,6 @@
 MESH = pl.DeviceIdType.MESH
 
 
-def one_axis_at_a_time(shard, axes):
-    return functools.reduce(lax.psum, axes, shard)
-
-
-def extended(block, sides, width):
-    for axis, dim in sides:
-        count = lax.axis_size(axis)
-        forward = [(i, i + 1) for i in range(count - 1)]
-        backward = [(target, source) for source, target in forward]
-        low = lax.ppermute(
-            lax.slice_in_dim(block, block.shape[dim] - width, None, axis=dim), axis, forward
-        )
-        high = lax.ppermute(lax.slice_in_dim(block, 0, width, axis=dim), axis, backward)
-        block = jnp.concatenate([low, block, high], axis=dim)
-    return block
-
-
-def gather_rows(local, border):
-    padded = jnp.concatenate([local, jnp.zeros((1, local.shape[1]), local.dtype)], axis=0)
-    return jnp.take(padded, border, axis=0, mode="clip")
-
-
-def make_table(local, around):
-    flat = around.reshape(-1, local.shape[1])
-    tail = jnp.zeros((WIN, C), local.dtype)
-    return jnp.concatenate([local, flat, tail], axis=0)
-
-
 C = 256
 R = 2048
 SUB = 128
@@ -50,22 +20,6 @@
 FAR = 1.0e6
 
 
-def plan_windows(links):
-    idx = links[::-1]
-    idx = jnp.where(idx < NROW, idx, jnp.int32(FAR))
-    cut = idx.reshape(9, 3, R // SUB, SUB)
-    starts = []
-    for _ in range(3):
-        low = jnp.min(cut, axis=(1, 3))
-        start = jnp.where(low < NROW, low // 16 * 16, jnp.int32(FAR))
-        starts.append(start)
-        cut = jnp.where(cut >= start[:, None, :, None] + WIN, cut, jnp.int32(FAR))
-    first, second, third = starts
-    starts = jnp.stack([jnp.minimum(first, NROW), jnp.minimum(second, NROW), third], axis=-1)
-    columns = jnp.pad(idx.astype(jnp.float32).T, ((0, 0), (0, 5)), constant_values=FAR)
-    return columns, starts.reshape(-1)
-
-
 def one_hot(columns, start):
     lanes = lax.broadcasted_iota(jnp.int32, (SUB, WIN), 1).astype(jnp.float32)
     place = columns - start.astype(jnp.float32)
@@ -79,6 +33,7 @@
 def conv_kernel(starts, idx, table, feat, weight, in_grad, wgrad, acc, feat_t, picked, colbuf):
     step = pl.program_id(0)
     tiles = R // TILE
+    lane0 = jnp.maximum(24 - 3 * step, 0)
 
     @pl.when(step == 0)
     def _():
@@ -92,13 +47,13 @@
     def gather(t, slot):
         for half in range(TILE // SUB):
             row = pl.multiple_of(t * TILE + half * SUB, SUB)
-            at = (step * (R // SUB) + t * (TILE // SUB) + half) * 3
-            columns = pltpu.roll(idx[pl.ds(row, SUB), :], (128 - 3 * step) % 128, 1)
+            at = (t * (TILE // SUB) + half) * 8
+            columns = pltpu.roll(idx[pl.ds(row, SUB), :], (128 - lane0) % 128, 1)
             colbuf[pl.ds(half * SUB, SUB), :] = columns
             total = None
-            cols = [jnp.broadcast_to(columns[:, i : i + 1], (SUB, WIN)) for i in range(3)]
+            cols = [jnp.broadcast_to(columns[:, 2 - i : 3 - i], (SUB, WIN)) for i in range(3)]
             for w in range(2):
-                start = pl.multiple_of(starts[at + w], 16)
+                start = pl.multiple_of(starts[at + w, lane0], 16)
                 hot = jnp.concatenate([one_hot(c, start) for c in cols], axis=0)
                 part = dot(hot, table[pl.ds(start, WIN), :], ((1,), (0,)))
                 total = part if total is None else total + part
@@ -109,12 +64,12 @@
     def gather_rest(t, slot):
         for half in range(TILE // SUB):
             row = pl.multiple_of(t * TILE + half * SUB, SUB)
-            at = (step * (R // SUB) + t * (TILE // SUB) + half) * 3
+            at = (t * (TILE // SUB) + half) * 8
 
             def more(start):
                 columns = colbuf[pl.ds(half * SUB, SUB), :]
                 start = pl.multiple_of(start, 16)
-                cols = [jnp.broadcast_to(columns[:, i : i + 1], (SUB, WIN)) for i in range(3)]
+                cols = [jnp.broadcast_to(columns[:, 2 - i : 3 - i], (SUB, WIN)) for i in range(3)]
                 hot = jnp.concatenate([one_hot(c, start) for c in cols], axis=0)
                 part = dot(hot, table[pl.ds(start, WIN), :], ((1,), (0,))).astype(jnp.bfloat16)
                 for i in range(3):
@@ -126,7 +81,7 @@
                 low = jnp.min(jnp.where(ahead, columns, FAR)).astype(jnp.int32)
                 return jnp.where(low < NROW, low // 16 * 16, jnp.int32(FAR))
 
-            lax.while_loop(lambda start: start < NROW, more, starts[at + 2])
+            lax.while_loop(lambda start: start < NROW, more, starts[at + 2, lane0])
 
     def dense(t, slot):
         rows = pl.ds(pl.multiple_of(t * TILE, TILE), TILE)
@@ -167,7 +122,6 @@
 
 
 def convolve(starts, idx, table, feat, weight):
-    idx = jnp.pad(idx, ((0, 0), (0, 96)), constant_values=FAR)
     whole = pl.BlockSpec(memory_space=pltpu.VMEM)
     in_grad, wgrad = pl.pallas_call(
         conv_kernel,
@@ -381,48 +335,309 @@
     )(part)
 
 
+HB = 704
+ROWS = NROW + WIN
+
+
+def seg(b):
+    return R + b * HB
+
+
+def front_kernel(
+    count, pre, cot, gamma, beta, links, border,
+    table, columns, starts, gamma_grad, beta_grad,
+    grad, pick, near, far, near_sem, far_sem, halo_sem,
+):
+    f32 = jnp.float32
+    z, y, core, x = (lax.axis_index(a) for a in GX_GY)
+    slab = (z * 4 + y) * 2 + core
+    me_near, me_far = x * 2 + core, z * 4 + y
+
+    def near_id(p):
+        return {"gy": p // 2, "gx_2": lax.rem(p, 2)}
+
+    def far_id(p):
+        return {"gx_0": p // 4, "gx_1": lax.rem(p, 4)}
+
+    def slab_id(s):
+        return {"gx_0": s // 8, "gx_1": lax.rem(s // 2, 4), "gx_2": lax.rem(s, 2)}
+
+    barrier = pltpu.get_barrier_semaphore()
+    for d in range(1, 8):
+        pl.semaphore_signal(
+            barrier, 1, device_id=near_id(lax.rem(me_near + d, 8)), device_id_type=MESH
+        )
+    for d in range(1, 16):
+        pl.semaphore_signal(
+            barrier, 1, device_id=far_id(lax.rem(me_far + d, 16)), device_id_type=MESH
+        )
+    up, down = (core == 1) & (slab < 31), (core == 0) & (slab > 0)
+
+    @pl.when(up)
+    def _():
+        pl.semaphore_signal(barrier, 1, device_id=slab_id(slab + 1), device_id_type=MESH)
+
+    @pl.when(down)
+    def _():
+        pl.semaphore_signal(barrier, 1, device_id=slab_id(slab - 1), device_id_type=MESH)
+
+    live_rows = count[0, 0]
+    block = 128
+
+    def live_at(t):
+        row = lax.broadcasted_iota(jnp.int32, (block, C), 0) + t * block
+        return row < live_rows
+
+    def rows_at(t):
+        return pl.ds(pl.multiple_of(t * block, block), block)
+
+    def fold(a):
+        return jnp.sum(a.reshape(block // 8, 8, C), axis=0)
+
+    def first_sums(t, sums):
+        zval = pre[rows_at(t), :].astype(f32)
+        zlive = jnp.where(live_at(t), zval, 0.0)
+        return sums[0] + fold(zlive), sums[1] + fold(zlive * zval)
+
+    zero = jnp.zeros((8, C), f32)
+    line = lax.broadcasted_iota(jnp.int32, (8, C), 0)
+
+    def stacked(a, b, c):
+        a, b = jnp.sum(a, axis=0, keepdims=True), jnp.sum(b, axis=0, keepdims=True)
+        return jnp.where(line == 0, a, jnp.where(line == 1, b, jnp.where(line == 2, c, 0.0)))
+
+    def exchange(slots, me, size, sems, turn, ids):
+        copies = []
+        for d in range(1, size):
+            copies.append(
+                pltpu.make_async_remote_copy(
+                    src_ref=slots.at[turn, me],
+                    dst_ref=slots.at[turn, me],
+                    send_sem=sems.at[turn, 0, d - 1],
+                    recv_sem=sems.at[turn, 1, d - 1],
+                    device_id=ids(lax.rem(me + d, size)),
+                    device_id_type=MESH,
+                )
+            )
+            copies[-1].start()
+        return copies
+
+    def add_up(slots, size, turn, copies):
+        for copy in copies:
+            copy.wait_recv()
+        total = slots[turn, 0]
+        for i in range(1, size):
+            total = total + slots[turn, i]
+        return total
+
+    def all_sum(turn, value, meanwhile):
+        near[turn, me_near] = value
+        one = exchange(near, me_near, 8, near_sem, turn, near_id)
+        meanwhile()
+        far[turn, me_far] = add_up(near, 8, turn, one)
+        two = exchange(far, me_far, 16, far_sem, turn, far_id)
+        total = add_up(far, 16, turn, two)
+        for copy in one + two:
+            copy.wait_send()
+        return total
+
+    def plan():
+        lane = lax.broadcasted_iota(jnp.int32, (1, 128), 1)
+        third = lax.rem(lane, 3)
+
+        @pl.loop(0, R // SUB)
+        def _(j):
+            at = pl.ds(pl.multiple_of(j * SUB, SUB), SUB)
+            idx = links[:, at]
+            idx = jnp.where(idx < NROW, idx, jnp.int32(FAR)).astype(f32)
+            idx = jnp.concatenate([idx, jnp.full((101, SUB), FAR, f32)], axis=0).T
+            columns[at, :] = idx
+            begin = []
+            for w in range(3):
+                low = jnp.min(idx, axis=0, keepdims=True)
+                low = jnp.minimum(low, jnp.minimum(pltpu.roll(low, 127, 1), pltpu.roll(low, 126, 1)))
+                low = jnp.where(
+                    third == 0,
+                    low,
+                    jnp.where(third == 1, pltpu.roll(low, 1, 1), pltpu.roll(low, 2, 1)),
+                )
+                start = jnp.where(low < NROW, jnp.floor(low * 0.0625) * 16.0, FAR)
+                idx = jnp.where(idx >= start + WIN, idx, FAR)
+                begin.append(jnp.minimum(start, float(NROW)) if w < 2 else start)
+            begin = [jnp.broadcast_to(b, (8, 128)) for b in begin]
+            row = lax.broadcasted_iota(jnp.int32, (8, 128), 0)
+            begin = jnp.where(row == 0, begin[0], jnp.where(row == 1, begin[1], begin[2]))
+            starts[pl.ds(pl.multiple_of(j * 8, 8), 8), :] = begin.astype(jnp.int32)
+
+    def choose():
+        @pl.loop(0, 11)
+        def _(t):
+            at = pl.ds(pl.multiple_of(t * 64, 64), 64)
+            wanted = jnp.broadcast_to(border[at, :], (64, R))
+            row = lax.broadcasted_iota(jnp.int32, (64, R), 1)
+            pick[at, :] = jnp.where(wanted == row, 1.0, 0.0).astype(jnp.bfloat16)
+
+        def clear(at, size):
+            table[at : at + size, :] = jnp.zeros((size, C), jnp.bfloat16)
+
+        clear(NROW, WIN)
+
+        @pl.when(slab == 0)
+        def _():
+            for b in (0, 1, 2):
+                clear(seg(b), HB)
+
+        @pl.when(slab == 31)
+        def _():
+            for b in (6, 7, 8):
+                clear(seg(b), WIN)
+
+        for b in (6, 7, 8):
+            clear(seg(b) + WIN, HB - WIN)
+
+        for edge, db in ((0, 0), (3, 2)):
+            @pl.when(x == edge)
+            def _():
+                clear(seg(3 + db), HB)
+
+                @pl.when(slab > 0)
+                def _():
+                    clear(seg(db), HB)
+
+                @pl.when(slab < 31)
+                def _():
+                    clear(seg(6 + db), WIN)
+
+    sum_z, sum_sq = lax.fori_loop(0, R // block, first_sums, (zero, zero))
+    extra = jnp.where(up | down, 1, 0)
+    pl.semaphore_wait(barrier, 22 + extra)
+    whole = all_sum(0, stacked(sum_z, sum_sq, live_rows.astype(f32)), plan)
+    amount = whole[2:3]
+    mean = whole[0:1] / amount
+    var = whole[1:2] / amount - mean * mean
+    rstd = lax.rsqrt(var + 1e-05)
+    gain, shift = gamma[...], beta[...]
+
+    def second_sums(t, sums):
+        zhat = (pre[rows_at(t), :].astype(f32) - mean) * rstd
+        act = gain * zhat + shift
+        sig = jax.nn.sigmoid(act)
+        g = cot[rows_at(t), :].astype(f32) * sig * (1.0 + act * (1.0 - sig))
+        g = jnp.where(live_at(t), g, 0.0)
+        grad[rows_at(t), :] = g
+        return sums[0] + fold(g), sums[1] + fold(g * zhat)
+
+    sum_g, sum_gz = lax.fori_loop(0, R // block, second_sums, (zero, zero))
+    whole = all_sum(1, stacked(sum_g, sum_gz, 0.0), choose)
+    beta_grad[...] = whole[0:1]
+    gamma_grad[...] = whole[1:2]
+    scale = gain * rstd
+    part_g, part_gz = whole[0:1] / amount, whole[1:2] / amount
+
+    @pl.loop(0, R // block)
+    def _(t):
+        zhat = (pre[rows_at(t), :].astype(f32) - mean) * rstd
+        dz = scale * (grad[rows_at(t), :] - part_g - zhat * part_gz)
+        table[rows_at(t), :] = jnp.where(live_at(t), dz, 0.0).astype(jnp.bfloat16)
+
+    @pl.loop(0, 4)
+    def _(t):
+        at = pl.multiple_of(t * 176, 16)
+        rows = dot(pick[pl.ds(at, 176), :], table[0:R, :], ((1,), (0,)))
+        table[pl.ds(pl.multiple_of(seg(4) + at, 16), 176), :] = rows.astype(jnp.bfloat16)
+
+    def hop(source, target, size, device):
+        return pltpu.make_async_remote_copy(
+            src_ref=table.at[pl.ds(seg(source), size), :],
+            dst_ref=table.at[pl.ds(seg(target), size), :],
+            send_sem=halo_sem.at[0, target],
+            recv_sem=halo_sem.at[1, target],
+            device_id=device,
+            device_id_type=MESH,
+        )
+
+    def right():
+        return hop(4, 3, HB, {"gy": x + 1})
+
+    def left():
+        return hop(4, 5, HB, {"gy": x - 1})
+
+    def ahead(db):
+        return hop(3 + db, db, HB, slab_id(slab + 1))
+
+    def behind(db):
+        return hop(3 + db, 6 + db, WIN, slab_id(slab - 1))
+
+    has_right, has_left, has_next, has_last = x < 3, x > 0, slab < 31, slab > 0
+
+    def when(cond, act):
+        @pl.when(cond)
+        def _():
+            act()
+
+    when(has_right, lambda: right().start())
+    when(has_left, lambda: left().start())
+    when(has_next, lambda: ahead(1).start())
+    when(has_last, lambda: behind(1).start())
+    for db, there, came in ((0, has_left, right), (2, has_right, left)):
+        when(there, lambda: came().wait_recv())
+        when(there & has_next, lambda: ahead(db).start())
+        when(there & has_last, lambda: behind(db).start())
+    for db, there in ((1, True), (0, has_left), (2, has_right)):
+        when(has_last & there, lambda: ahead(db).wait_recv())
+        when(has_next & there, lambda: behind(db).wait_recv())
+    when(has_right, lambda: right().wait_send())
+    when(has_left, lambda: left().wait_send())
+    for db, there in ((1, True), (0, has_left), (2, has_right)):
+        when(has_next & there, lambda: ahead(db).wait_send())
+        when(has_last & there, lambda: behind(db).wait_send())
+
+
+def front(counts, pre_norm, out_grad, gamma, beta, links, border):
+    vmem = pl.BlockSpec(memory_space=pltpu.VMEM)
+    return pl.pallas_call(
+        front_kernel,
+        out_shape=(
+            jax.ShapeDtypeStruct((ROWS, C), jnp.bfloat16),
+            jax.ShapeDtypeStruct((R, 128), jnp.float32),
+            jax.ShapeDtypeStruct((R // SUB * 8, 128), jnp.int32),
+            jax.ShapeDtypeStruct((1, C), jnp.float32),
+            jax.ShapeDtypeStruct((1, C), jnp.float32),
+        ),
+        in_specs=[pl.BlockSpec(memory_space=pltpu.SMEM)] + [vmem] * 6,
+        out_specs=(vmem,) * 5,
+        scratch_shapes=[
+            pltpu.VMEM((R, C), jnp.float32),
+            pltpu.VMEM((HB, R), jnp.bfloat16),
+            pltpu.VMEM((2, 8, 8, C), jnp.float32),
+            pltpu.VMEM((2, 16, 8, C), jnp.float32),
+            pltpu.SemaphoreType.DMA((2, 2, 7)),
+            pltpu.SemaphoreType.DMA((2, 2, 15)),
+            pltpu.SemaphoreType.DMA((2, 9)),
+        ],
+        compiler_params=pltpu.CompilerParams(
+            collective_id=0, has_side_effects=True, vmem_limit_bytes=40 * 1024 * 1024
+        ),
+        cost_estimate=pl.CostEstimate(
+            flops=1_000_000_000, bytes_accessed=10_000_000, transcendentals=1_000_000
+        ),
+        name="front",
+    )(counts, pre_norm, out_grad, gamma, beta, links, border)
+
+
 def body(features, pre_norm, out_grad, weight, gamma, beta, neighbors, boundary, counts):
-    feat = features[0, 0]
-    rows = feat.shape[0]
-    chans = feat.shape[1]
-    border = boundary[0, 0]
-    links = neighbors[0, 0]
-    live = (lax.iota(jnp.int32, rows) < counts[0, 0])[:, None]
-    zval = pre_norm[0, 0].astype(jnp.float32)
-    zlive = jnp.where(live, zval, jnp.float32(0.0))
-    sum_z, sum_sq, sum_count = (
-        one_axis_at_a_time(jnp.sum(zlive, axis=0), GX_GY),
-        one_axis_at_a_time(jnp.sum(zlive * zval, axis=0), GX_GY),
-        one_axis_at_a_time(counts[0].astype(jnp.float32), GX_GY),
+    table, columns, starts, gamma_grad, beta_grad = front(
+        counts,
+        pre_norm[0, 0],
+        out_grad[0, 0],
+        gamma[None],
+        beta[None],
+        neighbors[0, 0],
+        boundary[0, 0][:, None],
     )
-    count = sum_count[0]
-    mean = sum_z / count
-    var = sum_sq / count - mean * mean
-    rstd = lax.rsqrt(var + 1e-05)
-    zhat = (zval - mean) * rstd
-    act = gamma * zhat + beta
-    sig = jax.nn.sigmoid(act)
-    grad_act = jnp.where(
-        live, out_grad[0, 0].astype(jnp.float32) * sig * (1.0 + act * (1.0 - sig)), jnp.float32(0.0)
-    )
-    beta_grad, gamma_grad = (
-        one_axis_at_a_time(jnp.sum(grad_act, axis=0), GX_GY),
-        one_axis_at_a_time(jnp.sum(grad_act * zhat, axis=0), GX_GY),
-    )
-    dz = jnp.where(
-        live,
-        gamma * rstd * (grad_act - beta_grad / count - zhat * gamma_grad / count),
-        jnp.float32(0.0),
-    ).astype(jnp.bfloat16)
-    grad_edge = gather_rows(dz, border)
-    grad_around = extended(grad_edge[None, None], ((GX, 0), ("gy", 1)), 1)
-    grad_table = make_table(dz, grad_around)
-
-    idx, starts = plan_windows(links)
-    in_grad, local_wgrad = convolve(starts, idx, grad_table, feat, weight)
+    in_grad, local_wgrad = convolve(starts, columns, table, features[0, 0], weight)
     weight_grad = scatter_sum(local_wgrad)
-    in_grad = in_grad[None, None]
-    return (in_grad, weight_grad, gamma_grad, beta_grad)
+    return (in_grad[None, None], weight_grad, gamma_grad[0], beta_grad[0])
 
 
 def solution(mesh):

time: 248 us -> 170 us (0.69)
  blocking collectives: 64.1 us -> 0 us
  Pallas kernels: 104 us -> 153 us
  other arithmetic: 28.6 us -> 0 us
  waiting for transfers between devices: 20.7 us -> 0 us
  starting transfers between devices: 11.9 us -> 0 us
  local copies, waits for them, and re-layouts: 16.8 us -> 14.2 us
    psum x8 -> x0, blocking collectives: 64.1 us -> none  [one_axis_at_a_time(): return functools.reduce(lax.psum, axes, shard)]
    pallas_call x0 -> x1, Pallas kernels: none -> 45.3 us  [front(): pl.pallas_call(front_kernel, out_shape=(jax.ShapeDtypeStruct((ROWS, C), j...]
    ppermute x4 -> x0, waiting for transfers between devices: 20.7 us -> none  [the longest x2 19 us: extended(): lax.ppermute(lax.slice_in_dim(block, 0, width, axis=dim), axis, backward)]
    concatenate x3 -> x0, other arithmetic: 15.6 us -> none  [the longest x1 11.4 us: make_table(): return jnp.concatenate([local, flat, tail], axis=0)]
    ppermute x4 -> x0, starting transfers between devices: 11.9 us -> none  [the longest x2 9.35 us: extended(): lax.ppermute(lax.slice_in_dim(block, block.shape[dim] - width, None, axis...]
    unnamed x14 -> x20, local copies, waits for them, and re-layouts: 5.02 us -> 13.3 us
    rev x1 -> x0, local copies, waits for them, and re-layouts: 5.85 us -> none  [plan_windows(): idx = links[::-1]]
    reduce_sum x2 -> x0, other arithmetic: 5.34 us -> none  [the longest x1 3.72 us: body(): jnp.sum(grad_act, axis=0)]
  transfers between devices with their start and end apart: 4 -> 0, of which waited for: 2 -> 0; matrix products, arithmetic and copies ran while one was open for 5% -> 0% of each run, Pallas kernels for 0% -> 0%
where the time goes in v3:
time: 170 us; the launch traced here: 169 us
  Pallas kernels  153 us (90%)
  local copies, waits for them, and re-layouts  14.2 us (8%)
    pallas_call x1, Pallas kernels, convolve(): pl.pallas_call(conv_kernel, grid=(10,), out_shape=(jax.ShapeDtypeStruct((...  70 us
    pallas_call x1, Pallas kernels, front(): pl.pallas_call(front_kernel, out_shape=(jax.ShapeDtypeStruct((ROWS, C), j...  45.3 us
    pallas_call x1, Pallas kernels, scatter_sum(): pl.pallas_call(scatter_kernel, out_shape=jax.ShapeDtypeStruct((54, C), jn...  37.7 us
    unnamed x20, local copies, waits for them, and re-layouts  13.3 us

profile of v3, /device:TPU:0, one launch (start us, length us, event | category | flops | bytes accessed | tf_op | source)
XLA Modules:
  0.0 168.6 jit_solution(17662082467594482653)
XLA Ops:
  1.3 1.0 copy.16
  2.3 0.9 copy.13.border
  3.2 0.0 copy-start.1
  3.2 1.2 copy-done.1
  4.4 0.0 copy-start.2
  4.4 1.2 copy-done.2
  5.6 0.0 copy-start.3
  5.6 0.7 copy-done.3
  6.3 0.0 copy-start.4
  6.3 0.7 copy-done.4
  7.0 45.3 %front.1 = (bf16[8640,256]{1,0:T(8,128)(2,1)S(1)}, f32[2048,128]{1,0:T(8,128)S(1)}, s32[128,128]{1,0:T(8,128)S(1)}, f32[1,256]{1,0:T(1,128)S(1)}, f32[1,256]{1,0:T(1,128)S(1)}) custom-call(s32[1,1]{1,0:T(1,128)S(6)} %copy.20.count, bf16[2048,256]{1,0:T(8,128)(2,1)S(1)} %bitcast.17, bf16[2048,256]{1,0:T(8,128)(2,1)S(1)} %bitcast.18, f32[1,256]{1,0:T(1,128)S(1)} %bitcast.19, ...), custom_call_target="tpu_custom_call" | custom-call | flops 1000000000 | bytes 10000000 | tf_op jit(solution)/shard_map/front/pallas_call | solution.py:598
  52.3 0.0 copy-start.5
  52.3 2.1 %copy-done.5 = bf16[8640,256]{1,0:T(8,128)(2,1)} copy-done((bf16[8640,256]{1,0:T(8,128)(2,1)}, bf16[8640,256]{1,0:T(8,128)(2,1)S(1)}, u32[]{:S(2)}) %copy-start.5) | copy-done | bytes 4423704
  54.5 0.0 copy-start.6
  54.5 1.0 copy-done.6
  55.5 0.0 copy-start.7
  55.5 0.6 copy-done.7
  56.1 70.0 %conv_backward.1 = (bf16[2048,256]{1,0:T(8,128)(2,1)}, f32[27,256,256]{2,1,0:T(8,128)}) custom-call(s32[128,128]{1,0:T(8,128)} %copy-done.7, f32[2048,128]{1,0:T(8,128)} %copy-done.6, bf16[8640,256]{1,0:T(8,128)(2,1)} %copy-done.5, bf16[2048,256]{1,0:T(8,128)(2,1)} %bitcast.22, bf16[27,256,256]{2,1,0:T(8,128)(2,1)} %weight.1), custom_call_target="tpu_custom_call" | custom-call | flops 30000001024 | bytes 20000000 | tf_op jit(solution)/shard_map/conv_backward/pallas_call | solution.py:126
  126.1 0.0 copy-start
  126.1 3.0 %copy-done = f32[27,256,256]{2,1,0:T(8,128)S(1)} copy-done((f32[27,256,256]{2,1,0:T(8,128)S(1)}, f32[27,256,256]{2,1,0:T(8,128)}, u32[]{:S(2)}) %copy-start) | copy-done | bytes 7077912
  129.1 37.7 %scatter_sum.1 = f32[54,256]{1,0:T(8,128)S(1)} custom-call(f32[6912,256]{1,0:T(8,128)S(1)} %bitcast.13), custom_call_target="tpu_custom_call" | custom-call | flops 10000000 | bytes 7000000 | tf_op jit(solution)/shard_map/scatter_sum/pallas_call | solution.py:309
  166.8 0.6 copy.21
  167.5 0.6 copy.22
  168.0 0.6 copy.23
Async XLA Ops:
  3.2 1.2 copy-start.1
  4.4 1.2 copy-start.2
  5.6 0.7 copy-start.3
  6.3 0.7 copy-start.4
  52.3 2.2 %copy-start.5 = (bf16[8640,256]{1,0:T(8,128)(2,1)}, bf16[8640,256]{1,0:T(8,128)(2,1)S(1)}, u32[]{:S(2)}) copy-start(bf16[8640,256]{1,0:T(8,128)(2,1)S(1)} %get-tuple-element.13.table) | copy-start | bytes 13271044
  54.5 1.0 copy-start.6
  55.5 0.6 copy-start.7
  126.1 3.0 %copy-start = (f32[27,256,256]{2,1,0:T(8,128)S(1)}, f32[27,256,256]{2,1,0:T(8,128)}, u32[]{:S(2)}) copy-start(f32[27,256,256]{2,1,0:T(8,128)} %get-tuple-element.15) | copy-start | bytes 21233668

commit v4 on v3

--- a/solution.py
+++ b/solution.py
@@ -14,10 +14,13 @@
 C = 256
 R = 2048
 SUB = 128
-TILE = 256
 WIN = 256
 NROW = 8384
 FAR = 1.0e6
+
+
+def dot(a, b, dims):
+    return lax.dot_general(a, b, (dims, ((), ())), preferred_element_type=jnp.float32)
 
 
 def one_hot(columns, start):
@@ -25,99 +28,69 @@
     place = columns - start.astype(jnp.float32)
     return jnp.where(place == lanes, 1.0, 0.0).astype(jnp.bfloat16)
 
-
-def dot(a, b, dims):
-    return lax.dot_general(a, b, (dims, ((), ())), preferred_element_type=jnp.float32)
-
-
-def conv_kernel(starts, idx, table, feat, weight, in_grad, wgrad, acc, feat_t, picked, colbuf):
+def conv_kernel(starts, idx, table, feat, weight, in_grad, wgrad, acc, feat_t, picked):
     step = pl.program_id(0)
-    tiles = R // TILE
-    lane0 = jnp.maximum(24 - 3 * step, 0)
+    lane0 = 24 - 3 * step
 
     @pl.when(step == 0)
     def _():
         acc[...] = jnp.zeros_like(acc)
 
-        @pl.loop(0, tiles)
+        @pl.loop(0, 8)
         def _(t):
-            rows = pl.ds(pl.multiple_of(t * TILE, TILE), TILE)
-            feat_t[t] = feat[rows, :].T
-
-    def gather(t, slot):
-        for half in range(TILE // SUB):
-            row = pl.multiple_of(t * TILE + half * SUB, SUB)
-            at = (t * (TILE // SUB) + half) * 8
-            columns = pltpu.roll(idx[pl.ds(row, SUB), :], (128 - lane0) % 128, 1)
-            colbuf[pl.ds(half * SUB, SUB), :] = columns
-            total = None
-            cols = [jnp.broadcast_to(columns[:, 2 - i : 3 - i], (SUB, WIN)) for i in range(3)]
-            for w in range(2):
-                start = pl.multiple_of(starts[at + w, lane0], 16)
-                hot = jnp.concatenate([one_hot(c, start) for c in cols], axis=0)
-                part = dot(hot, table[pl.ds(start, WIN), :], ((1,), (0,)))
-                total = part if total is None else total + part
-            total = total.astype(jnp.bfloat16)
+            rows = pl.ds(pl.multiple_of(t * 256, 256), 256)
+            feat_t[:, rows] = feat[rows, :].T
+
+    def columns_at(row):
+        columns = pltpu.roll(idx[pl.ds(row, SUB), :], 128 - lane0, 1)
+        return columns
+
+    def window(columns, start):
+        hot = [
+            one_hot(jnp.broadcast_to(columns[:, 2 - i : 3 - i], (SUB, WIN)), start)
+            for i in range(3)
+        ]
+        return jnp.concatenate(hot, axis=0)
+
+    def gather(j):
+        row = j * SUB
+        columns = columns_at(row)
+        s = [pl.multiple_of(starts[j * 8 + w, lane0], 16) for w in range(2)]
+        hots = [window(columns, a) for a in s]
+        tabs = [table[pl.ds(a, WIN), :] for a in s]
+        total = dot(jnp.concatenate(hots, axis=1), jnp.concatenate(tabs, axis=0), ((1,), (0,)))
+        total = total.astype(jnp.bfloat16)
+        for i in range(3):
+            picked[pl.ds(row, SUB), i * C : (i + 1) * C] = total[i * SUB : (i + 1) * SUB]
+
+    def gather_rest(j):
+        row = j * SUB
+
+        def more(start):
+            columns = columns_at(row)
+            start = pl.multiple_of(start, 16)
+            part = dot(window(columns, start), table[pl.ds(start, WIN), :], ((1,), (0,)))
+            part = part.astype(jnp.bfloat16)
             for i in range(3):
-                picked[slot, pl.ds(row, SUB), i * C : (i + 1) * C] = total[i * SUB : (i + 1) * SUB]
-
-    def gather_rest(t, slot):
-        for half in range(TILE // SUB):
-            row = pl.multiple_of(t * TILE + half * SUB, SUB)
-            at = (t * (TILE // SUB) + half) * 8
-
-            def more(start):
-                columns = colbuf[pl.ds(half * SUB, SUB), :]
-                start = pl.multiple_of(start, 16)
-                cols = [jnp.broadcast_to(columns[:, 2 - i : 3 - i], (SUB, WIN)) for i in range(3)]
-                hot = jnp.concatenate([one_hot(c, start) for c in cols], axis=0)
-                part = dot(hot, table[pl.ds(start, WIN), :], ((1,), (0,))).astype(jnp.bfloat16)
-                for i in range(3):
-                    picked[slot, pl.ds(row, SUB), i * C : (i + 1) * C] += part[
-                        i * SUB : (i + 1) * SUB
-                    ]
-                lane = lax.broadcasted_iota(jnp.int32, (SUB, 128), 1)
-                ahead = (lane < 3) & (columns >= (start + WIN).astype(jnp.float32))
-                low = jnp.min(jnp.where(ahead, columns, FAR)).astype(jnp.int32)
-                return jnp.where(low < NROW, low // 16 * 16, jnp.int32(FAR))
-
-            lax.while_loop(lambda start: start < NROW, more, starts[at + 2, lane0])
-
-    def dense(t, slot):
-        rows = pl.ds(pl.multiple_of(t * TILE, TILE), TILE)
-        total = acc[rows, :]
-        for i in range(3):
-            block = picked[slot, rows, i * C : (i + 1) * C]
-            total = total + dot(block, weight[i], ((1,), (1,)))
-            wgrad[i] += dot(feat_t[t], block, ((1,), (0,)))
-        acc[rows, :] = total
-
-    now = step % 2
-
-    @pl.when(step > 0)
+                picked[pl.ds(row, SUB), i * C : (i + 1) * C] += part[i * SUB : (i + 1) * SUB]
+            lane = lax.broadcasted_iota(jnp.int32, (SUB, 128), 1)
+            ahead = (lane < 3) & (columns >= (start + WIN).astype(jnp.float32))
+            low = jnp.min(jnp.where(ahead, columns, FAR)).astype(jnp.int32)
+            return jnp.where(low < NROW, low // 16 * 16, jnp.int32(FAR))
+
+        lax.while_loop(lambda start: start < NROW, more, starts[j * 8 + 2, lane0])
+
+    for j in range(R // SUB):
+        gather(j)
+    for j in range(R // SUB):
+        gather_rest(j)
+    for i in range(3):
+        wgrad[i] = dot(feat_t[...], picked[:, i * C : (i + 1) * C], ((1,), (0,)))
+    turned = jnp.concatenate([weight[i].T for i in range(3)], axis=0)
+    acc[...] += dot(picked[...], turned, ((1,), (0,)))
+
+    @pl.when(step == 8)
     def _():
-        wgrad[...] = jnp.zeros_like(wgrad)
-
-    @pl.when(step == 0)
-    def _():
-        @pl.loop(0, tiles)
-        def _(t):
-            gather(t, now)
-            gather_rest(t, now)
-
-    @pl.when((step > 0) & (step < 9))
-    def _():
-        @pl.loop(0, tiles)
-        def _(t):
-            gather(t, now)
-            dense(t, 1 - now)
-            gather_rest(t, now)
-
-    @pl.when(step == 9)
-    def _():
-        @pl.loop(0, tiles)
-        def _(t):
-            dense(t, 1 - now)
         in_grad[...] = acc[...].astype(jnp.bfloat16)
 
 
@@ -125,7 +98,7 @@
     whole = pl.BlockSpec(memory_space=pltpu.VMEM)
     in_grad, wgrad = pl.pallas_call(
         conv_kernel,
-        grid=(10,),
+        grid=(9,),
         out_shape=(
             jax.ShapeDtypeStruct((R, C), jnp.bfloat16),
             jax.ShapeDtypeStruct((27, C, C), jnp.float32),
@@ -135,19 +108,15 @@
             whole,
             whole,
             whole,
-            pl.BlockSpec((3, C, C), lambda g: (jnp.maximum(g - 1, 0), 0, 0)),
+            pl.BlockSpec((3, C, C), lambda g: (g, 0, 0)),
         ],
-        out_specs=(
-            whole,
-            pl.BlockSpec((3, C, C), lambda g: (jnp.maximum(g - 1, 0), 0, 0)),
-        ),
+        out_specs=(whole, pl.BlockSpec((3, C, C), lambda g: (g, 0, 0))),
         scratch_shapes=[
             pltpu.VMEM((R, C), jnp.float32),
-            pltpu.VMEM((R // TILE, C, TILE), jnp.bfloat16),
-            pltpu.VMEM((2, R, 3 * C), jnp.bfloat16),
-            pltpu.VMEM((TILE, 128), jnp.float32),
+            pltpu.VMEM((C, R), jnp.bfloat16),
+            pltpu.VMEM((R, 3 * C), jnp.bfloat16),
         ],
-        compiler_params=pltpu.CompilerParams(vmem_limit_bytes=56 * 1024 * 1024),
+        compiler_params=pltpu.CompilerParams(vmem_limit_bytes=28 * 1024 * 1024),
         cost_estimate=pl.CostEstimate(
             flops=30_000_000_000, bytes_accessed=20_000_000, transcendentals=0
         ),
@@ -328,7 +297,7 @@
             pltpu.SemaphoreType.DMA((2, 3, 3)),
         ],
         compiler_params=pltpu.CompilerParams(
-            collective_id=1, has_side_effects=True, vmem_limit_bytes=40 * 1024 * 1024
+            collective_id=1, has_side_effects=True, vmem_limit_bytes=24 * 1024 * 1024
         ),
         cost_estimate=pl.CostEstimate(flops=10_000_000, bytes_accessed=7_000_000, transcendentals=0),
         name="scatter_sum",
@@ -616,7 +585,7 @@
             pltpu.SemaphoreType.DMA((2, 9)),
         ],
         compiler_params=pltpu.CompilerParams(
-            collective_id=0, has_side_effects=True, vmem_limit_bytes=40 * 1024 * 1024
+            collective_id=0, has_side_effects=True, vmem_limit_bytes=24 * 1024 * 1024
         ),
         cost_estimate=pl.CostEstimate(
             flops=1_000_000_000, bytes_accessed=10_000_000, transcendentals=1_000_000

time: 170 us -> 138 us (0.81)
  Pallas kernels: 153 us -> 124 us
  local copies, waits for them, and re-layouts: 14.2 us -> 10.6 us
    pallas_call x1, Pallas kernels: 70 us -> 40.9 us  [convolve(): pl.pallas_call(conv_kernel, grid=(9,), out_shape=(jax.ShapeDtypeStruct((R...]
    unnamed x20 -> x16, local copies, waits for them, and re-layouts: 13.3 us -> 9.79 us
where the time goes in v4:
time: 138 us; the launch traced here: 136 us
  Pallas kernels  124 us (90%)
  local copies, waits for them, and re-layouts  10.6 us (8%)
    pallas_call x1, Pallas kernels, front(): pl.pallas_call(front_kernel, out_shape=(jax.ShapeDtypeStruct((ROWS, C), j...  45.3 us
    pallas_call x1, Pallas kernels, convolve(): pl.pallas_call(conv_kernel, grid=(9,), out_shape=(jax.ShapeDtypeStruct((R...  40.9 us
    pallas_call x1, Pallas kernels, scatter_sum(): pl.pallas_call(scatter_kernel, out_shape=jax.ShapeDtypeStruct((54, C), jn...  38.2 us
    unnamed x16, local copies, waits for them, and re-layouts  9.79 us

profile of v4, /device:TPU:0, one launch (start us, length us, event | category | flops | bytes accessed | tf_op | source)
XLA Modules:
  0.0 136.4 jit_solution(17670761343183268410)
XLA Ops:
  1.3 1.0 copy.16
  2.3 0.9 copy.13.border
  3.2 0.0 copy-start.1
  3.2 1.2 copy-done.1
  4.4 0.0 copy-start.2
  4.4 1.2 copy-done.2
  5.6 0.0 copy-start.4
  5.6 0.7 copy-done.4
  6.3 0.0 copy-start.5
  6.3 0.7 copy-done.5
  7.0 45.3 %front.1 = (bf16[8640,256]{1,0:T(8,128)(2,1)S(1)}, f32[2048,128]{1,0:T(8,128)S(1)}, s32[128,128]{1,0:T(8,128)S(1)}, f32[1,256]{1,0:T(1,128)S(1)}, f32[1,256]{1,0:T(1,128)S(1)}) custom-call(s32[1,1]{1,0:T(1,128)S(6)} %copy.20.count, bf16[2048,256]{1,0:T(8,128)(2,1)S(1)} %bitcast.17, bf16[2048,256]{1,0:T(8,128)(2,1)S(1)} %bitcast.18, f32[1,256]{1,0:T(1,128)S(1)} %bitcast.20, ...), custom_call_target="tpu_custom_call" | custom-call | flops 1000000000 | bytes 10000000 | tf_op jit(solution)/shard_map/front/pallas_call | solution.py:567
  52.3 0.0 copy-start
  52.3 2.0 %copy-done = bf16[27,256,256]{2,1,0:T(8,128)(2,1)S(1)} copy-done((bf16[27,256,256]{2,1,0:T(8,128)(2,1)S(1)}, bf16[27,256,256]{2,1,0:T(8,128)(2,1)}, u32[]{:S(2)}) %copy-start) | copy-done | bytes 3538968
  54.3 0.0 copy-start.3
  54.3 1.2 copy-done.3
  55.5 40.9 %conv_backward.1 = (bf16[2048,256]{1,0:T(8,128)(2,1)}, f32[27,256,256]{2,1,0:T(8,128)S(1)}) custom-call(s32[128,128]{1,0:T(8,128)S(1)} %get-tuple-element.11.starts, f32[2048,128]{1,0:T(8,128)S(1)} %get-tuple-element.12.idx, bf16[8640,256]{1,0:T(8,128)(2,1)S(1)} %get-tuple-element.13.table, bf16[2048,256]{1,0:T(8,128)(2,1)S(1)} %bitcast.19, ...), custom_call_target="tpu_custom_call" | custom-call | flops 30000001024 | bytes 20000000 | tf_op jit(solution)/shard_map/conv_backward/pallas_call | solution.py:99
  96.5 38.2 %scatter_sum.1 = f32[54,256]{1,0:T(8,128)S(1)} custom-call(f32[6912,256]{1,0:T(8,128)S(1)} %bitcast.13), custom_call_target="tpu_custom_call" | custom-call | flops 10000000 | bytes 7000000 | tf_op jit(solution)/shard_map/scatter_sum/pallas_call | solution.py:278
  134.7 0.6 copy.21
  135.3 0.6 copy.22
  135.9 0.6 copy.23
Async XLA Ops:
  3.2 1.2 copy-start.1
  4.4 1.2 copy-start.2
  5.6 0.7 copy-start.4
  6.3 0.7 copy-start.5
  52.3 2.0 %copy-start = (bf16[27,256,256]{2,1,0:T(8,128)(2,1)S(1)}, bf16[27,256,256]{2,1,0:T(8,128)(2,1)}, u32[]{:S(2)}) copy-start(bf16[27,256,256]{2,1,0:T(8,128)(2,1)} %weight.1) | copy-start | bytes 10616836
  54.3 1.2 copy-start.3

commit v5 on v4

--- a/solution.py
+++ b/solution.py
@@ -28,18 +28,13 @@
     place = columns - start.astype(jnp.float32)
     return jnp.where(place == lanes, 1.0, 0.0).astype(jnp.bfloat16)
 
-def conv_kernel(starts, idx, table, feat, weight, in_grad, wgrad, acc, feat_t, picked):
+def conv_kernel(starts, idx, table, feat_t, turned, in_grad, wgrad, acc, picked):
     step = pl.program_id(0)
     lane0 = 24 - 3 * step
 
     @pl.when(step == 0)
     def _():
         acc[...] = jnp.zeros_like(acc)
-
-        @pl.loop(0, 8)
-        def _(t):
-            rows = pl.ds(pl.multiple_of(t * 256, 256), 256)
-            feat_t[:, rows] = feat[rows, :].T
 
     def columns_at(row):
         columns = pltpu.roll(idx[pl.ds(row, SUB), :], 128 - lane0, 1)
@@ -86,15 +81,14 @@
         gather_rest(j)
     for i in range(3):
         wgrad[i] = dot(feat_t[...], picked[:, i * C : (i + 1) * C], ((1,), (0,)))
-    turned = jnp.concatenate([weight[i].T for i in range(3)], axis=0)
-    acc[...] += dot(picked[...], turned, ((1,), (0,)))
+    acc[...] += dot(picked[...], turned[0], ((1,), (0,)))
 
     @pl.when(step == 8)
     def _():
         in_grad[...] = acc[...].astype(jnp.bfloat16)
 
 
-def convolve(starts, idx, table, feat, weight):
+def convolve(starts, idx, table, feat_t, turned):
     whole = pl.BlockSpec(memory_space=pltpu.VMEM)
     in_grad, wgrad = pl.pallas_call(
         conv_kernel,
@@ -108,12 +102,11 @@
             whole,
             whole,
             whole,
-            pl.BlockSpec((3, C, C), lambda g: (g, 0, 0)),
+            pl.BlockSpec((1, 3 * C, C), lambda g: (g, 0, 0)),
         ],
         out_specs=(whole, pl.BlockSpec((3, C, C), lambda g: (g, 0, 0))),
         scratch_shapes=[
             pltpu.VMEM((R, C), jnp.float32),
-            pltpu.VMEM((C, R), jnp.bfloat16),
             pltpu.VMEM((R, 3 * C), jnp.bfloat16),
         ],
         compiler_params=pltpu.CompilerParams(vmem_limit_bytes=28 * 1024 * 1024),
@@ -121,30 +114,24 @@
             flops=30_000_000_000, bytes_accessed=20_000_000, transcendentals=0
         ),
         name="conv_backward",
-    )(starts, idx, table, feat, weight)
+    )(starts, idx, table, feat_t, turned)
     return in_grad, wgrad.reshape(27 * C, C)
 
 
 AXES = ("gy", "gx_1", "gx_0")
 TILE_AT = (0, 16, 32, 38)
-HOLDS = ((0,), (1,), (2, 3))
-
-
-def scatter_kernel(part, out, local, s_a, r_a, *rest):
+HOLDS = (((0, 0), (0, 1), (3, 0)), ((1, 0), (1, 1), (3, 1)), ((2, 0), (2, 1)))
+
+
+def scatter_kernel(part, out, s_a, r_a, *rest):
     s_b, r_b, s_c, r_c, s_d, r_d = (rest[3 * i : 3 * i + 3] for i in range(6))
-    load_sem, a_sem, b_sem, c_sem, d_sem = rest[18:]
+    a_sem, b_sem, c_sem, d_sem = rest[18:]
     pos = [lax.axis_index(a) for a in AXES]
     core = lax.axis_index("gx_2")
     z = pos[2]
 
     def around(i):
         return lax.rem(z + 1 + i, 4)
-
-    loads = []
-    for i in range(4):
-        rows = pl.ds(pl.multiple_of(around(i) * 1728, 64), 1728)
-        loads.append(pltpu.make_async_copy(part.at[rows, :], local.at[i], load_sem.at[i]))
-        loads[-1].start()
 
     barrier = pltpu.get_barrier_semaphore()
     pl.semaphore_signal(barrier, 1, device_id={"gx_2": 1 - core}, device_id_type=MESH)
@@ -155,8 +142,8 @@
 
     def block(i, y, x, side, t):
         skip = (x * 54 + TILE_AT[t]) % 8
-        base = (y * 2 + side) * 216 + x * 54 + TILE_AT[t] - skip
-        rows = local[i, pl.ds(pl.multiple_of(base, 8), 24 if skip else 16), :]
+        base = around(i) * 1728 + (y * 2 + side) * 216 + x * 54 + TILE_AT[t] - skip
+        rows = part[pl.ds(pl.multiple_of(base, 8), 24 if skip else 16), :]
         return rows[skip : skip + 16]
 
     sends = []
@@ -176,8 +163,6 @@
 
     first = []
     for i in range(4):
-        loads[i].wait()
-
         @pl.loop(0, 4)
         def _(y):
             for x in range(4):
@@ -213,12 +198,17 @@
                 for t in range(4):
                     both = block(i, y, x, core, t) + r_a[i, y * 4 + x, t].astype(jnp.float32)
                     both = both.astype(jnp.bfloat16)
-                    if t == 0:
-                        s_b[0][x, y * 4 + z_of, 0] = both
-                    elif t == 1:
-                        s_b[1][y, z_of * 4 + x, 0] = both
-                    else:
-                        s_b[2][z_of, x * 4 + y, t - 2] = both
+                    for p, holds in enumerate(HOLDS):
+                        for n, (tile, side) in enumerate(holds):
+                            if tile != t:
+                                continue
+                            piece = both[:, side * 128 : (side + 1) * 128]
+                            if p == 0:
+                                s_b[0][x, y * 4 + z_of, n] = piece
+                            elif p == 1:
+                                s_b[1][y, z_of * 4 + x, n] = piece
+                            else:
+                                s_b[2][z_of, x * 4 + y, n] = piece
 
         if i < 3:
             second[2].append(
@@ -263,8 +253,9 @@
         for copy in fourth[p]:
             copy.wait_recv()
         me = pos[(p + 2) % 3]
-        for t, which in enumerate(HOLDS[p]):
-            out[TILE_AT[which] : TILE_AT[which] + 16, :] = total(s_d[p], r_d[p], (me, t))
+        for n, (tile, side) in enumerate(HOLDS[p]):
+            rows = pl.ds(TILE_AT[tile], 16)
+            out[rows, side * 128 : (side + 1) * 128] = total(s_d[p], r_d[p], (me, n))
 
     for copy in sends:
         copy.wait_send()
@@ -272,16 +263,15 @@
 
 def scatter_sum(part):
     def stage(lead, kind):
-        return [pltpu.VMEM(lead + (len(h), 16, C), kind) for h in HOLDS]
+        return [pltpu.VMEM(lead + (len(h), 16, 128), kind) for h in HOLDS]
 
     half, full = jnp.bfloat16, jnp.float32
     return pl.pallas_call(
         scatter_kernel,
         out_shape=jax.ShapeDtypeStruct((54, C), jnp.float32),
-        in_specs=[pl.BlockSpec(memory_space=pl.ANY)],
+        in_specs=[pl.BlockSpec(memory_space=pltpu.VMEM)],
         out_specs=pl.BlockSpec(memory_space=pltpu.VMEM),
         scratch_shapes=[
-            pltpu.VMEM((4, 1728, C), jnp.float32),
             pltpu.VMEM((4, 16, 4, 16, C), jnp.bfloat16),
             pltpu.VMEM((4, 16, 4, 16, C), jnp.bfloat16),
             *stage((4, 16), half),
@@ -290,7 +280,6 @@
             *stage((3, 4), half),
             *stage((4,), full),
             *stage((3,), full),
-            pltpu.SemaphoreType.DMA((4,)),
             pltpu.SemaphoreType.DMA((2, 4)),
             pltpu.SemaphoreType.DMA((2, 3, 3)),
             pltpu.SemaphoreType.DMA((2, 3, 3)),
@@ -305,6 +294,7 @@
 
 
 HB = 704
+HIGH = 272
 ROWS = NROW + WIN
 
 
@@ -313,9 +303,12 @@
 
 
 def front_kernel(
-    count, pre, cot, gamma, beta, links, border,
-    table, columns, starts, gamma_grad, beta_grad,
-    grad, pick, near, far, near_sem, far_sem, halo_sem,
+    count, pre_in, cot_in, gamma_in, beta_in, links_in, border_in, feat_in, weight_in,
+    table, columns, starts, gamma_grad, beta_grad, feat_t, turned,
+    pre, cot, gamma, beta, links, border, feat, weight,
+    grad, pick, near, far, list_left, list_own, list_right, high,
+    note_own, note_left, note_right, note_out, note_in,
+    load_sem, near_sem, far_sem, halo_sem, note_sem,
 ):
     f32 = jnp.float32
     z, y, core, x = (lax.axis_index(a) for a in GX_GY)
@@ -330,6 +323,20 @@
 
     def slab_id(s):
         return {"gx_0": s // 8, "gx_1": lax.rem(s // 2, 4), "gx_2": lax.rem(s, 2)}
+
+    loads = []
+    for source, target in (
+        (pre_in, pre),
+        (border_in, border),
+        (cot_in, cot),
+        (gamma_in, gamma),
+        (beta_in, beta),
+        (links_in, links),
+        (feat_in, feat),
+        (weight_in, weight),
+    ):
+        loads.append(pltpu.make_async_copy(source, target, load_sem.at[len(loads)]))
+        loads[-1].start()
 
     barrier = pltpu.get_barrier_semaphore()
     for d in range(1, 8):
@@ -410,14 +417,66 @@
             copy.wait_send()
         return total
 
+    def when(cond, act):
+        @pl.when(cond)
+        def _():
+            act()
+
+    has_right, has_left, has_next, has_last = x < 3, x > 0, slab < 31, slab > 0
+
+    def note(source, target, n, device):
+        return pltpu.make_async_remote_copy(
+            src_ref=source,
+            dst_ref=target,
+            send_sem=note_sem.at[0, n],
+            recv_sem=note_sem.at[1, n],
+            device_id=device,
+            device_id_type=MESH,
+        )
+
+    def note_to_right():
+        return note(note_own, note_left, 0, {"gy": x + 1})
+
+    def note_to_left():
+        return note(note_own, note_right, 1, {"gy": x - 1})
+
+    def note_ahead():
+        return note(note_out, note_in, 2, slab_id(slab + 1))
+
+    def blank(ref):
+        ref[...] = jnp.zeros_like(ref)
+
+    def notes_first():
+        size = jnp.sum(jnp.where(border[...] < R, 1, 0), axis=1, keepdims=True)
+        first = jnp.minimum(jnp.maximum(size - WIN, 0) // 16, (HB - HIGH) // 16)
+        note_own[...] = jnp.broadcast_to(first, (8, 128))
+        when(~has_left, lambda: blank(note_left))
+        when(~has_right, lambda: blank(note_right))
+        when(~has_last, lambda: blank(note_in))
+
+    def notes_second():
+        when(has_left, lambda: note_to_right().wait_recv())
+        when(has_right, lambda: note_to_left().wait_recv())
+        row = lax.broadcasted_iota(jnp.int32, (8, 128), 0)
+        note_out[...] = jnp.where(
+            row == 0, note_left[...], jnp.where(row == 1, note_own[...], note_right[...])
+        )
+        when(has_next, lambda: note_ahead().start())
+
     def plan():
+        loads[5].wait()
+        when(has_last, lambda: note_ahead().wait_recv())
+        moved = [note_in[b : b + 1, :] * 16 for b in range(3)]
         lane = lax.broadcasted_iota(jnp.int32, (1, 128), 1)
         third = lax.rem(lane, 3)
 
         @pl.loop(0, R // SUB)
         def _(j):
             at = pl.ds(pl.multiple_of(j * SUB, SUB), SUB)
-            idx = links[:, at]
+            idx = links[:, 0, at]
+            for b in range(3):
+                inside = (idx >= seg(b)) & (idx < seg(b + 1))
+                idx = jnp.where(inside, idx - moved[b], idx)
             idx = jnp.where(idx < NROW, idx, jnp.int32(FAR)).astype(f32)
             idx = jnp.concatenate([idx, jnp.full((101, SUB), FAR, f32)], axis=0).T
             columns[at, :] = idx
@@ -439,12 +498,18 @@
             starts[pl.ds(pl.multiple_of(j * 8, 8), 8), :] = begin.astype(jnp.int32)
 
     def choose():
-        @pl.loop(0, 11)
-        def _(t):
-            at = pl.ds(pl.multiple_of(t * 64, 64), 64)
-            wanted = jnp.broadcast_to(border[at, :], (64, R))
-            row = lax.broadcasted_iota(jnp.int32, (64, R), 1)
-            pick[at, :] = jnp.where(wanted == row, 1.0, 0.0).astype(jnp.bfloat16)
+        lane = lax.broadcasted_iota(jnp.int32, (128, 128), 1)
+        for t in range(6):
+            width = min(128, HB - t * 128)
+            names = border[:, t * 128 : t * 128 + width].astype(f32)
+            if width < 128:
+                names = jnp.concatenate([names, jnp.full((1, 128 - width), FAR, f32)], axis=1)
+            names = jnp.broadcast_to(names, (128, 128)).T[:width]
+            for c in range(R // 128):
+                row = (lane[:width] + c * 128).astype(f32)
+                pick[t * 128 : t * 128 + width, c * 128 : (c + 1) * 128] = jnp.where(
+                    names == row, 1.0, 0.0
+                ).astype(jnp.bfloat16)
 
         def clear(at, size):
             table[at : at + size, :] = jnp.zeros((size, C), jnp.bfloat16)
@@ -454,37 +519,52 @@
         @pl.when(slab == 0)
         def _():
             for b in (0, 1, 2):
-                clear(seg(b), HB)
+                clear(seg(b), HIGH)
 
         @pl.when(slab == 31)
         def _():
             for b in (6, 7, 8):
                 clear(seg(b), WIN)
 
+        for b in (0, 1, 2):
+            clear(seg(b) + HIGH, HB - HIGH)
+
         for b in (6, 7, 8):
             clear(seg(b) + WIN, HB - WIN)
 
-        for edge, db in ((0, 0), (3, 2)):
+        for edge, db, missing in ((0, 0, list_left), (3, 2, list_right)):
             @pl.when(x == edge)
             def _():
-                clear(seg(3 + db), HB)
+                blank(missing)
 
                 @pl.when(slab > 0)
                 def _():
-                    clear(seg(db), HB)
+                    clear(seg(db), HIGH)
 
                 @pl.when(slab < 31)
                 def _():
                     clear(seg(6 + db), WIN)
 
+    loads[0].wait()
     sum_z, sum_sq = lax.fori_loop(0, R // block, first_sums, (zero, zero))
+    loads[1].wait()
+    notes_first()
     extra = jnp.where(up | down, 1, 0)
     pl.semaphore_wait(barrier, 22 + extra)
-    whole = all_sum(0, stacked(sum_z, sum_sq, live_rows.astype(f32)), plan)
+    when(has_right, lambda: note_to_right().start())
+    when(has_left, lambda: note_to_left().start())
+
+    def during_first():
+        choose()
+        notes_second()
+
+    whole = all_sum(0, stacked(sum_z, sum_sq, live_rows.astype(f32)), during_first)
     amount = whole[2:3]
     mean = whole[0:1] / amount
     var = whole[1:2] / amount - mean * mean
     rstd = lax.rsqrt(var + 1e-05)
+    for load in loads[2:5]:
+        load.wait()
     gain, shift = gamma[...], beta[...]
 
     def second_sums(t, sums):
@@ -497,7 +577,7 @@
         return sums[0] + fold(g), sums[1] + fold(g * zhat)
 
     sum_g, sum_gz = lax.fori_loop(0, R // block, second_sums, (zero, zero))
-    whole = all_sum(1, stacked(sum_g, sum_gz, 0.0), choose)
+    whole = all_sum(1, stacked(sum_g, sum_gz, 0.0), plan)
     beta_grad[...] = whole[0:1]
     gamma_grad[...] = whole[1:2]
     scale = gain * rstd
@@ -513,45 +593,60 @@
     def _(t):
         at = pl.multiple_of(t * 176, 16)
         rows = dot(pick[pl.ds(at, 176), :], table[0:R, :], ((1,), (0,)))
-        table[pl.ds(pl.multiple_of(seg(4) + at, 16), 176), :] = rows.astype(jnp.bfloat16)
-
-    def hop(source, target, size, device):
+        list_own[pl.ds(at, 176), :] = rows.astype(jnp.bfloat16)
+
+    def hop(source, target, n, device):
         return pltpu.make_async_remote_copy(
-            src_ref=table.at[pl.ds(seg(source), size), :],
-            dst_ref=table.at[pl.ds(seg(target), size), :],
-            send_sem=halo_sem.at[0, target],
-            recv_sem=halo_sem.at[1, target],
+            src_ref=source,
+            dst_ref=target,
+            send_sem=halo_sem.at[0, n],
+            recv_sem=halo_sem.at[1, n],
             device_id=device,
             device_id_type=MESH,
         )
 
+    lists = (list_left, list_own, list_right)
+
     def right():
-        return hop(4, 3, HB, {"gy": x + 1})
+        return hop(list_own, list_left, 3, {"gy": x + 1})
 
     def left():
-        return hop(4, 5, HB, {"gy": x - 1})
+        return hop(list_own, list_right, 5, {"gy": x - 1})
 
     def ahead(db):
-        return hop(3 + db, db, HB, slab_id(slab + 1))
+        return hop(high.at[db], table.at[pl.ds(seg(db), HIGH), :], db, slab_id(slab + 1))
 
     def behind(db):
-        return hop(3 + db, 6 + db, WIN, slab_id(slab - 1))
-
-    has_right, has_left, has_next, has_last = x < 3, x > 0, slab < 31, slab > 0
-
-    def when(cond, act):
-        @pl.when(cond)
-        def _():
-            act()
+        target = table.at[pl.ds(seg(6 + db), WIN), :]
+        return hop(lists[db].at[pl.ds(0, WIN), :], target, 6 + db, slab_id(slab - 1))
+
+    def pass_on(db, mark):
+        at = jnp.max(mark[...]) * 16
+        high[db] = lists[db][pl.ds(at, HIGH), :]
+        when(has_next, lambda: ahead(db).start())
+        when(has_last, lambda: behind(db).start())
 
     when(has_right, lambda: right().start())
     when(has_left, lambda: left().start())
-    when(has_next, lambda: ahead(1).start())
-    when(has_last, lambda: behind(1).start())
-    for db, there, came in ((0, has_left, right), (2, has_right, left)):
+    pass_on(1, note_own)
+    table[seg(4) : seg(5), :] = list_own[...]
+    loads[6].wait()
+    for t in range(8):
+        feat_t[:, t * 256 : (t + 1) * 256] = feat[t * 256 : (t + 1) * 256, :].T
+    loads[7].wait()
+    for db, there, came, mark in (
+        (0, has_left, right, note_left),
+        (2, has_right, left, note_right),
+    ):
         when(there, lambda: came().wait_recv())
-        when(there & has_next, lambda: ahead(db).start())
-        when(there & has_last, lambda: behind(db).start())
+        when(there, lambda: pass_on(db, mark))
+        table[seg(3 + db) : seg(4 + db), :] = lists[db][...]
+
+    @pl.loop(0, 9)
+    def _(g):
+        for i in range(3):
+            turned[g, i * C : (i + 1) * C, :] = weight[g * 3 + i].T
+
     for db, there in ((1, True), (0, has_left), (2, has_right)):
         when(has_last & there, lambda: ahead(db).wait_recv())
         when(has_next & there, lambda: behind(db).wait_recv())
@@ -560,9 +655,12 @@
     for db, there in ((1, True), (0, has_left), (2, has_right)):
         when(has_next & there, lambda: ahead(db).wait_send())
         when(has_last & there, lambda: behind(db).wait_send())
-
-
-def front(counts, pre_norm, out_grad, gamma, beta, links, border):
+    when(has_right, lambda: note_to_right().wait_send())
+    when(has_left, lambda: note_to_left().wait_send())
+    when(has_next, lambda: note_ahead().wait_send())
+
+
+def front(counts, *arrays):
     vmem = pl.BlockSpec(memory_space=pltpu.VMEM)
     return pl.pallas_call(
         front_kernel,
@@ -572,17 +670,28 @@
             jax.ShapeDtypeStruct((R // SUB * 8, 128), jnp.int32),
             jax.ShapeDtypeStruct((1, C), jnp.float32),
             jax.ShapeDtypeStruct((1, C), jnp.float32),
+            jax.ShapeDtypeStruct((C, R), jnp.bfloat16),
+            jax.ShapeDtypeStruct((9, 3 * C, C), jnp.bfloat16),
         ),
-        in_specs=[pl.BlockSpec(memory_space=pltpu.SMEM)] + [vmem] * 6,
-        out_specs=(vmem,) * 5,
-        scratch_shapes=[
+        in_specs=[pl.BlockSpec(memory_space=pltpu.SMEM)]
+        + [pl.BlockSpec(memory_space=pltpu.HBM)] * 8,
+        out_specs=(vmem,) * 7,
+        scratch_shapes=[pltpu.VMEM(a.shape, a.dtype) for a in arrays]
+        + [
             pltpu.VMEM((R, C), jnp.float32),
             pltpu.VMEM((HB, R), jnp.bfloat16),
             pltpu.VMEM((2, 8, 8, C), jnp.float32),
             pltpu.VMEM((2, 16, 8, C), jnp.float32),
+            pltpu.VMEM((HB, C), jnp.bfloat16),
+            pltpu.VMEM((HB, C), jnp.bfloat16),
+            pltpu.VMEM((HB, C), jnp.bfloat16),
+            pltpu.VMEM((3, HIGH, C), jnp.bfloat16),
+            *[pltpu.VMEM((8, 128), jnp.int32)] * 5,
+            pltpu.SemaphoreType.DMA((8,)),
             pltpu.SemaphoreType.DMA((2, 2, 7)),
             pltpu.SemaphoreType.DMA((2, 2, 15)),
             pltpu.SemaphoreType.DMA((2, 9)),
+            pltpu.SemaphoreType.DMA((2, 3)),
         ],
         compiler_params=pltpu.CompilerParams(
             collective_id=0, has_side_effects=True, vmem_limit_bytes=24 * 1024 * 1024
@@ -591,20 +700,22 @@
             flops=1_000_000_000, bytes_accessed=10_000_000, transcendentals=1_000_000
         ),
         name="front",
-    )(counts, pre_norm, out_grad, gamma, beta, links, border)
+    )(counts, *arrays)
 
 
 def body(features, pre_norm, out_grad, weight, gamma, beta, neighbors, boundary, counts):
-    table, columns, starts, gamma_grad, beta_grad = front(
+    table, columns, starts, gamma_grad, beta_grad, feat_t, turned = front(
         counts,
         pre_norm[0, 0],
         out_grad[0, 0],
         gamma[None],
         beta[None],
-        neighbors[0, 0],
-        boundary[0, 0][:, None],
+        neighbors.reshape(27, 1, R),
+        boundary.reshape(1, HB),
+        features[0, 0],
+        weight,
     )
-    in_grad, local_wgrad = convolve(starts, columns, table, features[0, 0], weight)
+    in_grad, local_wgrad = convolve(starts, columns, table, feat_t, turned)
     weight_grad = scatter_sum(local_wgrad)
     return (in_grad[None, None], weight_grad, gamma_grad[0], beta_grad[0])
 

time: 138 us -> 131 us (0.949); the launches traced: 136 us -> 131 us
  Pallas kernels: 124 us -> 119 us
    pallas_call x1, Pallas kernels: 38.2 us -> 31.8 us  [scatter_sum(): pl.pallas_call(scatter_kernel, out_shape=jax.ShapeDtypeStruct((54, C), jn...]
    pallas_call x1, Pallas kernels: 45.3 us -> 47.1 us  [front(): pl.pallas_call(front_kernel, out_shape=(jax.ShapeDtypeStruct((ROWS, C), j...]
    unnamed x16 -> x19, local copies, waits for them, and re-layouts: 9.79 us -> 10.4 us
where the time goes in v5:
time: 131 us
  Pallas kernels  119 us (91%)
  local copies, waits for them, and re-layouts  10.4 us (8%)
  between operations  1.31 us (1%)
    pallas_call x1, Pallas kernels, front(): pl.pallas_call(front_kernel, out_shape=(jax.ShapeDtypeStruct((ROWS, C), j...  47.1 us
    pallas_call x1, Pallas kernels, convolve(): pl.pallas_call(conv_kernel, grid=(9,), out_shape=(jax.ShapeDtypeStruct((R...  40.4 us
    pallas_call x1, Pallas kernels, scatter_sum(): pl.pallas_call(scatter_kernel, out_shape=jax.ShapeDtypeStruct((54, C), jn...  31.8 us
    unnamed x19, local copies, waits for them, and re-layouts  10.4 us

profile of v5, /device:TPU:0, one launch (start us, length us, event | category | flops | bytes accessed | tf_op | source)
XLA Modules:
  0.0 130.9 jit_solution(3893834588197573896)
XLA Ops:
  1.3 0.0 copy-start
  1.3 2.0 %copy-done = bf16[27,256,256]{2,1,0:T(8,128)(2,1)S(1)} copy-done((bf16[27,256,256]{2,1,0:T(8,128)(2,1)S(1)}, bf16[27,256,256]{2,1,0:T(8,128)(2,1)}, u32[]{:S(2)}) %copy-start) | copy-done | bytes 3538968
  3.3 0.0 copy-start.1
  3.3 1.2 copy-done.1
  4.5 0.0 copy-start.2
  4.5 1.2 copy-done.2
  5.7 0.0 copy-start.3
  5.7 1.2 copy-done.3
  7.0 0.0 copy-start.4
  7.0 0.9 copy-done.4
  7.9 0.0 copy-start.5
  7.9 0.7 copy-done.5
  8.6 0.0 copy-start.6
  8.6 0.7 copy-done.6
  9.3 0.0 copy-start.7
  9.3 0.7 copy-done.7
  9.9 47.1 %front.1 = (bf16[8640,256]{1,0:T(8,128)(2,1)S(1)}, f32[2048,128]{1,0:T(8,128)S(1)}, s32[128,128]{1,0:T(8,128)S(1)}, f32[1,256]{1,0:T(1,128)S(1)}, f32[1,256]{1,0...) custom-call(s32[1,1]{1,0:T(1,128)S(6)} %copy.16.count, bf16[2048,256]{1,0:T(8,128)(2,1)S(1)} %bitcast.12, ...), custom_call_target="tpu_custom_call" | custom-call | flops 1000000000 | bytes 10000000 | tf_op jit(solution)/shard_map/front/pallas_call | solution.py:665
  57.0 40.4 %conv_backward.1 = (bf16[2048,256]{1,0:T(8,128)(2,1)}, f32[27,256,256]{2,1,0:T(8,128)S(1)}) custom-call(s32[128,128]{1,0:T(8,128)S(1)} %get-tuple-element.13.starts, f32[2048,128]{1,0:T(8,128)S(1)} %get-tuple-element.14.idx, bf16[8640,256]{1,0:T(8,128)(2,1)S(1)} %get-tuple-element.15.table, bf16[256,2048]{1,0:T(8,128)(2,1)S(1)} %get-tuple-element.16.feat_t, ...), custom_call_target="tpu_custom_call" | custom-call | flops 30000001024 | bytes 20000000 | tf_op jit(solution)/shard_map/conv_backward/pallas_call | solution.py:93
  97.4 31.8 %scatter_sum.1 = f32[54,256]{1,0:T(8,128)S(1)} custom-call(f32[6912,256]{1,0:T(8,128)S(1)} %bitcast.11), custom_call_target="tpu_custom_call" | custom-call | flops 10000000 | bytes 7000000 | tf_op jit(solution)/shard_map/scatter_sum/pallas_call | solution.py:269
  129.2 0.6 copy.17
  129.8 0.6 copy.18
  130.4 0.6 copy.19
Async XLA Ops:
  1.3 2.0 %copy-start = (bf16[27,256,256]{2,1,0:T(8,128)(2,1)S(1)}, bf16[27,256,256]{2,1,0:T(8,128)(2,1)}, u32[]{:S(2)}) copy-start(bf16[27,256,256]{2,1,0:T(8,128)(2,1)} %weight_in.1) | copy-start | bytes 10616836
  3.3 1.2 copy-start.1
  4.5 1.2 copy-start.2
  5.7 1.2 copy-start.3
  7.0 0.9 copy-start.4
  7.9 0.7 copy-start.5
  8.6 0.7 copy-start.6
  9.3 0.7 copy-start.7

commit v6 on v5

--- a/solution.py
+++ b/solution.py
@@ -28,13 +28,18 @@
     place = columns - start.astype(jnp.float32)
     return jnp.where(place == lanes, 1.0, 0.0).astype(jnp.bfloat16)
 
-def conv_kernel(starts, idx, table, feat_t, turned, in_grad, wgrad, acc, picked):
+def conv_kernel(
+    starts, idx, table, feat_t, turned, sums_in, in_grad, wgrad, gamma_grad, beta_grad,
+    acc, picked,
+):
     step = pl.program_id(0)
     lane0 = 24 - 3 * step
 
     @pl.when(step == 0)
     def _():
         acc[...] = jnp.zeros_like(acc)
+        beta_grad[...] = sums_in[0]
+        gamma_grad[...] = sums_in[1]
 
     def columns_at(row):
         columns = pltpu.roll(idx[pl.ds(row, SUB), :], 128 - lane0, 1)
@@ -88,14 +93,16 @@
         in_grad[...] = acc[...].astype(jnp.bfloat16)
 
 
-def convolve(starts, idx, table, feat_t, turned):
+def convolve(starts, idx, table, feat_t, turned, sums):
     whole = pl.BlockSpec(memory_space=pltpu.VMEM)
-    in_grad, wgrad = pl.pallas_call(
+    in_grad, wgrad, gamma_grad, beta_grad = pl.pallas_call(
         conv_kernel,
         grid=(9,),
         out_shape=(
             jax.ShapeDtypeStruct((R, C), jnp.bfloat16),
             jax.ShapeDtypeStruct((27, C, C), jnp.float32),
+            jax.ShapeDtypeStruct((1, C), jnp.float32),
+            jax.ShapeDtypeStruct((1, C), jnp.float32),
         ),
         in_specs=[
             pl.BlockSpec(memory_space=pltpu.SMEM),
@@ -103,8 +110,9 @@
             whole,
             whole,
             pl.BlockSpec((1, 3 * C, C), lambda g: (g, 0, 0)),
+            whole,
         ],
-        out_specs=(whole, pl.BlockSpec((3, C, C), lambda g: (g, 0, 0))),
+        out_specs=(whole, pl.BlockSpec((3, C, C), lambda g: (g, 0, 0)), whole, whole),
         scratch_shapes=[
             pltpu.VMEM((R, C), jnp.float32),
             pltpu.VMEM((R, 3 * C), jnp.bfloat16),
@@ -114,8 +122,8 @@
             flops=30_000_000_000, bytes_accessed=20_000_000, transcendentals=0
         ),
         name="conv_backward",
-    )(starts, idx, table, feat_t, turned)
-    return in_grad, wgrad.reshape(27 * C, C)
+    )(starts, idx, table, feat_t, turned, sums)
+    return in_grad, wgrad.reshape(27 * C, C), gamma_grad, beta_grad
 
 
 AXES = ("gy", "gx_1", "gx_0")
@@ -304,7 +312,7 @@
 
 def front_kernel(
     count, pre_in, cot_in, gamma_in, beta_in, links_in, border_in, feat_in, weight_in,
-    table, columns, starts, gamma_grad, beta_grad, feat_t, turned,
+    table, columns, starts, sums, feat_t, turned,
     pre, cot, gamma, beta, links, border, feat, weight,
     grad, pick, near, far, list_left, list_own, list_right, high,
     note_own, note_left, note_right, note_out, note_in,
@@ -578,8 +586,8 @@
 
     sum_g, sum_gz = lax.fori_loop(0, R // block, second_sums, (zero, zero))
     whole = all_sum(1, stacked(sum_g, sum_gz, 0.0), plan)
-    beta_grad[...] = whole[0:1]
-    gamma_grad[...] = whole[1:2]
+    sums[0] = whole[0:1]
+    sums[1] = whole[1:2]
     scale = gain * rstd
     part_g, part_gz = whole[0:1] / amount, whole[1:2] / amount
 
@@ -668,14 +676,13 @@
             jax.ShapeDtypeStruct((ROWS, C), jnp.bfloat16),
             jax.ShapeDtypeStruct((R, 128), jnp.float32),
             jax.ShapeDtypeStruct((R // SUB * 8, 128), jnp.int32),
-            jax.ShapeDtypeStruct((1, C), jnp.float32),
-            jax.ShapeDtypeStruct((1, C), jnp.float32),
+            jax.ShapeDtypeStruct((2, 1, C), jnp.float32),
             jax.ShapeDtypeStruct((C, R), jnp.bfloat16),
             jax.ShapeDtypeStruct((9, 3 * C, C), jnp.bfloat16),
         ),
         in_specs=[pl.BlockSpec(memory_space=pltpu.SMEM)]
         + [pl.BlockSpec(memory_space=pltpu.HBM)] * 8,
-        out_specs=(vmem,) * 7,
+        out_specs=(vmem,) * 6,
         scratch_shapes=[pltpu.VMEM(a.shape, a.dtype) for a in arrays]
         + [
             pltpu.VMEM((R, C), jnp.float32),
@@ -700,11 +707,11 @@
             flops=1_000_000_000, bytes_accessed=10_000_000, transcendentals=1_000_000
         ),
         name="front",
-    )(counts, *arrays)
+    )(counts, *[pltpu.with_memory_space_constraint(a, pltpu.HBM) for a in arrays])
 
 
 def body(features, pre_norm, out_grad, weight, gamma, beta, neighbors, boundary, counts):
-    table, columns, starts, gamma_grad, beta_grad, feat_t, turned = front(
+    table, columns, starts, sums, feat_t, turned = front(
         counts,
         pre_norm[0, 0],
         out_grad[0, 0],
@@ -715,7 +722,9 @@
         features[0, 0],
         weight,
     )
-    in_grad, local_wgrad = convolve(starts, columns, table, feat_t, turned)
+    in_grad, local_wgrad, gamma_grad, beta_grad = convolve(
+        starts, columns, table, feat_t, turned, sums
+    )
     weight_grad = scatter_sum(local_wgrad)
     return (in_grad[None, None], weight_grad, gamma_grad[0], beta_grad[0])
 

time: 131 us -> 120 us (0.916)
  local copies, waits for them, and re-layouts: 10.4 us -> 0.63 us
    unnamed x19 -> x1, local copies, waits for them, and re-layouts: 10.4 us -> 0.63 us
where the time goes in v6:
time: 120 us
  Pallas kernels  118 us (98%)
  between operations  1.3 us (1%)
    pallas_call x1, Pallas kernels, front(): pl.pallas_call(front_kernel, out_shape=(jax.ShapeDtypeStruct((ROWS, C), j...  46.1 us
    pallas_call x1, Pallas kernels, convolve(): pl.pallas_call(conv_kernel, grid=(9,), out_shape=(jax.ShapeDtypeStruct((R...  40.7 us
    pallas_call x1, Pallas kernels, scatter_sum(): pl.pallas_call(scatter_kernel, out_shape=jax.ShapeDtypeStruct((54, C), jn...  31 us

profile of v6, /device:TPU:0, one launch (start us, length us, event | category | flops | bytes accessed | tf_op | source)
XLA Modules:
  0.0 119.8 jit_solution(6571540898961703792)
XLA Ops:
  1.3 46.1 %front.1 = (bf16[8640,256]{1,0:T(8,128)(2,1)S(1)}, f32[2048,128]{1,0:T(8,128)S(1)}, s32[128,128]{1,0:T(8,128)S(1)}, f32[2,1,256]{2,1,0:T(1,128)S(1)}, bf16[256,2...) custom-call(s32[1,1]{1,0:T(1,128)S(6)} %copy.14.count, bf16[2048,256]{1,0:T(8,128)(2,1)} %bitcast.12, ...), custom_call_target="tpu_custom_call" | custom-call | flops 1000000000 | bytes 10000000 | tf_op jit(solution)/shard_map/front/pallas_call | solution.py:673
  47.4 40.7 %conv_backward.1 = (bf16[2048,256]{1,0:T(8,128)(2,1)}, f32[27,256,256]{2,1,0:T(8,128)S(1)}, f32[1,256]{1,0:T(1,128)}, f32[1,256]{1,0:T(1,128)}) custom-call(s32[128,128]{1,0:T(8,128)S(1)} %get-tuple-element.14.starts, f32[2048,128]{1,0:T(8,128)S(1)} %get-tuple-element.15.idx, bf16[8640,256]{1,0:T(8,128)(2,1)S(1)} %get-tuple-element.16.table, ...), custom_call_target="tpu_custom_call" | custom-call | flops 30000001024 | bytes 20000000 | tf_op jit(solution)/shard_map/conv_backward/pallas_call | solution.py:98
  88.2 31.0 %scatter_sum.1 = f32[54,256]{1,0:T(8,128)S(1)} custom-call(f32[6912,256]{1,0:T(8,128)S(1)} %bitcast.11), custom_call_target="tpu_custom_call" | custom-call | flops 10000000 | bytes 7000000 | tf_op jit(solution)/shard_map/scatter_sum/pallas_call | solution.py:277
  119.2 0.6 copy.15

commit v7 on v6

--- a/solution.py
+++ b/solution.py
@@ -32,14 +32,19 @@
     starts, idx, table, feat_t, turned, sums_in, in_grad, wgrad, gamma_grad, beta_grad,
     acc, picked,
 ):
-    step = pl.program_id(0)
+    acc[...] = jnp.zeros_like(acc)
+    beta_grad[...] = sums_in[0]
+    gamma_grad[...] = sums_in[1]
+
+    @pl.loop(0, 9)
+    def _(step):
+        conv_group(step, starts, idx, table, feat_t, turned, wgrad, acc, picked)
+
+    in_grad[...] = acc[...].astype(jnp.bfloat16)
+
+
+def conv_group(step, starts, idx, table, feat_t, turned, wgrad, acc, picked):
     lane0 = 24 - 3 * step
-
-    @pl.when(step == 0)
-    def _():
-        acc[...] = jnp.zeros_like(acc)
-        beta_grad[...] = sums_in[0]
-        gamma_grad[...] = sums_in[1]
 
     def columns_at(row):
         columns = pltpu.roll(idx[pl.ds(row, SUB), :], 128 - lane0, 1)
@@ -82,22 +87,21 @@
 
     for j in range(R // SUB):
         gather(j)
-    for j in range(R // SUB):
-        gather_rest(j)
+
+    @pl.when(starts[3, lane0] < NROW)
+    def _():
+        for j in range(R // SUB):
+            gather_rest(j)
+
     for i in range(3):
-        wgrad[i] = dot(feat_t[...], picked[:, i * C : (i + 1) * C], ((1,), (0,)))
-    acc[...] += dot(picked[...], turned[0], ((1,), (0,)))
-
-    @pl.when(step == 8)
-    def _():
-        in_grad[...] = acc[...].astype(jnp.bfloat16)
+        wgrad[step * 3 + i] = dot(feat_t[...], picked[:, i * C : (i + 1) * C], ((1,), (0,)))
+    acc[...] += dot(picked[...], turned[step], ((1,), (0,)))
 
 
 def convolve(starts, idx, table, feat_t, turned, sums):
     whole = pl.BlockSpec(memory_space=pltpu.VMEM)
     in_grad, wgrad, gamma_grad, beta_grad = pl.pallas_call(
         conv_kernel,
-        grid=(9,),
         out_shape=(
             jax.ShapeDtypeStruct((R, C), jnp.bfloat16),
             jax.ShapeDtypeStruct((27, C, C), jnp.float32),
@@ -109,10 +113,10 @@
             whole,
             whole,
             whole,
-            pl.BlockSpec((1, 3 * C, C), lambda g: (g, 0, 0)),
+            whole,
             whole,
         ],
-        out_specs=(whole, pl.BlockSpec((3, C, C), lambda g: (g, 0, 0)), whole, whole),
+        out_specs=(whole,) * 4,
         scratch_shapes=[
             pltpu.VMEM((R, C), jnp.float32),
             pltpu.VMEM((R, 3 * C), jnp.bfloat16),
@@ -471,15 +475,12 @@
         )
         when(has_next, lambda: note_ahead().start())
 
-    def plan():
-        loads[5].wait()
-        when(has_last, lambda: note_ahead().wait_recv())
+    def plan(part, spare):
         moved = [note_in[b : b + 1, :] * 16 for b in range(3)]
         lane = lax.broadcasted_iota(jnp.int32, (1, 128), 1)
         third = lax.rem(lane, 3)
 
-        @pl.loop(0, R // SUB)
-        def _(j):
+        def one(j, spare):
             at = pl.ds(pl.multiple_of(j * SUB, SUB), SUB)
             idx = links[:, 0, at]
             for b in range(3):
@@ -500,10 +501,19 @@
                 start = jnp.where(low < NROW, jnp.floor(low * 0.0625) * 16.0, FAR)
                 idx = jnp.where(idx >= start + WIN, idx, FAR)
                 begin.append(jnp.minimum(start, float(NROW)) if w < 2 else start)
+            spare = jnp.minimum(spare, begin[2])
             begin = [jnp.broadcast_to(b, (8, 128)) for b in begin]
             row = lax.broadcasted_iota(jnp.int32, (8, 128), 0)
             begin = jnp.where(row == 0, begin[0], jnp.where(row == 1, begin[1], begin[2]))
             starts[pl.ds(pl.multiple_of(j * 8, 8), 8), :] = begin.astype(jnp.int32)
+            return spare
+
+        def some(n, spare):
+            for u in range(4):
+                spare = one(part * 8 + n * 4 + u, spare)
+            return spare
+
+        return lax.fori_loop(0, 2, some, spare)
 
     def choose():
         lane = lax.broadcasted_iota(jnp.int32, (128, 128), 1)
@@ -575,6 +585,13 @@
         load.wait()
     gain, shift = gamma[...], beta[...]
 
+    def during_second():
+        loads[6].wait()
+        for t in range(8):
+            feat_t[:, t * 256 : (t + 1) * 256] = feat[t * 256 : (t + 1) * 256, :].T
+        loads[5].wait()
+        when(has_last, lambda: note_ahead().wait_recv())
+
     def second_sums(t, sums):
         zhat = (pre[rows_at(t), :].astype(f32) - mean) * rstd
         act = gain * zhat + shift
@@ -585,7 +602,7 @@
         return sums[0] + fold(g), sums[1] + fold(g * zhat)
 
     sum_g, sum_gz = lax.fori_loop(0, R // block, second_sums, (zero, zero))
-    whole = all_sum(1, stacked(sum_g, sum_gz, 0.0), plan)
+    whole = all_sum(1, stacked(sum_g, sum_gz, 0.0), during_second)
     sums[0] = whole[0:1]
     sums[1] = whole[1:2]
     scale = gain * rstd
@@ -638,9 +655,7 @@
     when(has_left, lambda: left().start())
     pass_on(1, note_own)
     table[seg(4) : seg(5), :] = list_own[...]
-    loads[6].wait()
-    for t in range(8):
-        feat_t[:, t * 256 : (t + 1) * 256] = feat[t * 256 : (t + 1) * 256, :].T
+    spare = plan(0, jnp.full((1, 128), FAR, f32))
     loads[7].wait()
     for db, there, came, mark in (
         (0, has_left, right, note_left),
@@ -649,6 +664,10 @@
         when(there, lambda: came().wait_recv())
         when(there, lambda: pass_on(db, mark))
         table[seg(3 + db) : seg(4 + db), :] = lists[db][...]
+
+    spare = plan(1, spare)
+    row = lax.broadcasted_iota(jnp.int32, (8, 128), 0)
+    starts[0:8, :] = jnp.where(row == 3, spare.astype(jnp.int32), starts[0:8, :])
 
     @pl.loop(0, 9)
     def _(g):

time: 120 us -> 113 us (0.942)
  Pallas kernels: 118 us -> 111 us
    pallas_call x1, Pallas kernels: 46.1 us -> 41.7 us  [front(): pl.pallas_call(front_kernel, out_shape=(jax.ShapeDtypeStruct((ROWS, C), j...]
    pallas_call x1, Pallas kernels: 40.7 us -> 39.5 us  [convolve(): pl.pallas_call(conv_kernel, out_shape=(jax.ShapeDtypeStruct((R, C), jnp.b...]
where the time goes in v7:
time: 113 us
  Pallas kernels  111 us (98%)
  between operations  1.3 us (1%)
    pallas_call x1, Pallas kernels, front(): pl.pallas_call(front_kernel, out_shape=(jax.ShapeDtypeStruct((ROWS, C), j...  41.7 us
    pallas_call x1, Pallas kernels, convolve(): pl.pallas_call(conv_kernel, out_shape=(jax.ShapeDtypeStruct((R, C), jnp.b...  39.5 us
    pallas_call x1, Pallas kernels, scatter_sum(): pl.pallas_call(scatter_kernel, out_shape=jax.ShapeDtypeStruct((54, C), jn...  30.2 us

profile of v7, /device:TPU:0, one launch (start us, length us, event | category | flops | bytes accessed | tf_op | source)
XLA Modules:
  0.0 113.3 jit_solution(7527539475303895694)
XLA Ops:
  1.3 41.7 %front.1 = (bf16[8640,256]{1,0:T(8,128)(2,1)S(1)}, f32[2048,128]{1,0:T(8,128)S(1)}, s32[128,128]{1,0:T(8,128)S(1)}, f32[2,1,256]{2,1,0:T(1,128)S(1)}, bf16[256,2...) custom-call(s32[1,1]{1,0:T(1,128)S(6)} %copy.14.count, bf16[2048,256]{1,0:T(8,128)(2,1)} %bitcast.12, ...), custom_call_target="tpu_custom_call" | custom-call | flops 1000000000 | bytes 10000000 | tf_op jit(solution)/shard_map/front/pallas_call | solution.py:692
  42.9 39.5 %conv_backward.1 = (bf16[2048,256]{1,0:T(8,128)(2,1)}, f32[27,256,256]{2,1,0:T(8,128)S(1)}, f32[1,256]{1,0:T(1,128)}, f32[1,256]{1,0:T(1,128)}) custom-call(s32[128,128]{1,0:T(8,128)S(1)} %get-tuple-element.14.starts, f32[2048,128]{1,0:T(8,128)S(1)} %get-tuple-element.15.idx, bf16[8640,256]{1,0:T(8,128)(2,1)S(1)} %get-tuple-element.16.table, ...), custom_call_target="tpu_custom_call" | custom-call | flops 30000001024 | bytes 20000000 | tf_op jit(solution)/shard_map/conv_backward/pallas_call | solution.py:103
  82.5 30.2 %scatter_sum.1 = f32[54,256]{1,0:T(8,128)S(1)} custom-call(f32[6912,256]{1,0:T(8,128)S(1)} %bitcast.11), custom_call_target="tpu_custom_call" | custom-call | flops 10000000 | bytes 7000000 | tf_op jit(solution)/shard_map/scatter_sum/pallas_call | solution.py:281
  112.7 0.6 copy.15

commit v8 on v7

--- a/solution.py
+++ b/solution.py
@@ -235,8 +235,8 @@
             came[(1,) + at[1:]].astype(kind) + came[(2,) + at[1:]].astype(kind)
         )
 
-    third = []
-    for p in range(3):
+    third = [None] * 3
+    for p in (2, 0, 1):
         for copy in second[p]:
             copy.wait_recv()
         me = pos[p]
@@ -246,10 +246,10 @@
             for t in range(len(HOLDS[p])):
                 s_c[p][j // 4, j % 4, t] = total(s_b[p], r_b[p], (me, j, t)).astype(jnp.bfloat16)
 
-        third.append(spread(p, 1, c_sem, s_c[p], r_c[p]))
-
-    fourth = []
-    for p in range(3):
+        third[p] = spread(p, 1, c_sem, s_c[p], r_c[p])
+
+    fourth = [None] * 3
+    for p in (2, 0, 1):
         for copy in third[p]:
             copy.wait_recv()
         me = pos[(p + 1) % 3]
@@ -259,9 +259,9 @@
             for t in range(len(HOLDS[p])):
                 s_d[p][j, t] = total(s_c[p], r_c[p], (me, j, t))
 
-        fourth.append(spread(p, 2, d_sem, s_d[p], r_d[p]))
-
-    for p in range(3):
+        fourth[p] = spread(p, 2, d_sem, s_d[p], r_d[p])
+
+    for p in (2, 0, 1):
         for copy in fourth[p]:
             copy.wait_recv()
         me = pos[(p + 2) % 3]
@@ -388,11 +388,10 @@
         return sums[0] + fold(zlive), sums[1] + fold(zlive * zval)
 
     zero = jnp.zeros((8, C), f32)
-    line = lax.broadcasted_iota(jnp.int32, (8, C), 0)
-
-    def stacked(a, b, c):
+
+    def stacked(a, b, *more):
         a, b = jnp.sum(a, axis=0, keepdims=True), jnp.sum(b, axis=0, keepdims=True)
-        return jnp.where(line == 0, a, jnp.where(line == 1, b, jnp.where(line == 2, c, 0.0)))
+        return jnp.concatenate([a, b] + [jnp.full((1, C), c, f32) for c in more], axis=1)
 
     def exchange(slots, me, size, sems, turn, ids):
         copies = []
@@ -418,16 +417,16 @@
             total = total + slots[turn, i]
         return total
 
+    pending = []
+
     def all_sum(turn, value, meanwhile):
         near[turn, me_near] = value
         one = exchange(near, me_near, 8, near_sem, turn, near_id)
         meanwhile()
         far[turn, me_far] = add_up(near, 8, turn, one)
         two = exchange(far, me_far, 16, far_sem, turn, far_id)
-        total = add_up(far, 16, turn, two)
-        for copy in one + two:
-            copy.wait_send()
-        return total
+        pending.extend(one + two)
+        return add_up(far, 16, turn, two)
 
     def when(cond, act):
         @pl.when(cond)
@@ -577,9 +576,9 @@
         notes_second()
 
     whole = all_sum(0, stacked(sum_z, sum_sq, live_rows.astype(f32)), during_first)
-    amount = whole[2:3]
-    mean = whole[0:1] / amount
-    var = whole[1:2] / amount - mean * mean
+    amount = whole[:, 2 * C :]
+    mean = whole[:, :C] / amount
+    var = whole[:, C : 2 * C] / amount - mean * mean
     rstd = lax.rsqrt(var + 1e-05)
     for load in loads[2:5]:
         load.wait()
@@ -603,10 +602,10 @@
 
     sum_g, sum_gz = lax.fori_loop(0, R // block, second_sums, (zero, zero))
     whole = all_sum(1, stacked(sum_g, sum_gz, 0.0), during_second)
-    sums[0] = whole[0:1]
-    sums[1] = whole[1:2]
+    sums[0] = whole[:, :C]
+    sums[1] = whole[:, C : 2 * C]
     scale = gain * rstd
-    part_g, part_gz = whole[0:1] / amount, whole[1:2] / amount
+    part_g, part_gz = whole[:, :C] / amount, whole[:, C : 2 * C] / amount
 
     @pl.loop(0, R // block)
     def _(t):
@@ -685,6 +684,8 @@
     when(has_right, lambda: note_to_right().wait_send())
     when(has_left, lambda: note_to_left().wait_send())
     when(has_next, lambda: note_ahead().wait_send())
+    for copy in pending:
+        copy.wait_send()
 
 
 def front(counts, *arrays):
@@ -706,8 +707,8 @@
         + [
             pltpu.VMEM((R, C), jnp.float32),
             pltpu.VMEM((HB, R), jnp.bfloat16),
-            pltpu.VMEM((2, 8, 8, C), jnp.float32),
-            pltpu.VMEM((2, 16, 8, C), jnp.float32),
+            pltpu.VMEM((2, 8, 1, 3 * C), jnp.float32),
+            pltpu.VMEM((2, 16, 1, 3 * C), jnp.float32),
             pltpu.VMEM((HB, C), jnp.bfloat16),
             pltpu.VMEM((HB, C), jnp.bfloat16),
             pltpu.VMEM((HB, C), jnp.bfloat16),

time: 113 us -> 113 us (level)
  no operation moved by 1% of the time
where the time goes in v8:
time: 113 us
  Pallas kernels  111 us (98%)
  between operations  1.3 us (1%)
    pallas_call x1, Pallas kernels, front(): pl.pallas_call(front_kernel, out_shape=(jax.ShapeDtypeStruct((ROWS, C), j...  40.8 us
    pallas_call x1, Pallas kernels, convolve(): pl.pallas_call(conv_kernel, out_shape=(jax.ShapeDtypeStruct((R, C), jnp.b...  39.5 us
    pallas_call x1, Pallas kernels, scatter_sum(): pl.pallas_call(scatter_kernel, out_shape=jax.ShapeDtypeStruct((54, C), jn...  30.6 us

profile of v8, /device:TPU:0, one launch (start us, length us, event | category | flops | bytes accessed | tf_op | source)
XLA Modules:
  0.0 112.8 jit_solution(1161311505053584247)
XLA Ops:
  1.3 40.8 %front.1 = (bf16[8640,256]{1,0:T(8,128)(2,1)S(1)}, f32[2048,128]{1,0:T(8,128)S(1)}, s32[128,128]{1,0:T(8,128)S(1)}, f32[2,1,256]{2,1,0:T(1,128)S(1)}, bf16[256,2...) custom-call(s32[1,1]{1,0:T(1,128)S(6)} %copy.14.count, bf16[2048,256]{1,0:T(8,128)(2,1)} %bitcast.12, ...), custom_call_target="tpu_custom_call" | custom-call | flops 1000000000 | bytes 10000000 | tf_op jit(solution)/shard_map/front/pallas_call | solution.py:693
  42.1 39.5 %conv_backward.1 = (bf16[2048,256]{1,0:T(8,128)(2,1)}, f32[27,256,256]{2,1,0:T(8,128)S(1)}, f32[1,256]{1,0:T(1,128)}, f32[1,256]{1,0:T(1,128)}) custom-call(s32[128,128]{1,0:T(8,128)S(1)} %get-tuple-element.14.starts, f32[2048,128]{1,0:T(8,128)S(1)} %get-tuple-element.15.idx, bf16[8640,256]{1,0:T(8,128)(2,1)S(1)} %get-tuple-element.16.table, ...), custom_call_target="tpu_custom_call" | custom-call | flops 30000001024 | bytes 20000000 | tf_op jit(solution)/shard_map/conv_backward/pallas_call | solution.py:103
  81.6 30.6 %scatter_sum.1 = f32[54,256]{1,0:T(8,128)S(1)} custom-call(f32[6912,256]{1,0:T(8,128)S(1)} %bitcast.11), custom_call_target="tpu_custom_call" | custom-call | flops 10000000 | bytes 7000000 | tf_op jit(solution)/shard_map/scatter_sum/pallas_call | solution.py:281
  112.2 0.6 copy.15

commit v9 on v8

--- a/solution.py
+++ b/solution.py
@@ -47,8 +47,7 @@
     lane0 = 24 - 3 * step
 
     def columns_at(row):
-        columns = pltpu.roll(idx[pl.ds(row, SUB), :], 128 - lane0, 1)
-        return columns
+        return idx[step, pl.ds(row, SUB), :]
 
     def window(columns, start):
         hot = [
@@ -121,7 +120,7 @@
             pltpu.VMEM((R, C), jnp.float32),
             pltpu.VMEM((R, 3 * C), jnp.bfloat16),
         ],
-        compiler_params=pltpu.CompilerParams(vmem_limit_bytes=28 * 1024 * 1024),
+        compiler_params=pltpu.CompilerParams(vmem_limit_bytes=20 * 1024 * 1024),
         cost_estimate=pl.CostEstimate(
             flops=30_000_000_000, bytes_accessed=20_000_000, transcendentals=0
         ),
@@ -487,7 +486,9 @@
                 idx = jnp.where(inside, idx - moved[b], idx)
             idx = jnp.where(idx < NROW, idx, jnp.int32(FAR)).astype(f32)
             idx = jnp.concatenate([idx, jnp.full((101, SUB), FAR, f32)], axis=0).T
-            columns[at, :] = idx
+            for g in range(9):
+                shift = (104 + 3 * g) % 128
+                columns[g, at, :] = pltpu.roll(idx, shift, 1)
             begin = []
             for w in range(3):
                 low = jnp.min(idx, axis=0, keepdims=True)
@@ -694,7 +695,7 @@
         front_kernel,
         out_shape=(
             jax.ShapeDtypeStruct((ROWS, C), jnp.bfloat16),
-            jax.ShapeDtypeStruct((R, 128), jnp.float32),
+            jax.ShapeDtypeStruct((9, R, 128), jnp.float32),
             jax.ShapeDtypeStruct((R // SUB * 8, 128), jnp.int32),
             jax.ShapeDtypeStruct((2, 1, C), jnp.float32),
             jax.ShapeDtypeStruct((C, R), jnp.bfloat16),

time: 113 us -> 110 us (0.973)
  Pallas kernels: 111 us -> 108 us
    pallas_call x1, Pallas kernels: 39.5 us -> 36.6 us  [convolve(): pl.pallas_call(conv_kernel, out_shape=(jax.ShapeDtypeStruct((R, C), jnp.b...]
    pallas_call x1, Pallas kernels: 40.8 us -> 42.3 us  [front(): pl.pallas_call(front_kernel, out_shape=(jax.ShapeDtypeStruct((ROWS, C), j...]
where the time goes in v9:
time: 110 us
  Pallas kernels  108 us (98%)
  between operations  1.3 us (1%)
    pallas_call x1, Pallas kernels, front(): pl.pallas_call(front_kernel, out_shape=(jax.ShapeDtypeStruct((ROWS, C), j...  42.3 us
    pallas_call x1, Pallas kernels, convolve(): pl.pallas_call(conv_kernel, out_shape=(jax.ShapeDtypeStruct((R, C), jnp.b...  36.6 us
    pallas_call x1, Pallas kernels, scatter_sum(): pl.pallas_call(scatter_kernel, out_shape=jax.ShapeDtypeStruct((54, C), jn...  29.5 us

profile of v9, /device:TPU:0, one launch (start us, length us, event | category | flops | bytes accessed | tf_op | source)
XLA Modules:
  0.0 110.3 jit_solution(16661180104073012315)
XLA Ops:
  1.3 42.3 %front.1 = (bf16[8640,256]{1,0:T(8,128)(2,1)S(1)}, f32[9,2048,128]{2,1,0:T(8,128)S(1)}, s32[128,128]{1,0:T(8,128)S(1)}, f32[2,1,256]{2,1,0:T(1,128)S(1)}, bf16[2...) custom-call(s32[1,1]{1,0:T(1,128)S(6)} %copy.14.count, bf16[2048,256]{1,0:T(8,128)(2,1)} %bitcast.12, ...), custom_call_target="tpu_custom_call" | custom-call | flops 1000000000 | bytes 10000000 | tf_op jit(solution)/shard_map/front/pallas_call | solution.py:694
  43.6 36.6 %conv_backward.1 = (bf16[2048,256]{1,0:T(8,128)(2,1)}, f32[27,256,256]{2,1,0:T(8,128)S(1)}, f32[1,256]{1,0:T(1,128)}, f32[1,256]{1,0:T(1,128)}) custom-call(s32[128,128]{1,0:T(8,128)S(1)} %get-tuple-element.14.starts, f32[9,2048,128]{2,1,0:T(8,128)S(1)} %get-tuple-element.15.idx, bf16[8640,256]{1,0:T(8,128)(2,1)S(1)} %get-tuple-element.16.table, ...), custom_call_target="tpu_custom_call" | custom-call | flops 30000001024 | bytes 20000000 | tf_op jit(solution)/shard_map/conv_backward/pallas_call | solution.py:102
  80.2 29.5 %scatter_sum.1 = f32[54,256]{1,0:T(8,128)S(1)} custom-call(f32[6912,256]{1,0:T(8,128)S(1)} %bitcast.11), custom_call_target="tpu_custom_call" | custom-call | flops 10000000 | bytes 7000000 | tf_op jit(solution)/shard_map/scatter_sum/pallas_call | solution.py:280
  109.7 0.6 copy.15

commit v10 on v9

--- a/solution.py
+++ b/solution.py
@@ -240,7 +240,7 @@
             copy.wait_recv()
         me = pos[p]
 
-        @pl.loop(0, 16)
+        @pl.loop(0, 16, unroll=4)
         def _(j):
             for t in range(len(HOLDS[p])):
                 s_c[p][j // 4, j % 4, t] = total(s_b[p], r_b[p], (me, j, t)).astype(jnp.bfloat16)
@@ -253,7 +253,7 @@
             copy.wait_recv()
         me = pos[(p + 1) % 3]
 
-        @pl.loop(0, 4)
+        @pl.loop(0, 4, unroll=4)
         def _(j):
             for t in range(len(HOLDS[p])):
                 s_d[p][j, t] = total(s_c[p], r_c[p], (me, j, t))

time: 110 us -> 111 us (level)
  no operation moved by 1% of the time
where the time goes in v10:
time: 111 us
  Pallas kernels  109 us (98%)
  between operations  1.3 us (1%)
    pallas_call x1, Pallas kernels, front(): pl.pallas_call(front_kernel, out_shape=(jax.ShapeDtypeStruct((ROWS, C), j...  42.3 us
    pallas_call x1, Pallas kernels, convolve(): pl.pallas_call(conv_kernel, out_shape=(jax.ShapeDtypeStruct((R, C), jnp.b...  36.5 us
    pallas_call x1, Pallas kernels, scatter_sum(): pl.pallas_call(scatter_kernel, out_shape=jax.ShapeDtypeStruct((54, C), jn...  29.9 us

profile of v10, /device:TPU:0, one launch (start us, length us, event | category | flops | bytes accessed | tf_op | source)
XLA Modules:
  0.0 110.6 jit_solution(12054285407929598639)
XLA Ops:
  1.3 42.3 %front.1 = (bf16[8640,256]{1,0:T(8,128)(2,1)S(1)}, f32[9,2048,128]{2,1,0:T(8,128)S(1)}, s32[128,128]{1,0:T(8,128)S(1)}, f32[2,1,256]{2,1,0:T(1,128)S(1)}, bf16[2...) custom-call(s32[1,1]{1,0:T(1,128)S(6)} %copy.14.count, bf16[2048,256]{1,0:T(8,128)(2,1)} %bitcast.12, ...), custom_call_target="tpu_custom_call" | custom-call | flops 1000000000 | bytes 10000000 | tf_op jit(solution)/shard_map/front/pallas_call | solution.py:694
  43.6 36.5 %conv_backward.1 = (bf16[2048,256]{1,0:T(8,128)(2,1)}, f32[27,256,256]{2,1,0:T(8,128)S(1)}, f32[1,256]{1,0:T(1,128)}, f32[1,256]{1,0:T(1,128)}) custom-call(s32[128,128]{1,0:T(8,128)S(1)} %get-tuple-element.14.starts, f32[9,2048,128]{2,1,0:T(8,128)S(1)} %get-tuple-element.15.idx, bf16[8640,256]{1,0:T(8,128)(2,1)S(1)} %get-tuple-element.16.table, ...), custom_call_target="tpu_custom_call" | custom-call | flops 30000001024 | bytes 20000000 | tf_op jit(solution)/shard_map/conv_backward/pallas_call | solution.py:102
  80.1 29.9 %scatter_sum.1 = f32[54,256]{1,0:T(8,128)S(1)} custom-call(f32[6912,256]{1,0:T(8,128)S(1)} %bitcast.11), custom_call_target="tpu_custom_call" | custom-call | flops 10000000 | bytes 7000000 | tf_op jit(solution)/shard_map/scatter_sum/pallas_call | solution.py:280
  110.0 0.6 copy.15

commit v11 on v9

--- a/solution.py
+++ b/solution.py
@@ -198,7 +198,7 @@
             for d in range(1, 4)
         ]
 
-    second = [None, None, []]
+    second = [[], [], []]
     for i in range(4):
         first[i].wait_recv()
         z_of = around(i)
@@ -215,9 +215,9 @@
                                 continue
                             piece = both[:, side * 128 : (side + 1) * 128]
                             if p == 0:
-                                s_b[0][x, y * 4 + z_of, n] = piece
+                                s_b[0][x, i * 4 + y, n] = piece
                             elif p == 1:
-                                s_b[1][y, z_of * 4 + x, n] = piece
+                                s_b[1][y, i * 4 + x, n] = piece
                             else:
                                 s_b[2][z_of, x * 4 + y, n] = piece
 
@@ -225,8 +225,20 @@
             second[2].append(
                 send(s_b[2].at[z_of], r_b[2].at[i], b_sem, (2, i), {"gx_0": z_of})
             )
-    for p in range(2):
-        second[p] = spread(p, 0, b_sem, s_b[p], r_b[p])
+        if i % 2:
+            part_of = pl.ds((i - 1) * 4, 8)
+            for p in range(2):
+                for d in range(1, 4):
+                    peer = lax.rem(pos[p] + d, 4)
+                    second[p].append(
+                        send(
+                            s_b[p].at[peer, part_of],
+                            r_b[p].at[d - 1, part_of],
+                            b_sem,
+                            (p, i // 2 * 3 + d - 1),
+                            {AXES[p]: peer},
+                        )
+                    )
 
     def total(own, came, at):
         kind = jnp.float32
@@ -243,7 +255,13 @@
         @pl.loop(0, 16)
         def _(j):
             for t in range(len(HOLDS[p])):
-                s_c[p][j // 4, j % 4, t] = total(s_b[p], r_b[p], (me, j, t)).astype(jnp.bfloat16)
+                piece = total(s_b[p], r_b[p], (me, j, t)).astype(jnp.bfloat16)
+                if p == 0:
+                    s_c[p][j % 4, around(j // 4), t] = piece
+                elif p == 1:
+                    s_c[p][around(j // 4), j % 4, t] = piece
+                else:
+                    s_c[p][j // 4, j % 4, t] = piece
 
         third[p] = spread(p, 1, c_sem, s_c[p], r_c[p])
 
@@ -292,7 +310,7 @@
             *stage((4,), full),
             *stage((3,), full),
             pltpu.SemaphoreType.DMA((2, 4)),
-            pltpu.SemaphoreType.DMA((2, 3, 3)),
+            pltpu.SemaphoreType.DMA((2, 3, 6)),
             pltpu.SemaphoreType.DMA((2, 3, 3)),
             pltpu.SemaphoreType.DMA((2, 3, 3)),
         ],

time: 110 us -> 109 us (level)
  no operation moved by 1% of the time
where the time goes in v11:
time: 109 us
  Pallas kernels  107 us (98%)
  between operations  1.3 us (1%)
    pallas_call x1, Pallas kernels, front(): pl.pallas_call(front_kernel, out_shape=(jax.ShapeDtypeStruct((ROWS, C), j...  42.3 us
    pallas_call x1, Pallas kernels, convolve(): pl.pallas_call(conv_kernel, out_shape=(jax.ShapeDtypeStruct((R, C), jnp.b...  36.6 us
    pallas_call x1, Pallas kernels, scatter_sum(): pl.pallas_call(scatter_kernel, out_shape=jax.ShapeDtypeStruct((54, C), jn...  28.5 us

profile of v11, /device:TPU:0, one launch (start us, length us, event | category | flops | bytes accessed | tf_op | source)
XLA Modules:
  0.0 109.4 jit_solution(11140723782991634886)
XLA Ops:
  1.3 42.3 %front.1 = (bf16[8640,256]{1,0:T(8,128)(2,1)S(1)}, f32[9,2048,128]{2,1,0:T(8,128)S(1)}, s32[128,128]{1,0:T(8,128)S(1)}, f32[2,1,256]{2,1,0:T(1,128)S(1)}, bf16[2...) custom-call(s32[1,1]{1,0:T(1,128)S(6)} %copy.14.count, bf16[2048,256]{1,0:T(8,128)(2,1)} %bitcast.12, ...), custom_call_target="tpu_custom_call" | custom-call | flops 1000000000 | bytes 10000000 | tf_op jit(solution)/shard_map/front/pallas_call | solution.py:712
  43.6 36.6 %conv_backward.1 = (bf16[2048,256]{1,0:T(8,128)(2,1)}, f32[27,256,256]{2,1,0:T(8,128)S(1)}, f32[1,256]{1,0:T(1,128)}, f32[1,256]{1,0:T(1,128)}) custom-call(s32[128,128]{1,0:T(8,128)S(1)} %get-tuple-element.14.starts, f32[9,2048,128]{2,1,0:T(8,128)S(1)} %get-tuple-element.15.idx, bf16[8640,256]{1,0:T(8,128)(2,1)S(1)} %get-tuple-element.16.table, ...), custom_call_target="tpu_custom_call" | custom-call | flops 30000001024 | bytes 20000000 | tf_op jit(solution)/shard_map/conv_backward/pallas_call | solution.py:102
  80.2 28.5 %scatter_sum.1 = f32[54,256]{1,0:T(8,128)S(1)} custom-call(f32[6912,256]{1,0:T(8,128)S(1)} %bitcast.11), custom_call_target="tpu_custom_call" | custom-call | flops 10000000 | bytes 7000000 | tf_op jit(solution)/shard_map/scatter_sum/pallas_call | solution.py:298
  108.7 0.6 copy.15
